TPU v7x, 32 devices: a whole 2x2x4 slice. The times are simulated.
32 devices in a mesh: depth: 4 (over z), gx: 2 (over y), gy: 4 (over x, core).
Axes of the slice: x: 2, y: 2, z: 4, core: 2. Of those that a mesh axis runs over, the one named last changes fastest.
Arguments:
- source: float32 [8, 2, 4, 128, 512], P('depth', None, None, 'gx', 'gy'), may hold values from -6 to 6
- observed: float32 [8, 2, 4, 128, 512], P('depth', None, None, 'gx', 'gy'), may hold values from -8 to 8
- wavenumber: float32 [8, 128, 512], P('depth', 'gx', 'gy'), may hold values from 0.5 to 1.5
- damping: float32 [8, 128, 512], P('depth', 'gx', 'gy'), may hold values from 0.5 to 2
Outputs:
- forward_field: float32 [8, 2, 4, 128, 512], P('depth', None, None, 'gx', 'gy')
- gradient: float32 [8, 128, 512], P('depth', 'gx', 'gy')
All inputs are finite; a program needn't handle non-finite values.
Results may differ from a plain program's by a relative error of at most 0.00002.
Values sent between devices are 32-bit elements; how exact they have to be, the bound alone decides.
No kernel may reach another device: no remote copies, remote signals or barrier semaphores. Data moves between devices by JAX's collectives and lax.ppermute only.
A program may use at most 64 MiB of HBM per device.

v0:
```python
import jax
import jax.numpy as jnp
from jax import lax
from jax.sharding import PartitionSpec as P


def with_halo(cells, sides, width):
    for axis, dim in sides:
        count = lax.axis_size(axis)
        ends = count - 1
        head = lax.slice_in_dim(cells, 0, width, axis=dim)
        tail = lax.slice_in_dim(cells, cells.shape[dim] - width, cells.shape[dim], axis=dim)
        cells = jnp.concatenate(
            [
                lax.ppermute(tail, axis, [(i, (i + 1) % count) for i in range(ends)]),
                cells,
                lax.ppermute(head, axis, [((i + 1) % count, i) for i in range(ends)]),
            ],
            axis=dim,
        )
    return cells


def shifted(block, axis, distance):
    devices = range(lax.axis_size(axis))
    route = [(i - distance, i) for i in devices if i - distance in devices]
    return lax.ppermute(block, axis, route)


def complex_scale(plane, inverse):
    real_part = inverse[0][None]
    imag_part = inverse[1][None]
    return jnp.stack(
        [plane[0] * real_part - plane[1] * imag_part, plane[0] * imag_part + plane[1] * real_part]
    )


def relax(drive, inverse, edges):
    field = complex_scale(drive, inverse)
    for sweep_step in range(2):
        padded = edges(field)
        beside = (
            padded[:, :, 2:, 1:-1]
            + padded[:, :, :-2, 1:-1]
            + padded[:, :, 1:-1, 2:]
            + padded[:, :, 1:-1, :-2]
        )
        field = complex_scale(drive + beside, inverse)
    return field


def sweep(drive, inverse, incoming, edges, reverse):

    def advance(carry, items):
        plane, inv_plane = items
        result = relax(plane + 2.5 * carry, inv_plane, edges)
        return (result, result)

    final, fields = lax.scan(advance, incoming, (drive, inverse), reverse=reverse)
    return fields


def edges_many(field):
    return with_halo(field, (("gx", 2), ("gy", 3)), 1)


def inverse_pair(wavenumber, damping):
    real_diag = 6.0 - wavenumber
    denom = real_diag * real_diag + damping * damping
    inv_real = real_diag / denom
    inv_imag = damping / denom
    return (jnp.stack([inv_real, -inv_imag], axis=1), jnp.stack([inv_real, inv_imag], axis=1))


def body(source, observed, wavenumber, damping):
    ndepth = lax.axis_size("depth")
    inv_fwd, inv_adj = inverse_pair(wavenumber, damping)
    incoming = jnp.zeros(source.shape[1:], jnp.float32)
    for round_idx in range(ndepth):
        forward_field = sweep(source, inv_fwd, incoming, edges_many, False)
        if round_idx + 1 < ndepth:
            incoming = shifted(forward_field[-1], "depth", 1)
    residual = forward_field - observed
    incoming = jnp.zeros(source.shape[1:], jnp.float32)
    for round_idx in range(ndepth):
        adjoint = sweep(residual, inv_adj, incoming, edges_many, True)
        if round_idx + 1 < ndepth:
            incoming = shifted(adjoint[0], "depth", -1)
    product = forward_field[:, 0] * adjoint[:, 0] + forward_field[:, 1] * adjoint[:, 1]
    gradient = jnp.mean(product, axis=1)
    return (forward_field, gradient)


def solution(mesh):
    return jax.shard_map(
        body,
        mesh=mesh,
        in_specs=(
            P("depth", None, None, "gx", "gy"),
            P("depth", None, None, "gx", "gy"),
            P("depth", "gx", "gy"),
            P("depth", "gx", "gy"),
        ),
        out_specs=(P("depth", None, None, "gx", "gy"), P("depth", "gx", "gy")),
        check_vma=False,
    )
```

profile of v0, /device:TPU:0, one launch (start us, length us, event | category | flops | bytes accessed | tf_op | source)
XLA Modules:
  0.0 615.1 jit_solution(18160422384756628229)
XLA Ops:
  2.6 68.4 %while.112 = (s32[]{:T(128)}, f32[2,4,64,128]{3,2,1,0:T(8,128)S(1)}, f32[2,2,4,64,128]{4,3,2,1,0:T(8,128)S(1)}, f32[2,2,4,64,128]{4,3,2,1,0:T(8,128)S(1)}, f32[2...) while((s32[]{:T(128)}, f32[2,4,64,128]{3,2,1,0:T(8,128)S(1)}, ...), condition=%wide.region_1.2_spmd, body=%wide.region_0.1_spmd.sunk | while | flops 3293187 | bytes 6809785 | solution.py:59
  4.0 4.9 collective-permute-start.1
  13.0 5.0 collective-permute-done.3
  19.6 4.5 collective-permute-start.5
  25.7 5.9 collective-permute-start.6
  37.3 4.5 collective-permute-start.1
  43.4 5.9 collective-permute-start.2
  54.8 4.5 collective-permute-start.5
  60.8 5.9 collective-permute-start.6
  78.5 70.3 %while.113 = (s32[]{:T(128)}, f32[2,4,64,128]{3,2,1,0:T(8,128)S(1)}, f32[2,2,4,64,128]{4,3,2,1,0:T(8,128)S(1)}, f32[2,2,4,64,128]{4,3,2,1,0:T(8,128)S(1)}, f32[2...) while((s32[]{:T(128)}, f32[2,4,64,128]{3,2,1,0:T(8,128)S(1)}, ...), condition=%wide.region_3.4_spmd, body=%wide.region_2.3_spmd.sunk | while | flops 3293187 | bytes 6809785 | solution.py:59
  79.9 4.5 collective-permute-start.9
  86.0 5.0 collective-permute-start.10
  97.4 4.5 collective-permute-start.13
  103.5 5.9 collective-permute-start.14
  115.1 4.5 collective-permute-start.9
  121.1 5.9 collective-permute-start.10
  132.6 4.5 collective-permute-start.13
  138.6 5.9 collective-permute-start.14
  157.2 70.3 %while.114 = (s32[]{:T(128)}, f32[2,4,64,128]{3,2,1,0:T(8,128)S(1)}, f32[2,2,4,64,128]{4,3,2,1,0:T(8,128)S(1)}, f32[2,2,4,64,128]{4,3,2,1,0:T(8,128)S(1)}, f32[2...) while((s32[]{:T(128)}, f32[2,4,64,128]{3,2,1,0:T(8,128)S(1)}, ...), condition=%wide.region_5.6_spmd, body=%wide.region_4.5_spmd.sunk | while | flops 3293187 | bytes 6809785 | solution.py:59
  158.6 4.5 collective-permute-start.17
  164.6 5.0 collective-permute-start.18
  176.1 4.5 collective-permute-start.21
  182.1 5.9 collective-permute-start.22
  193.8 4.5 collective-permute-start.17
  199.8 5.9 collective-permute-start.18
  211.3 4.5 collective-permute-start.21
  217.3 5.9 collective-permute-start.22
  235.8 70.3 %while.115 = (s32[]{:T(128)}, f32[2,4,64,128]{3,2,1,0:T(8,128)S(1)}, f32[2,2,4,64,128]{4,3,2,1,0:T(8,128)S(1)}, f32[2,2,4,64,128]{4,3,2,1,0:T(8,128)S(1)}, f32[2...) while((s32[]{:T(128)}, f32[2,4,64,128]{3,2,1,0:T(8,128)S(1)}, ...), condition=%wide.region_7.8_spmd, body=%wide.region_6.7_spmd.sunk | while | flops 3293187 | bytes 6809785 | solution.py:59
  237.3 4.5 collective-permute-start.25
  243.3 5.0 collective-permute-start.26
  254.8 4.5 collective-permute-start.29
  260.8 5.9 collective-permute-start.30
  272.4 4.5 collective-permute-start.25
  278.5 5.9 collective-permute-start.26
  296.0 5.9 collective-permute-start.30
  307.6 70.3 %while.116 = (s32[]{:T(128)}, f32[2,4,64,128]{3,2,1,0:T(8,128)S(1)}, f32[2,2,4,64,128]{4,3,2,1,0:T(8,128)S(1)}, f32[2,2,4,64,128]{4,3,2,1,0:T(8,128)S(1)}, f32[2...) while((s32[]{:T(128)}, f32[2,4,64,128]{3,2,1,0:T(8,128)S(1)}, ...), condition=%wide.region_9.10_spmd, body=%wide.region_8.9_spmd.sunk | while | flops 3293188 | bytes 6809789 | solution.py:59
  315.0 5.9 collective-permute-start.34
  326.5 4.5 collective-permute-start.37
  332.5 5.9 collective-permute-start.38
  344.2 4.5 collective-permute-start.33
  350.2 5.9 collective-permute-start.34
  367.7 5.9 collective-permute-start.38
  379.2 7.4 %collective-permute-done.67 = f32[2,4,64,128]{3,2,1,0:T(8,128)S(1)} collective-permute-done((f32[2,4,64,128]{3,2,1,0:T(8,128)S(1)}, f32[2,4,64,128]{3,2,1,0:T(8,128)S(1)}, u32[]{:S(2)}, u32[]{:S(2)}) %collective-permute-start.67) | collective-permute-done | bytes 262176 | tf_op jit(solution)/shard_map/ppermute | solution.py:27
  386.7 70.3 %while.117 = (s32[]{:T(128)}, f32[2,4,64,128]{3,2,1,0:T(8,128)S(1)}, f32[2,2,4,64,128]{4,3,2,1,0:T(8,128)S(1)}, f32[2,2,4,64,128]{4,3,2,1,0:T(8,128)S(1)}, f32[2...) while((s32[]{:T(128)}, f32[2,4,64,128]{3,2,1,0:T(8,128)S(1)}, ...), condition=%wide.region_11.12_spmd, body=%wide.region_10.11_spmd.sunk | while | flops 3293188 | bytes 6809789 | solution.py:59
  394.2 5.0 collective-permute-start.42
  405.6 4.5 collective-permute-start.45
  411.7 5.9 collective-permute-start.46
  423.3 4.5 collective-permute-start.41
  429.4 5.9 collective-permute-start.42
  446.9 5.9 collective-permute-start.46
  458.6 6.8 %collective-permute-done.68 = f32[2,4,64,128]{3,2,1,0:T(8,128)S(1)} collective-permute-done((f32[2,4,64,128]{3,2,1,0:T(8,128)S(1)}, f32[2,4,64,128]{3,2,1,0:T(8,128)S(1)}, u32[]{:S(2)}, u32[]{:S(2)}) %collective-permute-start.68) | collective-permute-done | bytes 262176 | tf_op jit(solution)/shard_map/ppermute | solution.py:27
  465.4 70.3 %while.118 = (s32[]{:T(128)}, f32[2,4,64,128]{3,2,1,0:T(8,128)S(1)}, f32[2,2,4,64,128]{4,3,2,1,0:T(8,128)S(1)}, f32[2,2,4,64,128]{4,3,2,1,0:T(8,128)S(1)}, f32[2...) while((s32[]{:T(128)}, f32[2,4,64,128]{3,2,1,0:T(8,128)S(1)}, ...), condition=%wide.region_13.14_spmd, body=%wide.region_12.13_spmd.sunk | while | flops 3293188 | bytes 6809789 | solution.py:59
  472.9 5.0 collective-permute-start.50
  490.4 5.9 collective-permute-start.54
  508.0 5.9 collective-permute-start.50
  525.5 5.9 collective-permute-start.54
  537.1 7.0 %collective-permute-done.69 = f32[2,4,64,128]{3,2,1,0:T(8,128)S(1)} collective-permute-done((f32[2,4,64,128]{3,2,1,0:T(8,128)S(1)}, f32[2,4,64,128]{3,2,1,0:T(8,128)S(1)}, u32[]{:S(2)}, u32[]{:S(2)}) %collective-permute-start.69) | collective-permute-done | bytes 262176 | tf_op jit(solution)/shard_map/ppermute | solution.py:27
  544.1 70.3 %while.119 = (s32[]{:T(128)}, f32[2,4,64,128]{3,2,1,0:T(8,128)S(1)}, f32[2,2,4,64,128]{4,3,2,1,0:T(8,128)S(1)}, f32[2,2,4,64,128]{4,3,2,1,0:T(8,128)S(1)}, f32[2...) while((s32[]{:T(128)}, f32[2,4,64,128]{3,2,1,0:T(8,128)S(1)}, ...), condition=%wide.region_15.16_spmd, body=%wide.region_14.15_spmd.sunk | while | flops 3293188 | bytes 6809789 | solution.py:59
  545.5 4.5 collective-permute-start.57
  551.6 5.0 collective-permute-start.58
  569.1 5.9 collective-permute-start.62
  586.7 5.9 collective-permute-start.58
  598.2 4.5 collective-permute-start.61
  604.2 5.9 collective-permute-start.62
  (463 shorter events, 312.8 us)
Async XLA Ops:
  2.7 6.2 %collective-permute-start = (f32[2,4,1,128]{3,2,1,0:T(1,128)S(1)}, f32[2,4,1,128]{3,2,1,0:T(1,128)S(1)}, u32[]{:S(2)}, u32[]{:S(2)}) collective-permute-start(f32[2,4,1,128]{3,2,1,0:T(1,128)S(1)} %get-tuple-element.1139), channel_id=1, source_target_pairs={{4,0},{5,1},{6,2},{7,3},{12,8},{13,9},{14,10},{15,11},{20,16},{21,... | collective-permute-start | bytes 12296 | tf_op jit(solution)/shard_map/while/body/eval_jaxpr/ppermute | solution.py:17
  4.0 6.2 %collective-permute-start.1 = (f32[2,4,1,128]{3,2,1,0:T(1,128)S(1)}, f32[2,4,1,128]{3,2,1,0:T(1,128)S(1)}, u32[]{:S(2)}, u32[]{:S(2)}) collective-permute-start(f32[2,4,1,128]{3,2,1,0:T(1,128)S(1)} %get-tuple-element.1140), channel_id=1, source_target_pairs={{0,4},{1,5},{2,6},{3,7},{8,12},{9,13},{10,14},{11,15},{16,20},{17,... | collective-permute-start | bytes 12296 | tf_op jit(solution)/shard_map/while/body/eval_jaxpr/ppermute | solution.py:15
  11.7 6.3 %collective-permute-start.3 = (f32[2,4,66,1]{3,2,1,0:T(8,128)S(1)}, f32[2,4,66,1]{3,2,1,0:T(8,128)S(1)}, u32[]{:S(2)}, u32[]{:S(2)}) collective-permute-start(f32[2,4,66,1]{3,2,1,0:T(8,128)S(1)} %get-tuple-element.1142), channel_id=1, source_target_pairs={{1,0},{2,1},{3,2},{5,4},{6,5},{7,6},{9,8},{10,9},{11,10},{13,12},{... | collective-permute-start | bytes 6344 | tf_op jit(solution)/shard_map/while/body/eval_jaxpr/ppermute | solution.py:17
  19.6 5.9 collective-permute-start.5
  25.7 7.2 %collective-permute-start.6 = (f32[2,4,66,1]{3,2,1,0:T(8,128)S(1)}, f32[2,4,66,1]{3,2,1,0:T(8,128)S(1)}, u32[]{:S(2)}, u32[]{:S(2)}) collective-permute-start(f32[2,4,66,1]{3,2,1,0:T(8,128)S(1)} %get-tuple-element.1147), channel_id=1, source_target_pairs={{0,1},{1,2},{2,3},{4,5},{5,6},{6,7},{8,9},{9,10},{10,11},{12,13},{... | collective-permute-start | bytes 6344 | tf_op jit(solution)/shard_map/while/body/eval_jaxpr/ppermute | solution.py:15
  37.3 5.9 collective-permute-start.1
  43.4 7.2 %collective-permute-start.2 = (f32[2,4,66,1]{3,2,1,0:T(8,128)S(1)}, f32[2,4,66,1]{3,2,1,0:T(8,128)S(1)}, u32[]{:S(2)}, u32[]{:S(2)}) collective-permute-start(f32[2,4,66,1]{3,2,1,0:T(8,128)S(1)} %get-tuple-element.1141), channel_id=1, source_target_pairs={{0,1},{1,2},{2,3},{4,5},{5,6},{6,7},{8,9},{9,10},{10,11},{12,13},{... | collective-permute-start | bytes 6344 | tf_op jit(solution)/shard_map/while/body/eval_jaxpr/ppermute | solution.py:15
  54.8 5.9 collective-permute-start.5
  60.8 7.2 %collective-permute-start.6 = (f32[2,4,66,1]{3,2,1,0:T(8,128)S(1)}, f32[2,4,66,1]{3,2,1,0:T(8,128)S(1)}, u32[]{:S(2)}, u32[]{:S(2)}) collective-permute-start(f32[2,4,66,1]{3,2,1,0:T(8,128)S(1)} %get-tuple-element.1147), channel_id=1, source_target_pairs={{0,1},{1,2},{2,3},{4,5},{5,6},{6,7},{8,9},{9,10},{10,11},{12,13},{... | collective-permute-start | bytes 6344 | tf_op jit(solution)/shard_map/while/body/eval_jaxpr/ppermute | solution.py:15
  71.1 7.4 %collective-permute-start.64 = (f32[2,4,64,128]{3,2,1,0:T(8,128)S(1)}, f32[2,4,64,128]{3,2,1,0:T(8,128)S(1)}, u32[]{:S(2)}, u32[]{:S(2)}) collective-permute-start(f32[2,4,64,128]{3,2,1,0:T(8,128)S(1)} %slice_bitcast_fusion.5), channel_id=1, source_target_pairs={{0,8},{8,16},{16,24},{1,9},{9,17},{17,25},{2,10},{10,18},{18,26},{... | collective-permute-start | bytes 786440 | tf_op jit(solution)/shard_map/ppermute | solution.py:27
  79.9 5.9 collective-permute-start.9
  86.0 6.3 %collective-permute-start.10 = (f32[2,4,66,1]{3,2,1,0:T(8,128)S(1)}, f32[2,4,66,1]{3,2,1,0:T(8,128)S(1)}, u32[]{:S(2)}, u32[]{:S(2)}) collective-permute-start(f32[2,4,66,1]{3,2,1,0:T(8,128)S(1)} %get-tuple-element.1164), channel_id=1, source_target_pairs={{0,1},{1,2},{2,3},{4,5},{5,6},{6,7},{8,9},{9,10},{10,11},{12,13},{... | collective-permute-start | bytes 6344 | tf_op jit(solution)/shard_map/while/body/eval_jaxpr/ppermute | solution.py:15
  97.4 5.9 collective-permute-start.13
  103.5 7.2 %collective-permute-start.14 = (f32[2,4,66,1]{3,2,1,0:T(8,128)S(1)}, f32[2,4,66,1]{3,2,1,0:T(8,128)S(1)}, u32[]{:S(2)}, u32[]{:S(2)}) collective-permute-start(f32[2,4,66,1]{3,2,1,0:T(8,128)S(1)} %get-tuple-element.1170), channel_id=1, source_target_pairs={{0,1},{1,2},{2,3},{4,5},{5,6},{6,7},{8,9},{9,10},{10,11},{12,13},{... | collective-permute-start | bytes 6344 | tf_op jit(solution)/shard_map/while/body/eval_jaxpr/ppermute | solution.py:15
  115.1 5.9 collective-permute-start.9
  121.1 7.2 %collective-permute-start.10 = (f32[2,4,66,1]{3,2,1,0:T(8,128)S(1)}, f32[2,4,66,1]{3,2,1,0:T(8,128)S(1)}, u32[]{:S(2)}, u32[]{:S(2)}) collective-permute-start(f32[2,4,66,1]{3,2,1,0:T(8,128)S(1)} %get-tuple-element.1164), channel_id=1, source_target_pairs={{0,1},{1,2},{2,3},{4,5},{5,6},{6,7},{8,9},{9,10},{10,11},{12,13},{... | collective-permute-start | bytes 6344 | tf_op jit(solution)/shard_map/while/body/eval_jaxpr/ppermute | solution.py:15
  132.6 5.9 collective-permute-start.13
  138.6 7.2 %collective-permute-start.14 = (f32[2,4,66,1]{3,2,1,0:T(8,128)S(1)}, f32[2,4,66,1]{3,2,1,0:T(8,128)S(1)}, u32[]{:S(2)}, u32[]{:S(2)}) collective-permute-start(f32[2,4,66,1]{3,2,1,0:T(8,128)S(1)} %get-tuple-element.1170), channel_id=1, source_target_pairs={{0,1},{1,2},{2,3},{4,5},{5,6},{6,7},{8,9},{9,10},{10,11},{12,13},{... | collective-permute-start | bytes 6344 | tf_op jit(solution)/shard_map/while/body/eval_jaxpr/ppermute | solution.py:15
  148.9 8.3 %collective-permute-start.65 = (f32[2,4,64,128]{3,2,1,0:T(8,128)S(1)}, f32[2,4,64,128]{3,2,1,0:T(8,128)S(1)}, u32[]{:S(2)}, u32[]{:S(2)}) collective-permute-start(f32[2,4,64,128]{3,2,1,0:T(8,128)S(1)} %slice_bitcast_fusion.4), channel_id=1, source_target_pairs={{0,8},{8,16},{16,24},{1,9},{9,17},{17,25},{2,10},{10,18},{18,26},{... | collective-permute-start | bytes 786440 | tf_op jit(solution)/shard_map/ppermute | solution.py:27
  158.6 5.9 collective-permute-start.17
  164.6 6.3 %collective-permute-start.18 = (f32[2,4,66,1]{3,2,1,0:T(8,128)S(1)}, f32[2,4,66,1]{3,2,1,0:T(8,128)S(1)}, u32[]{:S(2)}, u32[]{:S(2)}) collective-permute-start(f32[2,4,66,1]{3,2,1,0:T(8,128)S(1)} %get-tuple-element.1187), channel_id=1, source_target_pairs={{0,1},{1,2},{2,3},{4,5},{5,6},{6,7},{8,9},{9,10},{10,11},{12,13},{... | collective-permute-start | bytes 6344 | tf_op jit(solution)/shard_map/while/body/eval_jaxpr/ppermute | solution.py:15
  176.1 5.9 collective-permute-start.21
  182.1 7.2 %collective-permute-start.22 = (f32[2,4,66,1]{3,2,1,0:T(8,128)S(1)}, f32[2,4,66,1]{3,2,1,0:T(8,128)S(1)}, u32[]{:S(2)}, u32[]{:S(2)}) collective-permute-start(f32[2,4,66,1]{3,2,1,0:T(8,128)S(1)} %get-tuple-element.1193), channel_id=1, source_target_pairs={{0,1},{1,2},{2,3},{4,5},{5,6},{6,7},{8,9},{9,10},{10,11},{12,13},{... | collective-permute-start | bytes 6344 | tf_op jit(solution)/shard_map/while/body/eval_jaxpr/ppermute | solution.py:15
  193.8 5.9 collective-permute-start.17
  199.8 7.2 %collective-permute-start.18 = (f32[2,4,66,1]{3,2,1,0:T(8,128)S(1)}, f32[2,4,66,1]{3,2,1,0:T(8,128)S(1)}, u32[]{:S(2)}, u32[]{:S(2)}) collective-permute-start(f32[2,4,66,1]{3,2,1,0:T(8,128)S(1)} %get-tuple-element.1187), channel_id=1, source_target_pairs={{0,1},{1,2},{2,3},{4,5},{5,6},{6,7},{8,9},{9,10},{10,11},{12,13},{... | collective-permute-start | bytes 6344 | tf_op jit(solution)/shard_map/while/body/eval_jaxpr/ppermute | solution.py:15
  211.3 5.9 collective-permute-start.21
  217.3 7.2 %collective-permute-start.22 = (f32[2,4,66,1]{3,2,1,0:T(8,128)S(1)}, f32[2,4,66,1]{3,2,1,0:T(8,128)S(1)}, u32[]{:S(2)}, u32[]{:S(2)}) collective-permute-start(f32[2,4,66,1]{3,2,1,0:T(8,128)S(1)} %get-tuple-element.1193), channel_id=1, source_target_pairs={{0,1},{1,2},{2,3},{4,5},{5,6},{6,7},{8,9},{9,10},{10,11},{12,13},{... | collective-permute-start | bytes 6344 | tf_op jit(solution)/shard_map/while/body/eval_jaxpr/ppermute | solution.py:15
  227.5 8.3 %collective-permute-start.66 = (f32[2,4,64,128]{3,2,1,0:T(8,128)S(1)}, f32[2,4,64,128]{3,2,1,0:T(8,128)S(1)}, u32[]{:S(2)}, u32[]{:S(2)}) collective-permute-start(f32[2,4,64,128]{3,2,1,0:T(8,128)S(1)} %slice_bitcast_fusion.3), channel_id=1, source_target_pairs={{0,8},{8,16},{16,24},{1,9},{9,17},{17,25},{2,10},{10,18},{18,26},{... | collective-permute-start | bytes 786440 | tf_op jit(solution)/shard_map/ppermute | solution.py:27
  237.3 5.9 collective-permute-start.25
  243.3 6.3 %collective-permute-start.26 = (f32[2,4,66,1]{3,2,1,0:T(8,128)S(1)}, f32[2,4,66,1]{3,2,1,0:T(8,128)S(1)}, u32[]{:S(2)}, u32[]{:S(2)}) collective-permute-start(f32[2,4,66,1]{3,2,1,0:T(8,128)S(1)} %get-tuple-element.1210), channel_id=1, source_target_pairs={{0,1},{1,2},{2,3},{4,5},{5,6},{6,7},{8,9},{9,10},{10,11},{12,13},{... | collective-permute-start | bytes 6344 | tf_op jit(solution)/shard_map/while/body/eval_jaxpr/ppermute | solution.py:15
  254.8 5.9 collective-permute-start.29
  260.8 7.2 %collective-permute-start.30 = (f32[2,4,66,1]{3,2,1,0:T(8,128)S(1)}, f32[2,4,66,1]{3,2,1,0:T(8,128)S(1)}, u32[]{:S(2)}, u32[]{:S(2)}) collective-permute-start(f32[2,4,66,1]{3,2,1,0:T(8,128)S(1)} %get-tuple-element.1216), channel_id=1, source_target_pairs={{0,1},{1,2},{2,3},{4,5},{5,6},{6,7},{8,9},{9,10},{10,11},{12,13},{... | collective-permute-start | bytes 6344 | tf_op jit(solution)/shard_map/while/body/eval_jaxpr/ppermute | solution.py:15
  272.4 5.9 collective-permute-start.25
  278.5 7.2 %collective-permute-start.26 = (f32[2,4,66,1]{3,2,1,0:T(8,128)S(1)}, f32[2,4,66,1]{3,2,1,0:T(8,128)S(1)}, u32[]{:S(2)}, u32[]{:S(2)}) collective-permute-start(f32[2,4,66,1]{3,2,1,0:T(8,128)S(1)} %get-tuple-element.1210), channel_id=1, source_target_pairs={{0,1},{1,2},{2,3},{4,5},{5,6},{6,7},{8,9},{9,10},{10,11},{12,13},{... | collective-permute-start | bytes 6344 | tf_op jit(solution)/shard_map/while/body/eval_jaxpr/ppermute | solution.py:15
  289.9 5.9 collective-permute-start.29
  296.0 7.2 %collective-permute-start.30 = (f32[2,4,66,1]{3,2,1,0:T(8,128)S(1)}, f32[2,4,66,1]{3,2,1,0:T(8,128)S(1)}, u32[]{:S(2)}, u32[]{:S(2)}) collective-permute-start(f32[2,4,66,1]{3,2,1,0:T(8,128)S(1)} %get-tuple-element.1216), channel_id=1, source_target_pairs={{0,1},{1,2},{2,3},{4,5},{5,6},{6,7},{8,9},{9,10},{10,11},{12,13},{... | collective-permute-start | bytes 6344 | tf_op jit(solution)/shard_map/while/body/eval_jaxpr/ppermute | solution.py:15
  309.0 5.9 collective-permute-start.33
  315.0 7.2 %collective-permute-start.34 = (f32[2,4,66,1]{3,2,1,0:T(8,128)S(1)}, f32[2,4,66,1]{3,2,1,0:T(8,128)S(1)}, u32[]{:S(2)}, u32[]{:S(2)}) collective-permute-start(f32[2,4,66,1]{3,2,1,0:T(8,128)S(1)} %get-tuple-element.1233), channel_id=1, source_target_pairs={{0,1},{1,2},{2,3},{4,5},{5,6},{6,7},{8,9},{9,10},{10,11},{12,13},{... | collective-permute-start | bytes 6344 | tf_op jit(solution)/shard_map/while/body/eval_jaxpr/ppermute | solution.py:15
  326.5 5.9 collective-permute-start.37
  332.5 7.2 %collective-permute-start.38 = (f32[2,4,66,1]{3,2,1,0:T(8,128)S(1)}, f32[2,4,66,1]{3,2,1,0:T(8,128)S(1)}, u32[]{:S(2)}, u32[]{:S(2)}) collective-permute-start(f32[2,4,66,1]{3,2,1,0:T(8,128)S(1)} %get-tuple-element.1239), channel_id=1, source_target_pairs={{0,1},{1,2},{2,3},{4,5},{5,6},{6,7},{8,9},{9,10},{10,11},{12,13},{... | collective-permute-start | bytes 6344 | tf_op jit(solution)/shard_map/while/body/eval_jaxpr/ppermute | solution.py:15
  344.2 5.9 collective-permute-start.33
  350.2 7.2 %collective-permute-start.34 = (f32[2,4,66,1]{3,2,1,0:T(8,128)S(1)}, f32[2,4,66,1]{3,2,1,0:T(8,128)S(1)}, u32[]{:S(2)}, u32[]{:S(2)}) collective-permute-start(f32[2,4,66,1]{3,2,1,0:T(8,128)S(1)} %get-tuple-element.1233), channel_id=1, source_target_pairs={{0,1},{1,2},{2,3},{4,5},{5,6},{6,7},{8,9},{9,10},{10,11},{12,13},{... | collective-permute-start | bytes 6344 | tf_op jit(solution)/shard_map/while/body/eval_jaxpr/ppermute | solution.py:15
  361.7 5.9 collective-permute-start.37
  367.7 7.2 %collective-permute-start.38 = (f32[2,4,66,1]{3,2,1,0:T(8,128)S(1)}, f32[2,4,66,1]{3,2,1,0:T(8,128)S(1)}, u32[]{:S(2)}, u32[]{:S(2)}) collective-permute-start(f32[2,4,66,1]{3,2,1,0:T(8,128)S(1)} %get-tuple-element.1239), channel_id=1, source_target_pairs={{0,1},{1,2},{2,3},{4,5},{5,6},{6,7},{8,9},{9,10},{10,11},{12,13},{... | collective-permute-start | bytes 6344 | tf_op jit(solution)/shard_map/while/body/eval_jaxpr/ppermute | solution.py:15
  377.9 8.7 %collective-permute-start.67 = (f32[2,4,64,128]{3,2,1,0:T(8,128)S(1)}, f32[2,4,64,128]{3,2,1,0:T(8,128)S(1)}, u32[]{:S(2)}, u32[]{:S(2)}) collective-permute-start(f32[2,4,64,128]{3,2,1,0:T(8,128)S(1)} %slice_bitcast_fusion.2), channel_id=1, source_target_pairs={{8,0},{16,8},{24,16},{9,1},{17,9},{25,17},{10,2},{18,10},{26,18},{... | collective-permute-start | bytes 786440 | tf_op jit(solution)/shard_map/ppermute | solution.py:27
  388.2 5.9 collective-permute-start.41
  394.2 6.3 %collective-permute-start.42 = (f32[2,4,66,1]{3,2,1,0:T(8,128)S(1)}, f32[2,4,66,1]{3,2,1,0:T(8,128)S(1)}, u32[]{:S(2)}, u32[]{:S(2)}) collective-permute-start(f32[2,4,66,1]{3,2,1,0:T(8,128)S(1)} %get-tuple-element.1256), channel_id=1, source_target_pairs={{0,1},{1,2},{2,3},{4,5},{5,6},{6,7},{8,9},{9,10},{10,11},{12,13},{... | collective-permute-start | bytes 6344 | tf_op jit(solution)/shard_map/while/body/eval_jaxpr/ppermute | solution.py:15
  405.6 5.9 collective-permute-start.45
  411.7 7.2 %collective-permute-start.46 = (f32[2,4,66,1]{3,2,1,0:T(8,128)S(1)}, f32[2,4,66,1]{3,2,1,0:T(8,128)S(1)}, u32[]{:S(2)}, u32[]{:S(2)}) collective-permute-start(f32[2,4,66,1]{3,2,1,0:T(8,128)S(1)} %get-tuple-element.1262), channel_id=1, source_target_pairs={{0,1},{1,2},{2,3},{4,5},{5,6},{6,7},{8,9},{9,10},{10,11},{12,13},{... | collective-permute-start | bytes 6344 | tf_op jit(solution)/shard_map/while/body/eval_jaxpr/ppermute | solution.py:15
  423.3 5.9 collective-permute-start.41
  429.4 7.2 %collective-permute-start.42 = (f32[2,4,66,1]{3,2,1,0:T(8,128)S(1)}, f32[2,4,66,1]{3,2,1,0:T(8,128)S(1)}, u32[]{:S(2)}, u32[]{:S(2)}) collective-permute-start(f32[2,4,66,1]{3,2,1,0:T(8,128)S(1)} %get-tuple-element.1256), channel_id=1, source_target_pairs={{0,1},{1,2},{2,3},{4,5},{5,6},{6,7},{8,9},{9,10},{10,11},{12,13},{... | collective-permute-start | bytes 6344 | tf_op jit(solution)/shard_map/while/body/eval_jaxpr/ppermute | solution.py:15
  446.9 7.2 %collective-permute-start.46 = (f32[2,4,66,1]{3,2,1,0:T(8,128)S(1)}, f32[2,4,66,1]{3,2,1,0:T(8,128)S(1)}, u32[]{:S(2)}, u32[]{:S(2)}) collective-permute-start(f32[2,4,66,1]{3,2,1,0:T(8,128)S(1)} %get-tuple-element.1262), channel_id=1, source_target_pairs={{0,1},{1,2},{2,3},{4,5},{5,6},{6,7},{8,9},{9,10},{10,11},{12,13},{... | collective-permute-start | bytes 6344 | tf_op jit(solution)/shard_map/while/body/eval_jaxpr/ppermute | solution.py:15
  457.1 8.3 %collective-permute-start.68 = (f32[2,4,64,128]{3,2,1,0:T(8,128)S(1)}, f32[2,4,64,128]{3,2,1,0:T(8,128)S(1)}, u32[]{:S(2)}, u32[]{:S(2)}) collective-permute-start(f32[2,4,64,128]{3,2,1,0:T(8,128)S(1)} %slice_bitcast_fusion.1), channel_id=1, source_target_pairs={{8,0},{16,8},{24,16},{9,1},{17,9},{25,17},{10,2},{18,10},{26,18},{... | collective-permute-start | bytes 786440 | tf_op jit(solution)/shard_map/ppermute | solution.py:27
  472.9 6.3 %collective-permute-start.50 = (f32[2,4,66,1]{3,2,1,0:T(8,128)S(1)}, f32[2,4,66,1]{3,2,1,0:T(8,128)S(1)}, u32[]{:S(2)}, u32[]{:S(2)}) collective-permute-start(f32[2,4,66,1]{3,2,1,0:T(8,128)S(1)} %get-tuple-element.1279), channel_id=1, source_target_pairs={{0,1},{1,2},{2,3},{4,5},{5,6},{6,7},{8,9},{9,10},{10,11},{12,13},{... | collective-permute-start | bytes 6344 | tf_op jit(solution)/shard_map/while/body/eval_jaxpr/ppermute | solution.py:15
  490.4 7.2 %collective-permute-start.54 = (f32[2,4,66,1]{3,2,1,0:T(8,128)S(1)}, f32[2,4,66,1]{3,2,1,0:T(8,128)S(1)}, u32[]{:S(2)}, u32[]{:S(2)}) collective-permute-start(f32[2,4,66,1]{3,2,1,0:T(8,128)S(1)} %get-tuple-element.1285), channel_id=1, source_target_pairs={{0,1},{1,2},{2,3},{4,5},{5,6},{6,7},{8,9},{9,10},{10,11},{12,13},{... | collective-permute-start | bytes 6344 | tf_op jit(solution)/shard_map/while/body/eval_jaxpr/ppermute | solution.py:15
  508.0 7.2 %collective-permute-start.50 = (f32[2,4,66,1]{3,2,1,0:T(8,128)S(1)}, f32[2,4,66,1]{3,2,1,0:T(8,128)S(1)}, u32[]{:S(2)}, u32[]{:S(2)}) collective-permute-start(f32[2,4,66,1]{3,2,1,0:T(8,128)S(1)} %get-tuple-element.1279), channel_id=1, source_target_pairs={{0,1},{1,2},{2,3},{4,5},{5,6},{6,7},{8,9},{9,10},{10,11},{12,13},{... | collective-permute-start | bytes 6344 | tf_op jit(solution)/shard_map/while/body/eval_jaxpr/ppermute | solution.py:15
  525.5 7.2 %collective-permute-start.54 = (f32[2,4,66,1]{3,2,1,0:T(8,128)S(1)}, f32[2,4,66,1]{3,2,1,0:T(8,128)S(1)}, u32[]{:S(2)}, u32[]{:S(2)}) collective-permute-start(f32[2,4,66,1]{3,2,1,0:T(8,128)S(1)} %get-tuple-element.1285), channel_id=1, source_target_pairs={{0,1},{1,2},{2,3},{4,5},{5,6},{6,7},{8,9},{9,10},{10,11},{12,13},{... | collective-permute-start | bytes 6344 | tf_op jit(solution)/shard_map/while/body/eval_jaxpr/ppermute | solution.py:15
  535.8 8.3 %collective-permute-start.69 = (f32[2,4,64,128]{3,2,1,0:T(8,128)S(1)}, f32[2,4,64,128]{3,2,1,0:T(8,128)S(1)}, u32[]{:S(2)}, u32[]{:S(2)}) collective-permute-start(f32[2,4,64,128]{3,2,1,0:T(8,128)S(1)} %slice_bitcast_fusion), channel_id=1, source_target_pairs={{8,0},{16,8},{24,16},{9,1},{17,9},{25,17},{10,2},{18,10},{26,18},{... | collective-permute-start | bytes 786440 | tf_op jit(solution)/shard_map/ppermute | solution.py:27
  545.5 5.9 collective-permute-start.57
  551.6 6.3 %collective-permute-start.58 = (f32[2,4,66,1]{3,2,1,0:T(8,128)S(1)}, f32[2,4,66,1]{3,2,1,0:T(8,128)S(1)}, u32[]{:S(2)}, u32[]{:S(2)}) collective-permute-start(f32[2,4,66,1]{3,2,1,0:T(8,128)S(1)} %get-tuple-element.1302), channel_id=1, source_target_pairs={{0,1},{1,2},{2,3},{4,5},{5,6},{6,7},{8,9},{9,10},{10,11},{12,13},{... | collective-permute-start | bytes 6344 | tf_op jit(solution)/shard_map/while/body/eval_jaxpr/ppermute | solution.py:15
  569.1 7.2 %collective-permute-start.62 = (f32[2,4,66,1]{3,2,1,0:T(8,128)S(1)}, f32[2,4,66,1]{3,2,1,0:T(8,128)S(1)}, u32[]{:S(2)}, u32[]{:S(2)}) collective-permute-start(f32[2,4,66,1]{3,2,1,0:T(8,128)S(1)} %get-tuple-element.1308), channel_id=1, source_target_pairs={{0,1},{1,2},{2,3},{4,5},{5,6},{6,7},{8,9},{9,10},{10,11},{12,13},{... | collective-permute-start | bytes 6344 | tf_op jit(solution)/shard_map/while/body/eval_jaxpr/ppermute | solution.py:15
  586.7 7.2 %collective-permute-start.58 = (f32[2,4,66,1]{3,2,1,0:T(8,128)S(1)}, f32[2,4,66,1]{3,2,1,0:T(8,128)S(1)}, u32[]{:S(2)}, u32[]{:S(2)}) collective-permute-start(f32[2,4,66,1]{3,2,1,0:T(8,128)S(1)} %get-tuple-element.1302), channel_id=1, source_target_pairs={{0,1},{1,2},{2,3},{4,5},{5,6},{6,7},{8,9},{9,10},{10,11},{12,13},{... | collective-permute-start | bytes 6344 | tf_op jit(solution)/shard_map/while/body/eval_jaxpr/ppermute | solution.py:15
  598.2 5.9 collective-permute-start.61
  604.2 7.2 %collective-permute-start.62 = (f32[2,4,66,1]{3,2,1,0:T(8,128)S(1)}, f32[2,4,66,1]{3,2,1,0:T(8,128)S(1)}, u32[]{:S(2)}, u32[]{:S(2)}) collective-permute-start(f32[2,4,66,1]{3,2,1,0:T(8,128)S(1)} %get-tuple-element.1308), channel_id=1, source_target_pairs={{0,1},{1,2},{2,3},{4,5},{5,6},{6,7},{8,9},{9,10},{10,11},{12,13},{... | collective-permute-start | bytes 6344 | tf_op jit(solution)/shard_map/while/body/eval_jaxpr/ppermute | solution.py:15
  (72 other events, 661.6 us)
where the time goes:
time: 623 us; the launch traced here: 615 us
  starting transfers between devices  422 us (68%)
  waiting for transfers between devices  166 us (27%)
  other arithmetic  16.4 us (3%)
    ppermute x64, starting transfers between devices, with_halo(): lax.ppermute(tail, axis, [(i, (i + 1) % count) for i in range(ends)])  323 us
    ppermute x64, waiting for transfers between devices, with_halo(): lax.ppermute(head, axis, [((i + 1) % count, i) for i in range(ends)])  91.7 us
    ppermute x64, starting transfers between devices, with_halo(): lax.ppermute(head, axis, [((i + 1) % count, i) for i in range(ends)])  82.7 us
    ppermute x64, waiting for transfers between devices, with_halo(): lax.ppermute(tail, axis, [(i, (i + 1) % count) for i in range(ends)])  41.7 us
    ppermute x6, waiting for transfers between devices, shifted(): return lax.ppermute(block, axis, route)  32.7 us
    ppermute x6, starting transfers between devices, shifted(): return lax.ppermute(block, axis, route)  16.4 us
  transfers between devices with their start and end apart: 134, of which 70 were waited for; matrix products, arithmetic and copies ran while one was open for 0% of the time, Pallas kernels for 0%

commit v1 on v0

v1 whole, which is shorter than its diff:
```python
import jax
import jax.numpy as jnp
from jax import lax
from jax.experimental import pallas as pl
from jax.experimental.pallas import tpu as pltpu
from jax.sharding import PartitionSpec as P

MEMBERS = 4
WIDE = 32
NARROW = 16
LANES = 128

VMEM = pltpu.VMEM
F32 = jnp.float32


def lane_ids(shape):
    return lax.broadcasted_iota(jnp.int32, shape, len(shape) - 1)


def call(kernel, outs, meta, *operands, scratch=()):
    return pl.pallas_call(
        kernel,
        out_shape=[jax.ShapeDtypeStruct(shape, F32) for shape in outs],
        in_specs=[pl.BlockSpec(memory_space=pltpu.SMEM)]
        + [pl.BlockSpec(memory_space=VMEM)] * len(operands),
        out_specs=[pl.BlockSpec(memory_space=VMEM)] * len(outs),
        scratch_shapes=list(scratch),
        compiler_params=pltpu.CompilerParams(vmem_limit_bytes=48 * 1024 * 1024),
    )(meta, *operands)


def member_swap(block, offset):
    nz, nx = lax.axis_size("depth"), lax.axis_size("gx")
    dz, dx = offset >> 1, offset & 1
    pairs = [(z * nx + x, (z ^ dz) * nx + (x ^ dx)) for z in range(nz) for x in range(nx)]
    return lax.ppermute(block, ("depth", "gx"), pairs)


def depth_pair_swap(block):
    return lax.ppermute(block, "depth", [(z, z ^ 2) for z in range(lax.axis_size("depth"))])


def neighbour_swaps(first, second, axis, stride):
    size = lax.axis_size(axis)
    count = size // stride

    def pairs(start):
        found = []
        for low in range(start, count - 1, 2):
            for part in range(stride):
                a, b = low * stride + part, (low + 1) * stride + part
                found += [(a, b), (b, a)]
        return found

    got_first = lax.ppermute(first, axis, pairs(0)) if count > 1 else jnp.zeros_like(first)
    got_second = lax.ppermute(second, axis, pairs(1)) if count > 2 else jnp.zeros_like(second)
    return got_first, got_second


def with_row_halo(block, width):
    groups = lax.axis_size("gx") // 2
    if groups == 1:
        return block
    even = (lax.axis_index("gx") // 2) % 2 == 0
    top, bottom = block[..., :width, :], block[..., -width:, :]
    one, two = neighbour_swaps(
        jnp.where(even, bottom, top), jnp.where(even, top, bottom), "gx", 2
    )
    above, below = jnp.where(even, two, one), jnp.where(even, one, two)
    return jnp.concatenate([above, block, below], axis=-2)


def merge_members(meta, pieces, out):
    me = meta[0]
    for k, piece in enumerate(pieces):
        fields, planes, _, rows, _ = piece.shape
        who = me ^ k
        at_plane = (who // 2) * planes
        at_row = pl.multiple_of((who % 2) * rows, rows)
        for f in range(fields):
            for p in range(planes):
                for c in range(2):
                    out[f, at_plane + p, c, pl.ds(at_row, rows), :] = piece[f, p, c]


def pack_edges(meta, tiles, width, first, second):
    even = meta[1] == 0
    lanes = lane_ids(tiles[0].shape)
    left = right = None
    for j, tile in enumerate(tiles):
        at = j * width
        from_left = pltpu.roll(tile, at, 1) if at else tile
        turn = (at + width) % LANES
        from_right = pltpu.roll(tile, turn, 1) if turn else tile
        if left is None:
            left, right = from_left, from_right
        else:
            left = jnp.where(lanes >= at, from_left, left)
            right = jnp.where(lanes >= at, from_right, right)
    first[...] = jnp.where(even, right, left)
    second[...] = jnp.where(even, left, right)


def unpack_edges(meta, first, second, j, width):
    even = meta[1] == 0
    right, left = jnp.where(even, first, second), jnp.where(even, second, first)
    lanes = lane_ids(first.shape)
    at = j * width
    right = pltpu.roll(right, LANES - at, 1) if at else right
    turn = (LANES - width - at) % LANES
    left = pltpu.roll(left, turn, 1) if turn else left
    return jnp.where(lanes < width, right, jnp.where(lanes >= LANES - width, left, 0.0))


def pack_carry(field, at, out):
    real, imag = field[at, 0, :, LANES:], field[at, 1, :, LANES:]
    lanes = lane_ids(real.shape)
    middle = (lanes >= WIDE) & (lanes < LANES - WIDE)
    out[0] = field[at, 0, :, :LANES]
    out[1] = field[at, 1, :, :LANES]
    out[2] = jnp.where(middle, pltpu.roll(imag, LANES // 2, 1), real)


def unpack_carry(packed, use, out):
    edges = packed[2]
    lanes = lane_ids(edges.shape)
    middle = (lanes >= WIDE) & (lanes < LANES - WIDE)
    keep = use & jnp.logical_not(middle)
    for c in range(2):
        out[c, :, :LANES] = jnp.where(use, packed[c], 0.0)
        out[c, :, LANES:] = jnp.where(keep, pltpu.roll(edges, LANES // 2, 1) if c else edges, 0.0)


def times(a, b, q_real, q_imag, sign):
    if sign > 0:
        return a * q_real - b * q_imag, a * q_imag + b * q_real
    return a * q_real + b * q_imag, b * q_real - a * q_imag


def sweep(drive, inverse, out, carry, work, planes, rows, reverse):
    rhs, ping, pong = work
    sign = -1 if reverse else 1
    zeros = jnp.zeros((8, 2 * LANES), F32)
    for buffer in (ping, pong):
        for c in range(2):
            buffer[c, :8, :] = zeros
            buffer[c, rows + 8 : rows + 16, :] = zeros

    def beside(buffer, c, r):
        here = buffer[c, r + 8 : r + 16, :]
        return (
            buffer[c, r + 7 : r + 15, :]
            + buffer[c, r + 9 : r + 17, :]
            + (pltpu.roll(here, 1, 1) + pltpu.roll(here, 2 * LANES - 1, 1))
        )

    def plane(step, _):
        z = planes - 1 - step if reverse else step
        for r in range(0, rows, 8):
            strip = slice(r, r + 8)
            a = drive[z, 0, strip, :] + 2.5 * carry[0, strip, :]
            b = drive[z, 1, strip, :] + 2.5 * carry[1, strip, :]
            rhs[0, strip, :] = a
            rhs[1, strip, :] = b
            a, b = times(a, b, inverse[z, 0, strip, :], inverse[z, 1, strip, :], sign)
            ping[0, r + 8 : r + 16, :] = a
            ping[1, r + 8 : r + 16, :] = b
        for r in range(0, rows, 8):
            strip = slice(r, r + 8)
            a = rhs[0, strip, :] + beside(ping, 0, r)
            b = rhs[1, strip, :] + beside(ping, 1, r)
            a, b = times(a, b, inverse[z, 0, strip, :], inverse[z, 1, strip, :], sign)
            pong[0, r + 8 : r + 16, :] = a
            pong[1, r + 8 : r + 16, :] = b
        for r in range(0, rows, 8):
            strip = slice(r, r + 8)
            a = rhs[0, strip, :] + beside(pong, 0, r)
            b = rhs[1, strip, :] + beside(pong, 1, r)
            a, b = times(a, b, inverse[z, 0, strip, :], inverse[z, 1, strip, :], sign)
            out[z, 0, strip, :] = a
            out[z, 1, strip, :] = b
            carry[0, strip, :] = a
            carry[1, strip, :] = b
        return 0

    lax.fori_loop(0, planes, plane, 0)


def sweep_scratch(rows):
    wide = 2 * LANES
    return [
        VMEM((2, rows, wide), F32),
        VMEM((2, rows, wide), F32),
        VMEM((2, rows + 16, wide), F32),
        VMEM((2, rows + 16, wide), F32),
    ]


def prepare_kernel(meta, source, wavenumber, damping, *sends):
    real_diag = 6.0 - wavenumber[...]
    damp = damping[...]
    denom = real_diag * real_diag + damp * damp
    real = real_diag / denom
    imag = -(damp / denom)
    for k, send in enumerate(sends):
        send[0] = source[:, :, meta[0] ^ k]
        send[1, :, 0] = real
        send[1, :, 1] = imag


def prepare_observed_kernel(meta, observed, *sends):
    for k, send in enumerate(sends):
        send[0] = observed[:, :, meta[0] ^ k]


def merge_kernel(meta, *refs):
    merge_members(meta, refs[:MEMBERS], refs[MEMBERS])


def pack_wide(meta, merged, first, second):
    for f in range(2):
        for c in range(2):
            tiles = [merged[f, p, c] for p in range(merged.shape[1])]
            pack_edges(meta, tiles, WIDE, first.at[f, c], second.at[f, c])


def pack_narrow(meta, merged, first, second):
    tiles = [merged[0, p, c] for p in range(merged.shape[1]) for c in range(2)]
    pack_edges(meta, tiles, NARROW, first, second)


def widen(merged, edges, outs):
    for f, out in enumerate(outs):
        for p in range(merged.shape[1]):
            for c in range(2):
                out[p, c, :, :LANES] = merged[f, p, c]
                out[p, c, :, LANES:] = edges(f, p, c)


def forward_kernel(meta, merged, first, second, drive, inverse, send, field, carry, *work):
    planes, rows = merged.shape[1], merged.shape[3]
    widen(
        merged,
        lambda f, p, c: unpack_edges(meta, first[f, c], second[f, c], p, WIDE),
        (drive, inverse),
    )
    carry[...] = jnp.zeros_like(carry)
    sweep(drive, inverse, field, carry, work, planes, rows, False)
    pack_carry(field, planes - 1, send)


def turn_kernel(
    height, meta, drive, inverse, got, observed, first, second, field, residual, send, *rest
):
    pieces, (adjoint, carry, *work) = rest[:MEMBERS], rest[MEMBERS:]
    planes, rows = drive.shape[0], drive.shape[2]
    margin = (rows - 2 * height) // 2
    unpack_carry(got, meta[2] == 1, carry)
    sweep(drive, inverse, field, carry, work, planes, rows, False)
    for p in range(planes):
        for c in range(2):
            edges = unpack_edges(meta, first[...], second[...], 2 * p + c, NARROW)
            residual[p, c, :, :LANES] = field[p, c, :, :LANES] - observed[0, p, c]
            residual[p, c, :, LANES:] = field[p, c, :, LANES:] - edges
    carry[...] = jnp.zeros_like(carry)
    sweep(residual, inverse, adjoint, carry, work, planes, rows, True)
    pack_carry(adjoint, 0, send)
    for k, piece in enumerate(pieces):
        who = meta[0] ^ k
        at_plane = (who // 2) * (planes // 2)
        at_row = pl.multiple_of((who % 2) * height + margin, 8)
        for p in range(planes // 2):
            for c in range(2):
                piece[p, c] = field[at_plane + p, c, pl.ds(at_row, height), :LANES]


def adjoint_kernel(height, meta, residual, inverse, got, field, *rest):
    pieces, (adjoint, carry, *work) = rest[:MEMBERS], rest[MEMBERS:]
    planes, rows = residual.shape[0], residual.shape[2]
    margin = (rows - 2 * height) // 2
    unpack_carry(got, meta[2] == 0, carry)
    sweep(residual, inverse, adjoint, carry, work, planes, rows, True)
    for k, piece in enumerate(pieces):
        who = meta[0] ^ k
        at_plane = (who // 2) * (planes // 2)
        at_row = pl.multiple_of((who % 2) * height + margin, 8)
        for p in range(planes // 2):
            total = 0.0
            for c in range(2):
                total += (
                    field[at_plane + p, c, pl.ds(at_row, height), :LANES]
                    * adjoint[at_plane + p, c, pl.ds(at_row, height), :LANES]
                )
            piece[p] = total * (1.0 / MEMBERS)


def field_kernel(meta, *refs):
    out = refs[MEMBERS]
    for k, piece in enumerate(refs[:MEMBERS]):
        out[:, :, meta[0] ^ k] = piece[...]


def body(source, observed, wavenumber, damping):
    own_planes, _, shots, height, width = source.shape
    zi, xi, yi = (lax.axis_index(a) for a in ("depth", "gx", "gy"))
    meta = jnp.stack([2 * (zi % 2) + xi % 2, yi % 2, zi // 2]).astype(jnp.int32)
    planes, high = 2 * own_planes, 2 * height
    one_group = lax.axis_size("gx") == 2
    rows = high if one_group else high + 2 * WIDE
    tile = (own_planes, 2, height, width)
    all_ks = range(1, MEMBERS)

    def gathered(sends, fields, pack, edge_shape):
        pieces = [sends[0]] + [member_swap(sends[k], k) for k in all_ks]
        merged_shape = (fields, planes, 2, high, width)
        if one_group:

            def merge_pack(meta, *refs):
                merge_members(meta, refs[:MEMBERS], refs[MEMBERS])
                pack(meta, *refs[MEMBERS:])

            merged, first, second = call(
                merge_pack, [merged_shape, edge_shape, edge_shape], meta, *pieces
            )
        else:
            merged = with_row_halo(call(merge_kernel, [merged_shape], meta, *pieces)[0], WIDE)
            first, second = call(pack, [edge_shape, edge_shape], meta, merged)
        return merged, *neighbour_swaps(first, second, "gy", 1)

    sends = call(prepare_kernel, [(2, *tile)] * MEMBERS, meta, source, wavenumber, damping)
    merged, first, second = gathered(sends, 2, pack_wide, (2, 2, rows, width))
    seen_sends = call(prepare_observed_kernel, [(1, *tile)] * MEMBERS, meta, observed)
    seen, seen_first, seen_second = gathered(seen_sends, 1, pack_narrow, (rows, width))

    whole = (planes, 2, rows, 2 * width)
    packed = (3, rows, width)
    drive, inverse, send = call(
        forward_kernel,
        [whole, whole, packed],
        meta,
        merged,
        first,
        second,
        scratch=[VMEM(whole, F32), *sweep_scratch(rows)],
    )
    got = depth_pair_swap(send)
    field, residual, send, *pieces = call(
        lambda *refs: turn_kernel(height, *refs),
        [whole, whole, packed] + [tile] * MEMBERS,
        meta,
        drive,
        inverse,
        got,
        seen,
        seen_first,
        seen_second,
        scratch=[VMEM(whole, F32), *sweep_scratch(rows)],
    )
    got = depth_pair_swap(send)
    pieces = [pieces[0]] + [member_swap(pieces[k], k) for k in all_ks]
    sums = call(
        lambda *refs: adjoint_kernel(height, *refs),
        [(own_planes, height, width)] * MEMBERS,
        meta,
        residual,
        inverse,
        got,
        field,
        scratch=[VMEM(whole, F32), *sweep_scratch(rows)],
    )
    gradient = sums[0]
    for k in all_ks:
        gradient = gradient + member_swap(sums[k], k)
    (forward_field,) = call(field_kernel, [source.shape], meta, *pieces)
    return forward_field, gradient


def solution(mesh):
    lateral = P("depth", None, None, "gx", "gy")
    return jax.shard_map(
        body,
        mesh=mesh,
        in_specs=(lateral, lateral, P("depth", "gx", "gy"), P("depth", "gx", "gy")),
        out_specs=(lateral, P("depth", "gx", "gy")),
        check_vma=False,
    )
```

time: 623 us -> 67.9 us (0.11); the launches traced: 615 us -> 67.6 us
  starting transfers between devices: 422 us -> 26.1 us
  waiting for transfers between devices: 166 us -> 23.6 us
  other arithmetic: 16.4 us -> 0.72 us
  Pallas kernels: 0 us -> 13.8 us
    ppermute x134 -> x18, starting transfers between devices: 422 us -> 26.1 us  [the longest x12 19.7 us: member_swap(): return lax.ppermute(block, ('depth', 'gx'), pairs)]
    ppermute x134 -> x18, waiting for transfers between devices: 166 us -> 23.6 us  [the longest x12 14.9 us: member_swap(): return lax.ppermute(block, ('depth', 'gx'), pairs)]
    pallas_call x0 -> x8, Pallas kernels: none -> 13.8 us  [call(): pl.pallas_call(kernel, out_shape=[jax.ShapeDtypeStruct(shape, F32) for sh...]
    add x48 -> x1, other arithmetic: 9.86 us -> 0.64 us  [body(): gradient = gradient + member_swap(sums[k], k)]
  transfers between devices with their start and end apart: 134 -> 18, of which waited for: 70 -> 9; matrix products, arithmetic and copies ran while one was open for 0% -> 0% of each run, Pallas kernels for 0% -> 12%
where the time goes in v1:
time: 67.9 us; the launch traced here: 67.6 us
  starting transfers between devices  26.1 us (38%)
  waiting for transfers between devices  23.6 us (35%)
  Pallas kernels  13.8 us (20%)
  local copies, waits for them, and re-layouts  2.61 us (4%)
  between operations  0.78 us (1%)
  other arithmetic  0.72 us (1%)
    ppermute x12, starting transfers between devices, member_swap(): return lax.ppermute(block, ('depth', 'gx'), pairs)  19.7 us
    ppermute x12, waiting for transfers between devices, member_swap(): return lax.ppermute(block, ('depth', 'gx'), pairs)  14.9 us
    pallas_call x8, Pallas kernels, call(): pl.pallas_call(kernel, out_shape=[jax.ShapeDtypeStruct(shape, F32) for sh...  13.8 us
    ppermute x2, waiting for transfers between devices, depth_pair_swap(): lax.ppermute(block, 'depth', [(z, z ^ 2) for z in range(lax.axis_size('de...  8.49 us
    ppermute x2, starting transfers between devices, depth_pair_swap(): lax.ppermute(block, 'depth', [(z, z ^ 2) for z in range(lax.axis_size('de...  2.87 us
    unnamed x8, local copies, waits for them, and re-layouts  2.61 us
    ppermute x2, starting transfers between devices, neighbour_swaps(): lax.ppermute(first, axis, pairs(0))  2.16 us
  transfers between devices with their start and end apart: 18, of which 9 were waited for; matrix products, arithmetic and copies ran while one was open for 0% of the time, Pallas kernels for 12%

profile of v1, /device:TPU:0, one launch (start us, length us, event | category | flops | bytes accessed | tf_op | source)
XLA Modules:
  0.0 67.6 jit_solution(14794083829750431701)
XLA Ops:
  0.6 0.0 copy-start.2
  0.7 0.1 pad_add_fusion.meta.refs_0_
  0.8 0.7 %copy-done.2 = f32[2,64,128]{2,1,0:T(8,128)S(1)} copy-done((f32[2,64,128]{2,1,0:T(8,128)S(1)}, f32[2,64,128]{2,1,0:T(8,128)}, u32[]{:S(2)}) %copy-start.2) | copy-done | bytes 65560
  1.5 0.0 copy-start.1
  1.5 1.0 %copy-done.1 = f32[2,2,4,64,128]{4,3,2,1,0:T(8,128)S(1)} copy-done((f32[2,2,4,64,128]{4,3,2,1,0:T(8,128)S(1)}, f32[2,2,4,64,128]{4,3,2,1,0:T(8,128)}, u32[]{:S(2)}) %copy-start.1) | copy-done | bytes 524312
  2.5 0.0 copy-start.3
  2.5 0.8 %copy-done.3 = f32[2,64,128]{2,1,0:T(8,128)S(1)} copy-done((f32[2,64,128]{2,1,0:T(8,128)S(1)}, f32[2,64,128]{2,1,0:T(8,128)}, u32[]{:S(2)}) %copy-start.3) | copy-done | bytes 65560
  3.4 0.6 shard_map.59
  4.0 3.0 %collective-permute-start = (f32[2,2,2,64,128]{4,3,2,1,0:T(8,128)S(1)}, f32[2,2,2,64,128]{4,3,2,1,0:T(8,128)S(1)}, u32[]{:S(2)}, u32[]{:S(2)}) collective-permute-start(f32[2,2,2,64,128]{4,3,2,1,0:T(8,128)S(1)} %get-tuple-element.31), channel_id=1, source_target_pairs={{0,4},{4,0},{8,12},{12,8},{16,20},{20,16},{24,28},{28,24},{1,5},{5... | collective-permute-start | bytes 786440 | tf_op jit(solution)/shard_map/ppermute | solution.py:37
  7.0 1.6 %collective-permute-start.1 = (f32[2,2,2,64,128]{4,3,2,1,0:T(8,128)S(1)}, f32[2,2,2,64,128]{4,3,2,1,0:T(8,128)S(1)}, u32[]{:S(2)}, u32[]{:S(2)}) collective-permute-start(f32[2,2,2,64,128]{4,3,2,1,0:T(8,128)S(1)} %get-tuple-element.32), channel_id=1, source_target_pairs={{0,8},{4,12},{8,0},{12,4},{16,24},{20,28},{24,16},{28,20},{1,9},{5... | collective-permute-start | bytes 786440 | tf_op jit(solution)/shard_map/ppermute | solution.py:37
  8.6 0.0 collective-permute-start.2
  8.6 4.7 %collective-permute-done.refs_1_ = f32[2,2,2,64,128]{4,3,2,1,0:T(8,128)S(1)} collective-permute-done((f32[2,2,2,64,128]{4,3,2,1,0:T(8,128)S(1)}, f32[2,2,2,64,128]{4,3,2,1,0:T(8,128)S(1)}, u32[]{:S(2)}, u32[]{:S(2)}) %collective-permute-start) | collective-permute-done | bytes 262176 | tf_op jit(solution)/shard_map/ppermute | solution.py:37
  13.3 2.9 %collective-permute-done.1.refs_2_ = f32[2,2,2,64,128]{4,3,2,1,0:T(8,128)S(1)} collective-permute-done((f32[2,2,2,64,128]{4,3,2,1,0:T(8,128)S(1)}, f32[2,2,2,64,128]{4,3,2,1,0:T(8,128)S(1)}, u32[]{:S(2)}, u32[]{:S(2)}) %collective-permute-start.1) | collective-permute-done | bytes 262176 | tf_op jit(solution)/shard_map/ppermute | solution.py:37
  16.2 3.9 %collective-permute-done.2.refs_3_ = f32[2,2,2,64,128]{4,3,2,1,0:T(8,128)S(1)} collective-permute-done((f32[2,2,2,64,128]{4,3,2,1,0:T(8,128)S(1)}, f32[2,2,2,64,128]{4,3,2,1,0:T(8,128)S(1)}, u32[]{:S(2)}, u32[]{:S(2)}) %collective-permute-start.2) | collective-permute-done | bytes 262176 | tf_op jit(solution)/shard_map/ppermute | solution.py:37
  20.2 0.0 copy-start
  20.2 1.1 %shard_map.60 = (f32[2,4,2,128,128]{4,3,2,1,0:T(8,128)S(1)}, f32[2,2,128,128]{3,2,1,0:T(8,128)S(1)}, f32[2,2,128,128]{3,2,1,0:T(8,128)S(1)}) custom-call(s32[3]{0:T(128)S(1)} %pad_add_fusion.meta.refs_0_, f32[2,2,2,64,128]{4,3,2,1,0:T(8,128)S(1)} %get-tuple-element.30.refs_0_, f32[2,2,2,64,128]{4,3,2,1,0:T(8,128)S(1)} %collective-permute-done.refs_1_, ...), custom_call_target="tpu_custom_call" | custom-call | tf_op jit(solution)/shard_map/pallas_call | solution.py:22
  21.3 0.1 collective-permute-start.3
  21.4 0.7 %collective-permute-start.4 = (f32[2,2,128,128]{3,2,1,0:T(8,128)S(1)}, f32[2,2,128,128]{3,2,1,0:T(8,128)S(1)}, u32[]{:S(2)}, u32[]{:S(2)}) collective-permute-start(f32[2,2,128,128]{3,2,1,0:T(8,128)S(1)} %get-tuple-element.36), channel_id=1, source_target_pairs={{1,2},{2,1},{5,6},{6,5},{9,10},{10,9},{13,14},{14,13},{17,18},{18,... | collective-permute-start | bytes 786440 | tf_op jit(solution)/shard_map/ppermute | solution.py:57
  22.1 0.0 copy-done
  22.1 0.6 shard_map.62
  22.6 1.7 %collective-permute-start.6 = (f32[1,2,2,64,128]{4,3,2,1,0:T(8,128)S(1)}, f32[1,2,2,64,128]{4,3,2,1,0:T(8,128)S(1)}, u32[]{:S(2)}, u32[]{:S(2)}) collective-permute-start(f32[1,2,2,64,128]{4,3,2,1,0:T(8,128)S(1)} %get-tuple-element.41), channel_id=1, source_target_pairs={{0,4},{4,0},{8,12},{12,8},{16,20},{20,16},{24,28},{28,24},{1,5},{5... | collective-permute-start | bytes 393224 | tf_op jit(solution)/shard_map/ppermute | solution.py:37
  24.4 1.6 %collective-permute-start.7 = (f32[1,2,2,64,128]{4,3,2,1,0:T(8,128)S(1)}, f32[1,2,2,64,128]{4,3,2,1,0:T(8,128)S(1)}, u32[]{:S(2)}, u32[]{:S(2)}) collective-permute-start(f32[1,2,2,64,128]{4,3,2,1,0:T(8,128)S(1)} %get-tuple-element.42), channel_id=1, source_target_pairs={{0,8},{4,12},{8,0},{12,4},{16,24},{20,28},{24,16},{28,20},{1,9},{5... | collective-permute-start | bytes 393224 | tf_op jit(solution)/shard_map/ppermute | solution.py:37
  26.0 0.2 collective-permute-start.8
  26.2 0.0 collective-permute-done.3.first
  26.2 0.0 collective-permute-done.4.second
  26.2 2.7 %shard_map.61 = (f32[4,2,128,256]{3,2,1,0:T(8,128)S(1)}, f32[4,2,128,256]{3,2,1,0:T(8,128)S(1)}, f32[3,128,128]{2,1,0:T(8,128)S(1)}) custom-call(s32[3]{0:T(128)S(1)} %pad_add_fusion.meta.refs_0_, f32[2,4,2,128,128]{4,3,2,1,0:T(8,128)S(1)} %get-tuple-element.34.merged, f32[2,2,128,128]{3,2,1,0:T(8,128)S(1)} %collective-permute-done.3.first, ...), custom_call_target="tpu_custom_call" | custom-call | tf_op jit(solution)/shard_map/pallas_call | solution.py:22
  29.0 2.8 %collective-permute-start.5 = (f32[3,128,128]{2,1,0:T(8,128)S(1)}, f32[3,128,128]{2,1,0:T(8,128)S(1)}, u32[]{:S(2)}, u32[]{:S(2)}) collective-permute-start(f32[3,128,128]{2,1,0:T(8,128)S(1)} %get-tuple-element.39), channel_id=1, source_target_pairs={{0,16},{8,24},{16,0},{24,8},{1,17},{9,25},{17,1},{25,9},{2,18},{10... | collective-permute-start | bytes 589832 | tf_op jit(solution)/shard_map/ppermute | solution.py:41
  31.8 0.0 collective-permute-done.6.refs_1_
  31.8 0.0 collective-permute-done.7.refs_2_
  31.8 1.0 %collective-permute-done.8.refs_3_ = f32[1,2,2,64,128]{4,3,2,1,0:T(8,128)S(1)} collective-permute-done((f32[1,2,2,64,128]{4,3,2,1,0:T(8,128)S(1)}, f32[1,2,2,64,128]{4,3,2,1,0:T(8,128)S(1)}, u32[]{:S(2)}, u32[]{:S(2)}) %collective-permute-start.8) | collective-permute-done | bytes 131104 | tf_op jit(solution)/shard_map/ppermute | solution.py:37
  32.8 0.9 %shard_map.63 = (f32[1,4,2,128,128]{4,3,2,1,0:T(8,128)S(1)}, f32[128,128]{1,0:T(8,128)S(1)}, f32[128,128]{1,0:T(8,128)S(1)}) custom-call(s32[3]{0:T(128)S(1)} %pad_add_fusion.meta.refs_0_, f32[1,2,2,64,128]{4,3,2,1,0:T(8,128)S(1)} %get-tuple-element.40.refs_0_, f32[1,2,2,64,128]{4,3,2,1,0:T(8,128)S(1)} %collective-permute-done.6.refs_1_, ...), custom_call_target="tpu_custom_call" | custom-call | tf_op jit(solution)/shard_map/pallas_call | solution.py:22
  33.7 2.1 %collective-permute-start.9 = (f32[128,128]{1,0:T(8,128)S(1)}, f32[128,128]{1,0:T(8,128)S(1)}, u32[]{:S(2)}, u32[]{:S(2)}) collective-permute-start(f32[128,128]{1,0:T(8,128)S(1)} %get-tuple-element.45), channel_id=1, source_target_pairs={{0,1},{1,0},{2,3},{3,2},{4,5},{5,4},{6,7},{7,6},{8,9},{9,8},{10,11... | collective-permute-start | bytes 196616 | tf_op jit(solution)/shard_map/ppermute | solution.py:56
  35.8 0.7 collective-permute-start.10
  36.4 0.2 collective-permute-done.9.refs_5_
  36.7 0.0 collective-permute-done.10.refs_6_
  36.7 3.4 %collective-permute-done.5.refs_3_ = f32[3,128,128]{2,1,0:T(8,128)S(1)} collective-permute-done((f32[3,128,128]{2,1,0:T(8,128)S(1)}, f32[3,128,128]{2,1,0:T(8,128)S(1)}, u32[]{:S(2)}, u32[]{:S(2)}) %collective-permute-start.5) | collective-permute-done | bytes 196640 | tf_op jit(solution)/shard_map/ppermute | solution.py:41
  40.1 4.2 %shard_map.64 = (f32[4,2,128,256]{3,2,1,0:T(8,128)S(1)}, f32[4,2,128,256]{3,2,1,0:T(8,128)S(1)}, f32[3,128,128]{2,1,0:T(8,128)S(1)}, f32[2,2,64,128]{3,2,1,0:T(8...) custom-call(s32[3]{0:T(128)S(1)} %pad_add_fusion.meta.refs_0_, ...), custom_call_target="tpu_custom_call" | custom-call | tf_op jit(solution)/shard_map/pallas_call | solution.py:22
  44.3 0.1 collective-permute-start.14
  44.4 2.3 %collective-permute-start.11 = (f32[2,2,64,128]{3,2,1,0:T(8,128)S(1)}, f32[2,2,64,128]{3,2,1,0:T(8,128)S(1)}, u32[]{:S(2)}, u32[]{:S(2)}) collective-permute-start(f32[2,2,64,128]{3,2,1,0:T(8,128)S(1)} %get-tuple-element.48), channel_id=1, source_target_pairs={{0,4},{4,0},{8,12},{12,8},{16,20},{20,16},{24,28},{28,24},{1,5},{5... | collective-permute-start | bytes 393224 | tf_op jit(solution)/shard_map/ppermute | solution.py:37
  46.7 4.6 %collective-permute-start.12 = (f32[2,2,64,128]{3,2,1,0:T(8,128)S(1)}, f32[2,2,64,128]{3,2,1,0:T(8,128)S(1)}, u32[]{:S(2)}, u32[]{:S(2)}) collective-permute-start(f32[2,2,64,128]{3,2,1,0:T(8,128)S(1)} %get-tuple-element.49), channel_id=1, source_target_pairs={{0,8},{4,12},{8,0},{12,4},{16,24},{20,28},{24,16},{28,20},{1,9},{5... | collective-permute-start | bytes 393224 | tf_op jit(solution)/shard_map/ppermute | solution.py:37
  51.2 0.4 collective-permute-start.13
  51.6 5.1 %collective-permute-done.14.refs_3_ = f32[3,128,128]{2,1,0:T(8,128)S(1)} collective-permute-done((f32[3,128,128]{2,1,0:T(8,128)S(1)}, f32[3,128,128]{2,1,0:T(8,128)S(1)}, u32[]{:S(2)}, u32[]{:S(2)}) %collective-permute-start.14) | collective-permute-done | bytes 196640 | tf_op jit(solution)/shard_map/ppermute | solution.py:41
  56.7 2.3 %shard_map.66 = (f32[2,64,128]{2,1,0:T(8,128)S(1)}, f32[2,64,128]{2,1,0:T(8,128)S(1)}, f32[2,64,128]{2,1,0:T(8,128)S(1)}, f32[2,64,128]{2,1,0:T(8,128)S(1)}) custom-call(s32[3]{0:T(128)S(1)} %pad_add_fusion.meta.refs_0_, f32[4,2,128,256]{3,2,1,0:T(8,128)S(1)} %get-tuple-element.51.refs_1_, f32[4,2,128,256]{3,2,1,0:T(8,128)S(1)} %get-tuple-element.38.refs_2_, ...), custom_call_target="tpu_custom_call" | custom-call | tf_op jit(solution)/shard_map/pallas_call | solution.py:22
  59.0 2.8 %collective-permute-start.15 = (f32[2,64,128]{2,1,0:T(8,128)S(1)}, f32[2,64,128]{2,1,0:T(8,128)S(1)}, u32[]{:S(2)}, u32[]{:S(2)}) collective-permute-start(f32[2,64,128]{2,1,0:T(8,128)S(1)} %get-tuple-element.55), channel_id=1, source_target_pairs={{0,4},{4,0},{8,12},{12,8},{16,20},{20,16},{24,28},{28,24},{1,5},{5... | collective-permute-start | bytes 196616 | tf_op jit(solution)/shard_map/ppermute | solution.py:37
  61.8 0.0 collective-permute-start.16
  61.8 0.0 collective-permute-done.11.refs_1_
  61.8 1.5 %collective-permute-start.17 = (f32[2,64,128]{2,1,0:T(8,128)S(1)}, f32[2,64,128]{2,1,0:T(8,128)S(1)}, u32[]{:S(2)}, u32[]{:S(2)}) collective-permute-start(f32[2,64,128]{2,1,0:T(8,128)S(1)} %get-tuple-element.57), channel_id=1, source_target_pairs={{0,12},{4,8},{8,4},{12,0},{16,28},{20,24},{24,20},{28,16},{1,13},{... | collective-permute-start | bytes 196616 | tf_op jit(solution)/shard_map/ppermute | solution.py:37
  63.3 0.0 collective-permute-done.12.refs_2_
  63.3 0.0 collective-permute-done.13.refs_3_
  63.4 1.4 %shard_map.65 = f32[2,2,4,64,128]{4,3,2,1,0:T(8,128)} custom-call(s32[3]{0:T(128)S(1)} %pad_add_fusion.meta.refs_0_, f32[2,2,64,128]{3,2,1,0:T(8,128)S(1)} %get-tuple-element.47.refs_0_, f32[2,2,64,128]{3,2,1,0:T(8,128)S(1)} %collective-permute-done.11.refs_1_, f32[2,2,64,128]{3,2,1,0:T(8,128)S(1)} %collective-permute-done.12.refs_2_, ...), custom_call_target="tpu_custom_call" | custom-call | tf_op jit(solution)/shard_map/pallas_call | solution.py:22
  64.7 0.0 collective-permute-done.15
  64.7 1.7 %collective-permute-done.16 = f32[2,64,128]{2,1,0:T(8,128)S(1)} collective-permute-done((f32[2,64,128]{2,1,0:T(8,128)S(1)}, f32[2,64,128]{2,1,0:T(8,128)S(1)}, u32[]{:S(2)}, u32[]{:S(2)}) %collective-permute-start.16) | collective-permute-done | bytes 65568 | tf_op jit(solution)/shard_map/ppermute | solution.py:37
  66.4 0.6 collective-permute-done.17
  67.0 0.6 add_add_fusion
Async XLA Ops:
  0.6 0.8 %copy-start.2 = (f32[2,64,128]{2,1,0:T(8,128)S(1)}, f32[2,64,128]{2,1,0:T(8,128)}, u32[]{:S(2)}) copy-start(f32[2,64,128]{2,1,0:T(8,128)} %wavenumber.1) | copy-start | bytes 196612
  1.5 1.0 %copy-start.1 = (f32[2,2,4,64,128]{4,3,2,1,0:T(8,128)S(1)}, f32[2,2,4,64,128]{4,3,2,1,0:T(8,128)}, u32[]{:S(2)}) copy-start(f32[2,2,4,64,128]{4,3,2,1,0:T(8,128)} %source.1) | copy-start | bytes 1572868
  2.5 0.8 %copy-start.3 = (f32[2,64,128]{2,1,0:T(8,128)S(1)}, f32[2,64,128]{2,1,0:T(8,128)}, u32[]{:S(2)}) copy-start(f32[2,64,128]{2,1,0:T(8,128)} %damping.1) | copy-start | bytes 196612
  4.0 9.3 %collective-permute-start = (f32[2,2,2,64,128]{4,3,2,1,0:T(8,128)S(1)}, f32[2,2,2,64,128]{4,3,2,1,0:T(8,128)S(1)}, u32[]{:S(2)}, u32[]{:S(2)}) collective-permute-start(f32[2,2,2,64,128]{4,3,2,1,0:T(8,128)S(1)} %get-tuple-element.31), channel_id=1, source_target_pairs={{0,4},{4,0},{8,12},{12,8},{16,20},{20,16},{24,28},{28,24},{1,5},{5... | collective-permute-start | bytes 786440 | tf_op jit(solution)/shard_map/ppermute | solution.py:37
  7.0 9.2 %collective-permute-start.1 = (f32[2,2,2,64,128]{4,3,2,1,0:T(8,128)S(1)}, f32[2,2,2,64,128]{4,3,2,1,0:T(8,128)S(1)}, u32[]{:S(2)}, u32[]{:S(2)}) collective-permute-start(f32[2,2,2,64,128]{4,3,2,1,0:T(8,128)S(1)} %get-tuple-element.32), channel_id=1, source_target_pairs={{0,8},{4,12},{8,0},{12,4},{16,24},{20,28},{24,16},{28,20},{1,9},{5... | collective-permute-start | bytes 786440 | tf_op jit(solution)/shard_map/ppermute | solution.py:37
  8.6 11.6 %collective-permute-start.2 = (f32[2,2,2,64,128]{4,3,2,1,0:T(8,128)S(1)}, f32[2,2,2,64,128]{4,3,2,1,0:T(8,128)S(1)}, u32[]{:S(2)}, u32[]{:S(2)}) collective-permute-start(f32[2,2,2,64,128]{4,3,2,1,0:T(8,128)S(1)} %get-tuple-element.33), channel_id=1, source_target_pairs={{0,12},{4,8},{8,4},{12,0},{16,28},{20,24},{24,20},{28,16},{1,13},{... | collective-permute-start | bytes 786440 | tf_op jit(solution)/shard_map/ppermute | solution.py:37
  20.2 1.9 %copy-start = (f32[2,2,4,64,128]{4,3,2,1,0:T(8,128)S(1)}, f32[2,2,4,64,128]{4,3,2,1,0:T(8,128)}, u32[]{:S(2)}) copy-start(f32[2,2,4,64,128]{4,3,2,1,0:T(8,128)} %observed.1) | copy-start | bytes 1572868
  21.3 4.9 %collective-permute-start.3 = (f32[2,2,128,128]{3,2,1,0:T(8,128)S(1)}, f32[2,2,128,128]{3,2,1,0:T(8,128)S(1)}, u32[]{:S(2)}, u32[]{:S(2)}) collective-permute-start(f32[2,2,128,128]{3,2,1,0:T(8,128)S(1)} %get-tuple-element.35), channel_id=1, source_target_pairs={{0,1},{1,0},{2,3},{3,2},{4,5},{5,4},{6,7},{7,6},{8,9},{9,8},{10,11... | collective-permute-start | bytes 786440 | tf_op jit(solution)/shard_map/ppermute | solution.py:56
  21.4 4.8 %collective-permute-start.4 = (f32[2,2,128,128]{3,2,1,0:T(8,128)S(1)}, f32[2,2,128,128]{3,2,1,0:T(8,128)S(1)}, u32[]{:S(2)}, u32[]{:S(2)}) collective-permute-start(f32[2,2,128,128]{3,2,1,0:T(8,128)S(1)} %get-tuple-element.36), channel_id=1, source_target_pairs={{1,2},{2,1},{5,6},{6,5},{9,10},{10,9},{13,14},{14,13},{17,18},{18,... | collective-permute-start | bytes 786440 | tf_op jit(solution)/shard_map/ppermute | solution.py:57
  22.6 9.1 %collective-permute-start.6 = (f32[1,2,2,64,128]{4,3,2,1,0:T(8,128)S(1)}, f32[1,2,2,64,128]{4,3,2,1,0:T(8,128)S(1)}, u32[]{:S(2)}, u32[]{:S(2)}) collective-permute-start(f32[1,2,2,64,128]{4,3,2,1,0:T(8,128)S(1)} %get-tuple-element.41), channel_id=1, source_target_pairs={{0,4},{4,0},{8,12},{12,8},{16,20},{20,16},{24,28},{28,24},{1,5},{5... | collective-permute-start | bytes 393224 | tf_op jit(solution)/shard_map/ppermute | solution.py:37
  24.4 7.4 %collective-permute-start.7 = (f32[1,2,2,64,128]{4,3,2,1,0:T(8,128)S(1)}, f32[1,2,2,64,128]{4,3,2,1,0:T(8,128)S(1)}, u32[]{:S(2)}, u32[]{:S(2)}) collective-permute-start(f32[1,2,2,64,128]{4,3,2,1,0:T(8,128)S(1)} %get-tuple-element.42), channel_id=1, source_target_pairs={{0,8},{4,12},{8,0},{12,4},{16,24},{20,28},{24,16},{28,20},{1,9},{5... | collective-permute-start | bytes 393224 | tf_op jit(solution)/shard_map/ppermute | solution.py:37
  26.0 6.8 %collective-permute-start.8 = (f32[1,2,2,64,128]{4,3,2,1,0:T(8,128)S(1)}, f32[1,2,2,64,128]{4,3,2,1,0:T(8,128)S(1)}, u32[]{:S(2)}, u32[]{:S(2)}) collective-permute-start(f32[1,2,2,64,128]{4,3,2,1,0:T(8,128)S(1)} %get-tuple-element.43), channel_id=1, source_target_pairs={{0,12},{4,8},{8,4},{12,0},{16,28},{20,24},{24,20},{28,16},{1,13},{... | collective-permute-start | bytes 393224 | tf_op jit(solution)/shard_map/ppermute | solution.py:37
  29.0 11.1 %collective-permute-start.5 = (f32[3,128,128]{2,1,0:T(8,128)S(1)}, f32[3,128,128]{2,1,0:T(8,128)S(1)}, u32[]{:S(2)}, u32[]{:S(2)}) collective-permute-start(f32[3,128,128]{2,1,0:T(8,128)S(1)} %get-tuple-element.39), channel_id=1, source_target_pairs={{0,16},{8,24},{16,0},{24,8},{1,17},{9,25},{17,1},{25,9},{2,18},{10... | collective-permute-start | bytes 589832 | tf_op jit(solution)/shard_map/ppermute | solution.py:41
  33.7 3.0 %collective-permute-start.9 = (f32[128,128]{1,0:T(8,128)S(1)}, f32[128,128]{1,0:T(8,128)S(1)}, u32[]{:S(2)}, u32[]{:S(2)}) collective-permute-start(f32[128,128]{1,0:T(8,128)S(1)} %get-tuple-element.45), channel_id=1, source_target_pairs={{0,1},{1,0},{2,3},{3,2},{4,5},{5,4},{6,7},{7,6},{8,9},{9,8},{10,11... | collective-permute-start | bytes 196616 | tf_op jit(solution)/shard_map/ppermute | solution.py:56
  35.8 0.9 %collective-permute-start.10 = (f32[128,128]{1,0:T(8,128)S(1)}, f32[128,128]{1,0:T(8,128)S(1)}, u32[]{:S(2)}, u32[]{:S(2)}) collective-permute-start(f32[128,128]{1,0:T(8,128)S(1)} %get-tuple-element.46), channel_id=1, source_target_pairs={{1,2},{2,1},{5,6},{6,5},{9,10},{10,9},{13,14},{14,13},{17,18},{18,... | collective-permute-start | bytes 196616 | tf_op jit(solution)/shard_map/ppermute | solution.py:57
  44.3 12.4 %collective-permute-start.14 = (f32[3,128,128]{2,1,0:T(8,128)S(1)}, f32[3,128,128]{2,1,0:T(8,128)S(1)}, u32[]{:S(2)}, u32[]{:S(2)}) collective-permute-start(f32[3,128,128]{2,1,0:T(8,128)S(1)} %get-tuple-element.52), channel_id=1, source_target_pairs={{0,16},{8,24},{16,0},{24,8},{1,17},{9,25},{17,1},{25,9},{2,18},{10... | collective-permute-start | bytes 589832 | tf_op jit(solution)/shard_map/ppermute | solution.py:41
  44.4 17.4 %collective-permute-start.11 = (f32[2,2,64,128]{3,2,1,0:T(8,128)S(1)}, f32[2,2,64,128]{3,2,1,0:T(8,128)S(1)}, u32[]{:S(2)}, u32[]{:S(2)}) collective-permute-start(f32[2,2,64,128]{3,2,1,0:T(8,128)S(1)} %get-tuple-element.48), channel_id=1, source_target_pairs={{0,4},{4,0},{8,12},{12,8},{16,20},{20,16},{24,28},{28,24},{1,5},{5... | collective-permute-start | bytes 393224 | tf_op jit(solution)/shard_map/ppermute | solution.py:37
  46.7 16.7 %collective-permute-start.12 = (f32[2,2,64,128]{3,2,1,0:T(8,128)S(1)}, f32[2,2,64,128]{3,2,1,0:T(8,128)S(1)}, u32[]{:S(2)}, u32[]{:S(2)}) collective-permute-start(f32[2,2,64,128]{3,2,1,0:T(8,128)S(1)} %get-tuple-element.49), channel_id=1, source_target_pairs={{0,8},{4,12},{8,0},{12,4},{16,24},{20,28},{24,16},{28,20},{1,9},{5... | collective-permute-start | bytes 393224 | tf_op jit(solution)/shard_map/ppermute | solution.py:37
  51.2 12.1 %collective-permute-start.13 = (f32[2,2,64,128]{3,2,1,0:T(8,128)S(1)}, f32[2,2,64,128]{3,2,1,0:T(8,128)S(1)}, u32[]{:S(2)}, u32[]{:S(2)}) collective-permute-start(f32[2,2,64,128]{3,2,1,0:T(8,128)S(1)} %get-tuple-element.50), channel_id=1, source_target_pairs={{0,12},{4,8},{8,4},{12,0},{16,28},{20,24},{24,20},{28,16},{1,13},{... | collective-permute-start | bytes 393224 | tf_op jit(solution)/shard_map/ppermute | solution.py:37
  59.0 5.7 %collective-permute-start.15 = (f32[2,64,128]{2,1,0:T(8,128)S(1)}, f32[2,64,128]{2,1,0:T(8,128)S(1)}, u32[]{:S(2)}, u32[]{:S(2)}) collective-permute-start(f32[2,64,128]{2,1,0:T(8,128)S(1)} %get-tuple-element.55), channel_id=1, source_target_pairs={{0,4},{4,0},{8,12},{12,8},{16,20},{20,16},{24,28},{28,24},{1,5},{5... | collective-permute-start | bytes 196616 | tf_op jit(solution)/shard_map/ppermute | solution.py:37
  61.8 4.6 %collective-permute-start.16 = (f32[2,64,128]{2,1,0:T(8,128)S(1)}, f32[2,64,128]{2,1,0:T(8,128)S(1)}, u32[]{:S(2)}, u32[]{:S(2)}) collective-permute-start(f32[2,64,128]{2,1,0:T(8,128)S(1)} %get-tuple-element.56), channel_id=1, source_target_pairs={{0,8},{4,12},{8,0},{12,4},{16,24},{20,28},{24,16},{28,20},{1,9},{5... | collective-permute-start | bytes 196616 | tf_op jit(solution)/shard_map/ppermute | solution.py:37
  61.8 5.2 %collective-permute-start.17 = (f32[2,64,128]{2,1,0:T(8,128)S(1)}, f32[2,64,128]{2,1,0:T(8,128)S(1)}, u32[]{:S(2)}, u32[]{:S(2)}) collective-permute-start(f32[2,64,128]{2,1,0:T(8,128)S(1)} %get-tuple-element.57), channel_id=1, source_target_pairs={{0,12},{4,8},{8,4},{12,0},{16,28},{20,24},{24,20},{28,16},{1,13},{... | collective-permute-start | bytes 196616 | tf_op jit(solution)/shard_map/ppermute | solution.py:37

commit v2 on v1

v2 whole, which is shorter than its diff:
```python
import jax
import jax.numpy as jnp
from jax import lax
from jax.experimental import pallas as pl
from jax.experimental.pallas import tpu as pltpu
from jax.sharding import PartitionSpec as P

MEMBERS = 4
WIDE = 32
NARROW = 16
LANES = 128

VMEM = pltpu.VMEM
F32 = jnp.float32


def lane_ids(shape):
    return lax.broadcasted_iota(jnp.int32, shape, len(shape) - 1)


def call(kernel, outs, meta, *operands, scratch=(), vmem=8):
    return pl.pallas_call(
        kernel,
        out_shape=[jax.ShapeDtypeStruct(shape, F32) for shape in outs],
        in_specs=[pl.BlockSpec(memory_space=pltpu.SMEM)]
        + [pl.BlockSpec(memory_space=VMEM)] * len(operands),
        out_specs=[pl.BlockSpec(memory_space=VMEM)] * len(outs),
        scratch_shapes=list(scratch),
        compiler_params=pltpu.CompilerParams(vmem_limit_bytes=vmem * 1024 * 1024),
    )(meta, *operands)


def member_swap(block, offset):
    nz, nx = lax.axis_size("depth"), lax.axis_size("gx")
    dz, dx = offset >> 1, offset & 1
    pairs = [(z * nx + x, (z ^ dz) * nx + (x ^ dx)) for z in range(nz) for x in range(nx)]
    return lax.ppermute(block, ("depth", "gx"), pairs)


def gathered(sends):
    return [sends[0]] + [member_swap(sends[k], k) for k in range(1, MEMBERS)]


def depth_pair_swap(block):
    return lax.ppermute(block, "depth", [(z, z ^ 2) for z in range(lax.axis_size("depth"))])


def neighbour_swaps(first, second, axis, stride):
    size = lax.axis_size(axis)
    count = size // stride

    def pairs(start):
        found = []
        for low in range(start, count - 1, 2):
            for part in range(stride):
                a, b = low * stride + part, (low + 1) * stride + part
                found += [(a, b), (b, a)]
        return found

    got_second = lax.ppermute(second, axis, pairs(1)) if count > 2 else jnp.zeros_like(second)
    got_first = lax.ppermute(first, axis, pairs(0)) if count > 1 else jnp.zeros_like(first)
    return got_first, got_second


def with_row_halo(block, width):
    groups = lax.axis_size("gx") // 2
    if groups == 1:
        return block
    even = (lax.axis_index("gx") // 2) % 2 == 0
    top, bottom = block[..., :width, :], block[..., -width:, :]
    one, two = neighbour_swaps(
        jnp.where(even, bottom, top), jnp.where(even, top, bottom), "gx", 2
    )
    above, below = jnp.where(even, two, one), jnp.where(even, one, two)
    return jnp.concatenate([above, block, below], axis=-2)


def merge_members(meta, pieces, out):
    me = meta[0]
    for k, piece in enumerate(pieces):
        fields, planes, _, rows, _ = piece.shape
        who = me ^ k
        at_plane = (who // 2) * planes
        at_row = pl.multiple_of((who % 2) * rows, rows)
        for f in range(fields):
            for p in range(planes):
                for c in range(2):
                    out[f, at_plane + p, c, pl.ds(at_row, rows), :] = piece[f, p, c]


def pack_edges(meta, pieces, width, first, out):
    me = meta[0]
    right = (meta[1] == 0) == first
    fields, planes, _, rows, count = pieces[0].shape
    lanes = lane_ids((rows, count))
    at = jnp.where(right, 0, width)
    second_plane = (lanes >= at) & (lanes < at + width)
    half = planes * width
    for k in range(2):
        who = me ^ k
        strip = pl.ds(pl.multiple_of((who % 2) * rows, rows), rows)
        at_lane = (who // 2) * half
        ours = (lanes >= at_lane) & (lanes < at_lane + half)
        turn = at_lane + jnp.where(right, width, 0)
        turns = turn, lax.rem(turn + half, count)
        for f in range(fields):
            for c in range(2):
                one, two = (
                    pltpu.roll(
                        jnp.where(
                            second_plane,
                            pltpu.roll(pieces[k + 2 * i][f, 1, c], width, 1),
                            pieces[k + 2 * i][f, 0, c],
                        ),
                        turns[i],
                        1,
                    )
                    for i in range(2)
                )
                out[f, c, strip, :] = jnp.where(ours, one, two)


def unpack_edges(meta, first, second, j, width):
    even = meta[1] == 0
    right, left = jnp.where(even, first, second), jnp.where(even, second, first)
    at = j * width
    return beside_tile(right, (LANES - at) % LANES, left, (LANES - width - at) % LANES, width)


def beside_tile(right, right_turn, left, left_turn, width):
    lanes = lane_ids(right.shape)
    right = pltpu.roll(right, right_turn, 1) if right_turn else right
    left = pltpu.roll(left, left_turn, 1) if left_turn else left
    return jnp.where(lanes < width, right, jnp.where(lanes >= LANES - width, left, 0.0))


def edge_lanes(shape, margin):
    lanes = lane_ids(shape)
    return (lanes < margin) | (lanes >= LANES - margin)


def slot_lanes(shape, block):
    return lax.rem(lane_ids(shape) + (LANES - 16 * block - LANES // 2 + 8), LANES // 2) < 16


def pack_carry(field, at, out, margin):
    rows = field.shape[2]
    real, imag = field[at, 0, :, LANES:], field[at, 1, :, LANES:]
    out[:rows] = field[at, 0, :, :LANES]
    out[rows : 2 * rows] = field[at, 1, :, :LANES]
    edges = jnp.where(edge_lanes(real.shape, WIDE), real, pltpu.roll(imag, LANES // 2, 1))
    if margin > 8:
        out[2 * rows :] = edges
        return
    part = rows // 4
    packed = edges[:part]
    for b in range(1, 4):
        turned = pltpu.roll(edges[b * part : (b + 1) * part], 16 * b, 1)
        packed = jnp.where(slot_lanes(packed.shape, b), turned, packed)
    out[2 * rows :] = packed


def unpack_carry(packed, use, out, margin):
    rows = out.shape[1]
    if margin > 8:
        edges = packed[2 * rows :]
    else:
        quarter = packed[2 * rows :]
        edges = jnp.concatenate(
            [pltpu.roll(quarter, LANES - 16 * b, 1) if b else quarter for b in range(4)], axis=0
        )
    keep = use & edge_lanes(edges.shape, WIDE if margin > 8 else 8)
    for c in range(2):
        out[c, :, :LANES] = jnp.where(use, packed[c * rows : (c + 1) * rows], 0.0)
        out[c, :, LANES:] = jnp.where(keep, pltpu.roll(edges, LANES // 2, 1) if c else edges, 0.0)


def times(a, b, q_real, q_imag, sign):
    if sign > 0:
        return a * q_real - b * q_imag, a * q_imag + b * q_real
    return a * q_real + b * q_imag, b * q_real - a * q_imag


def sweep(drive, inverse, out, carry, work, planes, rows, reverse):
    rhs, ping, pong = work
    sign = -1 if reverse else 1
    zeros = jnp.zeros((8, 2 * LANES), F32)
    for buffer in (ping, pong):
        for c in range(2):
            buffer[c, :8, :] = zeros
            buffer[c, rows + 8 : rows + 16, :] = zeros

    def beside(buffer, c, r):
        here = buffer[c, r + 8 : r + 16, :]
        return (
            buffer[c, r + 7 : r + 15, :]
            + buffer[c, r + 9 : r + 17, :]
            + (pltpu.roll(here, 1, 1) + pltpu.roll(here, 2 * LANES - 1, 1))
        )

    def plane(step, _):
        z = planes - 1 - step if reverse else step
        for r in range(0, rows, 8):
            strip = slice(r, r + 8)
            a = drive[z, 0, strip, :] + 2.5 * carry[0, strip, :]
            b = drive[z, 1, strip, :] + 2.5 * carry[1, strip, :]
            rhs[0, strip, :] = a
            rhs[1, strip, :] = b
            a, b = times(a, b, inverse[z, 0, strip, :], inverse[z, 1, strip, :], sign)
            ping[0, r + 8 : r + 16, :] = a
            ping[1, r + 8 : r + 16, :] = b
        for r in range(0, rows, 8):
            strip = slice(r, r + 8)
            a = rhs[0, strip, :] + beside(ping, 0, r)
            b = rhs[1, strip, :] + beside(ping, 1, r)
            a, b = times(a, b, inverse[z, 0, strip, :], inverse[z, 1, strip, :], sign)
            pong[0, r + 8 : r + 16, :] = a
            pong[1, r + 8 : r + 16, :] = b
        for r in range(0, rows, 8):
            strip = slice(r, r + 8)
            a = rhs[0, strip, :] + beside(pong, 0, r)
            b = rhs[1, strip, :] + beside(pong, 1, r)
            a, b = times(a, b, inverse[z, 0, strip, :], inverse[z, 1, strip, :], sign)
            out[z, 0, strip, :] = a
            out[z, 1, strip, :] = b
            carry[0, strip, :] = a
            carry[1, strip, :] = b
        return 0

    lax.fori_loop(0, planes, plane, 0)


def sweep_scratch(rows):
    wide = 2 * LANES
    return [
        VMEM((2, rows, wide), F32),
        VMEM((2, rows, wide), F32),
        VMEM((2, rows + 16, wide), F32),
        VMEM((2, rows + 16, wide), F32),
    ]


def inverses(wavenumber, damping):
    real_diag = 6.0 - wavenumber
    denom = real_diag * real_diag + damping * damping
    return jnp.stack([real_diag / denom, -(damping / denom)], axis=1)


def second_edges_kernel(meta, *refs):
    pack_edges(meta, refs[:MEMBERS], WIDE, False, refs[MEMBERS])


def merge_kernel(meta, *refs):
    pieces, (_, merged, out) = refs[:MEMBERS], refs[MEMBERS:]
    pack_edges(meta, pieces, WIDE, True, out)
    merge_members(meta, pieces, merged)


def observed_edges_kernel(meta, observed, first, second):
    even = meta[1] == 0
    planes, _, shots, rows, count = observed.shape
    lanes = lane_ids((rows, count))
    per_tile = count // NARROW
    sides = {}
    for s in range(shots):
        for p in range(planes):
            for c in range(2):
                tile, j = divmod((s * planes + p) * 2 + c, per_tile)
                at = j * NARROW
                block = observed[p, c, s]
                for side, turn in (("left", at), ("right", (at + NARROW) % count)):
                    got = pltpu.roll(block, turn, 1) if turn else block
                    if j:
                        got = jnp.where(lanes >= at, got, sides[side])
                    sides[side] = got
                if j == per_tile - 1:
                    first[tile] = jnp.where(even, sides["right"], sides["left"])
                    second[tile] = jnp.where(even, sides["left"], sides["right"])


def observed_sends_kernel(meta, observed, first, second, *sends):
    even = meta[1] == 0
    planes, _, _, rows, count = observed.shape
    lanes = lane_ids((rows, count))
    for k, send in enumerate(sends):
        shot = meta[0] ^ k
        for p in range(planes):
            for c in range(2):
                send[2 * p + c] = observed[p, c, shot]
        one, two = first[shot // 2], second[shot // 2]
        right, left = jnp.where(even, one, two), jnp.where(even, two, one)
        odd = lax.rem(shot, 2)
        right = pltpu.roll(right, odd * (count // 2), 1)
        left = pltpu.roll(left, (1 - odd) * (count // 2), 1)
        send[2 * planes] = jnp.where(lanes < count // 2, right, left)


def merge_observed_kernel(meta, *refs):
    pieces, out = refs[:MEMBERS], refs[MEMBERS]
    planes = out.shape[0] // 2
    _, rows, count = pieces[0].shape
    for k, piece in enumerate(pieces):
        who = meta[0] ^ k
        at_plane = (who // 2) * planes
        strip = pl.ds(pl.multiple_of((who % 2) * rows, rows), rows)
        edges = piece[2 * planes]
        for p in range(planes):
            for c in range(2):
                at = (2 * p + c) * NARROW
                out[at_plane + p, c, strip, :LANES] = piece[2 * p + c]
                out[at_plane + p, c, strip, LANES:] = beside_tile(
                    edges,
                    (count - at) % count,
                    edges,
                    (count // 2 - NARROW - at) % count,
                    NARROW,
                )


def widen(merged, edges, outs):
    for f, out in enumerate(outs):
        for p in range(merged.shape[1]):
            for c in range(2):
                out[p, c, :, :LANES] = merged[f, p, c]
                out[p, c, :, LANES:] = edges(f, p, c)


def cut_pieces(meta, field, height, pieces):
    planes, rows = field.shape[0], field.shape[2]
    margin = (rows - 2 * height) // 2
    for k, piece in enumerate(pieces):
        who = meta[0] ^ k
        at_plane = (who // 2) * (planes // 2)
        at_row = pl.multiple_of((who % 2) * height + margin, 8)
        for p in range(planes // 2):
            for c in range(2):
                piece[p, c] = field[at_plane + p, c, pl.ds(at_row, height), :LANES]


def forward_kernel(meta, merged, second, first, drive, inverse, field, send, *rest):
    carry, *work = rest
    planes, rows = merged.shape[1], merged.shape[3]
    widen(
        merged,
        lambda f, p, c: unpack_edges(meta, first[f, c], second[f, c], p, WIDE),
        (drive, inverse),
    )

    @pl.when(meta[2] == 0)
    def _():
        carry[...] = jnp.zeros_like(carry)
        sweep(drive, inverse, field, carry, work, planes, rows, False)
        pack_carry(field, planes - 1, send, WIDE)


def turn_kernel(
    height,
    meta,
    drive,
    inverse,
    got,
    observed,
    upper_field,
    field,
    residual,
    adjoint,
    send,
    *rest,
):
    pieces, (carry, *work) = rest[:MEMBERS], rest[MEMBERS:]
    planes, rows = drive.shape[0], drive.shape[2]
    lower = meta[2] == 1

    @pl.when(jnp.logical_not(lower))
    def _():
        field[...] = upper_field[...]

    @pl.when(lower)
    def _():
        unpack_carry(got, lower, carry, WIDE)
        sweep(drive, inverse, field, carry, work, planes, rows, False)

    residual[...] = field[...] - observed[...]

    @pl.when(lower)
    def _():
        carry[...] = jnp.zeros_like(carry)
        sweep(residual, inverse, adjoint, carry, work, planes, rows, True)
        pack_carry(adjoint, 0, send, 8)

    cut_pieces(meta, field, height, pieces)


def adjoint_kernel(height, meta, residual, inverse, got, field, lower_adjoint, *rest):
    pieces, (adjoint, carry, *work) = rest[:MEMBERS], rest[MEMBERS:]
    planes, rows = residual.shape[0], residual.shape[2]
    margin = (rows - 2 * height) // 2
    upper = meta[2] == 0

    def products(adjoint):
        for k, piece in enumerate(pieces):
            who = meta[0] ^ k
            at_plane = (who // 2) * (planes // 2)
            at_row = pl.multiple_of((who % 2) * height + margin, 8)
            for p in range(planes // 2):
                total = 0.0
                for c in range(2):
                    total += (
                        field[at_plane + p, c, pl.ds(at_row, height), :LANES]
                        * adjoint[at_plane + p, c, pl.ds(at_row, height), :LANES]
                    )
                piece[p] = total * (1.0 / MEMBERS)

    @pl.when(upper)
    def _():
        unpack_carry(got, upper, carry, 8)
        sweep(residual, inverse, adjoint, carry, work, planes, rows, True)
        products(adjoint)

    @pl.when(jnp.logical_not(upper))
    def _():
        products(lower_adjoint)


def field_kernel(meta, *refs):
    out = refs[MEMBERS]
    for k, piece in enumerate(refs[:MEMBERS]):
        out[:, :, meta[0] ^ k] = piece[...]


def body(source, observed, wavenumber, damping):
    own_planes, _, shots, height, width = source.shape
    zi, xi, yi = (lax.axis_index(a) for a in ("depth", "gx", "gy"))
    meta = jnp.stack([2 * (zi % 2) + xi % 2, yi % 2, zi // 2]).astype(jnp.int32)
    planes, high = 2 * own_planes, 2 * height
    one_group = lax.axis_size("gx") == 2
    rows = high if one_group else high + 2 * WIDE
    tile = (own_planes, 2, height, width)

    inverse = inverses(wavenumber, damping)
    sends = [
        jnp.stack([lax.dynamic_index_in_dim(source, meta[0] ^ k, 2, keepdims=False), inverse])
        for k in range(MEMBERS)
    ]
    observed, *sends = lax.optimization_barrier([observed, *sends])
    pieces = gathered(sends)
    seen_edges = call(observed_edges_kernel, [(2, height, width)] * 2, meta, observed)
    seen_edges = neighbour_swaps(*seen_edges, "gy", 1)
    *pieces, first, second = lax.optimization_barrier([*pieces, *seen_edges])
    seen_edges = first, second
    edge_shape = (2, 2, high, width)
    (second,) = call(second_edges_kernel, [edge_shape], meta, *pieces)
    merged, first = call(
        merge_kernel, [(2, planes, 2, high, width), edge_shape], meta, *pieces, second
    )
    if not one_group:
        merged, first, second = (with_row_halo(a, WIDE) for a in (merged, first, second))
    first, second = neighbour_swaps(first, second, "gy", 1)
    seen = gathered(
        call(
            observed_sends_kernel,
            [(2 * own_planes + 1, height, width)] * MEMBERS,
            meta,
            observed,
            *seen_edges,
        )
    )

    whole = (planes, 2, rows, 2 * width)
    scratch = sweep_scratch(rows)
    drive, inverse, field, send = call(
        forward_kernel,
        [whole, whole, whole, (3 * rows, width)],
        meta,
        merged,
        second,
        first,
        scratch=scratch,
    )
    got = depth_pair_swap(send)
    (seen,) = call(merge_observed_kernel, [(planes, 2, high, 2 * width)], meta, *seen)
    seen = seen if one_group else with_row_halo(seen, WIDE)
    field, residual, adjoint, send, *pieces = call(
        lambda *refs: turn_kernel(height, *refs),
        [whole, whole, whole, (2 * rows + rows // 4, width)] + [tile] * MEMBERS,
        meta,
        drive,
        inverse,
        got,
        seen,
        field,
        scratch=scratch,
    )
    got = depth_pair_swap(send)
    pieces = gathered(pieces)
    sums = call(
        lambda *refs: adjoint_kernel(height, *refs),
        [(own_planes, height, width)] * MEMBERS,
        meta,
        residual,
        inverse,
        got,
        field,
        adjoint,
        scratch=[VMEM(whole, F32), *scratch],
    )
    sums = gathered(sums)
    gradient = (sums[0] + sums[1]) + (sums[2] + sums[3])
    (forward_field,) = call(field_kernel, [source.shape], meta, *pieces)
    return forward_field, gradient


def solution(mesh):
    lateral = P("depth", None, None, "gx", "gy")
    return jax.shard_map(
        body,
        mesh=mesh,
        in_specs=(lateral, lateral, P("depth", "gx", "gy"), P("depth", "gx", "gy")),
        out_specs=(lateral, P("depth", "gx", "gy")),
        check_vma=False,
    )
```

time: 67.9 us -> 64.4 us (0.948)
  the two profiles are of different devices: /device:TPU:0 before, /device:TPU:2 now
where the time goes in v2:
time: 64.4 us; the launch traced here: 64.3 us
  starting transfers between devices  25.6 us (40%)
  waiting for transfers between devices  22.9 us (36%)
  Pallas kernels  12.4 us (19%)
  other arithmetic  1.71 us (3%)
  between operations  0.86 us (1%)
  local copies, waits for them, and re-layouts  0.84 us (1%)
    ppermute x12, starting transfers between devices, member_swap(): return lax.ppermute(block, ('depth', 'gx'), pairs)  14.9 us
    ppermute x12, waiting for transfers between devices, member_swap(): return lax.ppermute(block, ('depth', 'gx'), pairs)  14.1 us
    pallas_call x9, Pallas kernels, call(): pl.pallas_call(kernel, out_shape=[jax.ShapeDtypeStruct(shape, F32) for sh...  12.4 us
    ppermute x2, waiting for transfers between devices, neighbour_swaps(): lax.ppermute(second, axis, pairs(1))  8.71 us
    ppermute x2, starting transfers between devices, depth_pair_swap(): lax.ppermute(block, 'depth', [(z, z ^ 2) for z in range(lax.axis_size('de...  6.03 us
    ppermute x2, starting transfers between devices, neighbour_swaps(): lax.ppermute(second, axis, pairs(1))  4.53 us
  transfers between devices with their start and end apart: 18, of which 9 were waited for; matrix products, arithmetic and copies ran while one was open for 0% of the time, Pallas kernels for 9%

profile of v2, /device:TPU:2, one launch (start us, length us, event | category | flops | bytes accessed | tf_op | source)
XLA Modules:
  0.0 64.3 jit_solution(12210047669496120305)
XLA Ops:
  0.6 0.0 copy-start.2
  0.6 0.0 copy-start.1
  0.7 0.8 %copy-done.2 = f32[2,64,128]{2,1,0:T(8,128)S(1)} copy-done((f32[2,64,128]{2,1,0:T(8,128)S(1)}, f32[2,64,128]{2,1,0:T(8,128)}, u32[]{:S(2)}) %copy-start.2) | copy-done | bytes 65560
  1.5 0.9 %divide_bitcast_fusion = (f32[2,1,64,128]{3,2,1,0:T(8,128)S(1)}, f32[2,1,64,128]{3,2,1,0:T(8,128)S(1)}) fusion(f32[2,64,128]{2,1,0:T(8,128)S(1)} %copy-done.2, f32[2,64,128]{2,1,0:T(8,128)} %param.6), kind=kLoop, calls=%fused_computation.11 | loop fusion | flops 114688 | bytes 262144 | tf_op jit(solution)/shard_map/stack | solution.py:246
  2.4 0.0 copy-done.1
  2.4 0.0 copy-start
  2.4 0.1 pad_maximum_fusion
  2.6 1.6 %collective-permute-start = (f32[2,2,2,64,128]{4,3,2,1,0:T(8,128)S(1)}, f32[2,2,2,64,128]{4,3,2,1,0:T(8,128)S(1)}, u32[]{:S(2)}, u32[]{:S(2)}) collective-permute-start(f32[2,2,2,64,128]{4,3,2,1,0:T(8,128)S(1)} %get-tuple-element.38), channel_id=1, source_target_pairs={{0,4},{4,0},{8,12},{12,8},{16,20},{20,16},{24,28},{28,24},{1,5},{5... | collective-permute-start | bytes 786440 | tf_op jit(solution)/shard_map/ppermute | solution.py:37
  4.1 1.6 %collective-permute-start.1 = (f32[2,2,2,64,128]{4,3,2,1,0:T(8,128)S(1)}, f32[2,2,2,64,128]{4,3,2,1,0:T(8,128)S(1)}, u32[]{:S(2)}, u32[]{:S(2)}) collective-permute-start(f32[2,2,2,64,128]{4,3,2,1,0:T(8,128)S(1)} %get-tuple-element.39), channel_id=1, source_target_pairs={{0,8},{4,12},{8,0},{12,4},{16,24},{20,28},{24,16},{28,20},{1,9},{5... | collective-permute-start | bytes 786440 | tf_op jit(solution)/shard_map/ppermute | solution.py:37
  5.7 0.4 collective-permute-start.2
  6.1 0.1 pad_add_fusion.meta.refs_0_
  6.2 0.0 copy-done
  6.2 0.8 %shard_map.59 = (f32[2,64,128]{2,1,0:T(8,128)S(1)}, f32[2,64,128]{2,1,0:T(8,128)S(1)}) custom-call(s32[3]{0:T(128)S(1)} %pad_add_fusion.meta.refs_0_, f32[2,2,4,64,128]{4,3,2,1,0:T(8,128)S(1)} %copy-done), custom_call_target="tpu_custom_call" | custom-call | tf_op jit(solution)/shard_map/pallas_call | solution.py:22
  7.0 0.1 collective-permute-start.3
  7.1 2.1 %collective-permute-start.4 = (f32[2,64,128]{2,1,0:T(8,128)S(1)}, f32[2,64,128]{2,1,0:T(8,128)S(1)}, u32[]{:S(2)}, u32[]{:S(2)}) collective-permute-start(f32[2,64,128]{2,1,0:T(8,128)S(1)} %get-tuple-element.43), channel_id=1, source_target_pairs={{1,2},{2,1},{5,6},{6,5},{9,10},{10,9},{13,14},{14,13},{17,18},{18,... | collective-permute-start | bytes 196616 | tf_op jit(solution)/shard_map/ppermute | solution.py:60
  9.3 0.0 collective-permute-done.3.first
  9.3 3.4 %collective-permute-done.4.second = f32[2,64,128]{2,1,0:T(8,128)S(1)} collective-permute-done((f32[2,64,128]{2,1,0:T(8,128)S(1)}, f32[2,64,128]{2,1,0:T(8,128)S(1)}, u32[]{:S(2)}, u32[]{:S(2)}) %collective-permute-start.4) | collective-permute-done | bytes 65568 | tf_op jit(solution)/shard_map/ppermute | solution.py:60
  12.7 0.0 collective-permute-done.refs_1_
  12.7 0.7 %collective-permute-done.1.refs_2_ = f32[2,2,2,64,128]{4,3,2,1,0:T(8,128)S(1)} collective-permute-done((f32[2,2,2,64,128]{4,3,2,1,0:T(8,128)S(1)}, f32[2,2,2,64,128]{4,3,2,1,0:T(8,128)S(1)}, u32[]{:S(2)}, u32[]{:S(2)}) %collective-permute-start.1) | collective-permute-done | bytes 262176 | tf_op jit(solution)/shard_map/ppermute | solution.py:37
  13.4 4.1 %collective-permute-done.2.refs_3_ = f32[2,2,2,64,128]{4,3,2,1,0:T(8,128)S(1)} collective-permute-done((f32[2,2,2,64,128]{4,3,2,1,0:T(8,128)S(1)}, f32[2,2,2,64,128]{4,3,2,1,0:T(8,128)S(1)}, u32[]{:S(2)}, u32[]{:S(2)}) %collective-permute-start.2) | collective-permute-done | bytes 262176 | tf_op jit(solution)/shard_map/ppermute | solution.py:37
  17.5 1.4 %shard_map.60.refs_4_ = f32[2,2,128,128]{3,2,1,0:T(8,128)S(1)} custom-call(s32[3]{0:T(128)S(1)} %pad_add_fusion.meta.refs_0_, f32[2,2,2,64,128]{4,3,2,1,0:T(8,128)S(1)} %get-tuple-element.44.refs_0_, f32[2,2,2,64,128]{4,3,2,1,0:T(8,128)S(1)} %collective-permute-done.refs_1_, f32[2,2,2,64,128]{4,3,2,1,0:T(8,128)S(1)} %collective-permute-done.1.refs_2_, ...), custom_call_target="tpu_custom_call" | custom-call | tf_op jit(solution)/shard_map/pallas_call | solution.py:22
  18.9 1.4 %shard_map.61 = (f32[2,4,2,128,128]{4,3,2,1,0:T(8,128)S(1)}, f32[2,2,128,128]{3,2,1,0:T(8,128)S(1)}) custom-call(s32[3]{0:T(128)S(1)} %pad_add_fusion.meta.refs_0_, f32[2,2,2,64,128]{4,3,2,1,0:T(8,128)S(1)} %get-tuple-element.44.refs_0_, f32[2,2,2,64,128]{4,3,2,1,0:T(8,128)S(1)} %collective-permute-done.refs_1_, ...), custom_call_target="tpu_custom_call" | custom-call | tf_op jit(solution)/shard_map/pallas_call | solution.py:22
  20.3 0.1 collective-permute-start.6
  20.4 2.4 %collective-permute-start.5 = (f32[2,2,128,128]{3,2,1,0:T(8,128)S(1)}, f32[2,2,128,128]{3,2,1,0:T(8,128)S(1)}, u32[]{:S(2)}, u32[]{:S(2)}) collective-permute-start(f32[2,2,128,128]{3,2,1,0:T(8,128)S(1)} %shard_map.60.refs_4_), channel_id=1, source_target_pairs={{1,2},{2,1},{5,6},{6,5},{9,10},{10,9},{13,14},{14,13},{17,18},{18,... | collective-permute-start | bytes 786440 | tf_op jit(solution)/shard_map/ppermute | solution.py:60
  22.8 0.0 collective-permute-done.6.first
  22.8 5.3 %collective-permute-done.5.second = f32[2,2,128,128]{3,2,1,0:T(8,128)S(1)} collective-permute-done((f32[2,2,128,128]{3,2,1,0:T(8,128)S(1)}, f32[2,2,128,128]{3,2,1,0:T(8,128)S(1)}, u32[]{:S(2)}, u32[]{:S(2)}) %collective-permute-start.5) | collective-permute-done | bytes 262176 | tf_op jit(solution)/shard_map/ppermute | solution.py:60
  28.1 2.7 %shard_map.62 = (f32[4,2,128,256]{3,2,1,0:T(8,128)S(1)}, f32[4,2,128,256]{3,2,1,0:T(8,128)S(1)}, f32[4,2,128,256]{3,2,1,0:T(8,128)S(1)}, f32[384,128]{1,0:T(8,128)S(1)}) custom-call(s32[3]{0:T(128)S(1)} %pad_add_fusion.meta.refs_0_, f32[2,4,2,128,128]{4,3,2,1,0:T(8,128)S(1)} %get-tuple-element.48.merged, ...), custom_call_target="tpu_custom_call" | custom-call | tf_op jit(solution)/shard_map/pallas_call | solution.py:22
  30.8 1.0 %collective-permute-start.7 = (f32[384,128]{1,0:T(8,128)S(1)}, f32[384,128]{1,0:T(8,128)S(1)}, u32[]{:S(2)}, u32[]{:S(2)}) collective-permute-start(f32[384,128]{1,0:T(8,128)S(1)} %get-tuple-element.52), channel_id=1, source_target_pairs={{0,16},{8,24},{16,0},{24,8},{1,17},{9,25},{17,1},{25,9},{2,18},{10... | collective-permute-start | bytes 589832 | tf_op jit(solution)/shard_map/ppermute | solution.py:45
  31.8 0.7 %shard_map.63 = (f32[5,64,128]{2,1,0:T(8,128)S(1)}, f32[5,64,128]{2,1,0:T(8,128)S(1)}, f32[5,64,128]{2,1,0:T(8,128)S(1)}, f32[5,64,128]{2,1,0:T(8,128)S(1)}) custom-call(s32[3]{0:T(128)S(1)} %pad_add_fusion.meta.refs_0_, f32[2,2,4,64,128]{4,3,2,1,0:T(8,128)S(1)} %copy-done, f32[2,64,128]{2,1,0:T(8,128)S(1)} %collective-permute-done.3.first, ...), custom_call_target="tpu_custom_call" | custom-call | tf_op jit(solution)/shard_map/pallas_call | solution.py:22
  32.5 1.6 %collective-permute-start.8 = (f32[5,64,128]{2,1,0:T(8,128)S(1)}, f32[5,64,128]{2,1,0:T(8,128)S(1)}, u32[]{:S(2)}, u32[]{:S(2)}) collective-permute-start(f32[5,64,128]{2,1,0:T(8,128)S(1)} %get-tuple-element.56), channel_id=1, source_target_pairs={{0,4},{4,0},{8,12},{12,8},{16,20},{20,16},{24,28},{28,24},{1,5},{5... | collective-permute-start | bytes 491528 | tf_op jit(solution)/shard_map/ppermute | solution.py:37
  34.1 1.6 %collective-permute-start.9 = (f32[5,64,128]{2,1,0:T(8,128)S(1)}, f32[5,64,128]{2,1,0:T(8,128)S(1)}, u32[]{:S(2)}, u32[]{:S(2)}) collective-permute-start(f32[5,64,128]{2,1,0:T(8,128)S(1)} %get-tuple-element.57), channel_id=1, source_target_pairs={{0,8},{4,12},{8,0},{12,4},{16,24},{20,28},{24,16},{28,20},{1,9},{5... | collective-permute-start | bytes 491528 | tf_op jit(solution)/shard_map/ppermute | solution.py:37
  35.6 0.4 collective-permute-start.10
  36.0 1.8 %collective-permute-done.8.refs_1_ = f32[5,64,128]{2,1,0:T(8,128)S(1)} collective-permute-done((f32[5,64,128]{2,1,0:T(8,128)S(1)}, f32[5,64,128]{2,1,0:T(8,128)S(1)}, u32[]{:S(2)}, u32[]{:S(2)}) %collective-permute-start.8) | collective-permute-done | bytes 163872 | tf_op jit(solution)/shard_map/ppermute | solution.py:37
  37.9 2.5 %collective-permute-done.9.refs_2_ = f32[5,64,128]{2,1,0:T(8,128)S(1)} collective-permute-done((f32[5,64,128]{2,1,0:T(8,128)S(1)}, f32[5,64,128]{2,1,0:T(8,128)S(1)}, u32[]{:S(2)}, u32[]{:S(2)}) %collective-permute-start.9) | collective-permute-done | bytes 163872 | tf_op jit(solution)/shard_map/ppermute | solution.py:37
  40.4 1.9 %collective-permute-done.10.refs_3_ = f32[5,64,128]{2,1,0:T(8,128)S(1)} collective-permute-done((f32[5,64,128]{2,1,0:T(8,128)S(1)}, f32[5,64,128]{2,1,0:T(8,128)S(1)}, u32[]{:S(2)}, u32[]{:S(2)}) %collective-permute-start.10) | collective-permute-done | bytes 163872 | tf_op jit(solution)/shard_map/ppermute | solution.py:37
  42.3 0.8 %shard_map.64.refs_4_ = f32[4,2,128,256]{3,2,1,0:T(8,128)S(1)} custom-call(s32[3]{0:T(128)S(1)} %pad_add_fusion.meta.refs_0_, f32[5,64,128]{2,1,0:T(8,128)S(1)} %get-tuple-element.55.refs_0_, f32[5,64,128]{2,1,0:T(8,128)S(1)} %collective-permute-done.8.refs_1_, f32[5,64,128]{2,1,0:T(8,128)S(1)} %collective-permute-done.9.refs_2_, ...), custom_call_target="tpu_custom_call" | custom-call | tf_op jit(solution)/shard_map/pallas_call | solution.py:22
  43.1 0.0 collective-permute-done.7.refs_3_
  43.1 0.8 %shard_map.65 = (f32[4,2,128,256]{3,2,1,0:T(8,128)S(1)}, f32[4,2,128,256]{3,2,1,0:T(8,128)S(1)}, f32[4,2,128,256]{3,2,1,0:T(8,128)S(1)}, f32[288,128]{1,0:T(8,12...) custom-call(s32[3]{0:T(128)S(1)} %pad_add_fusion.meta.refs_0_, ...), custom_call_target="tpu_custom_call" | custom-call | tf_op jit(solution)/shard_map/pallas_call | solution.py:22
  43.9 5.1 %collective-permute-start.14 = (f32[288,128]{1,0:T(8,128)S(1)}, f32[288,128]{1,0:T(8,128)S(1)}, u32[]{:S(2)}, u32[]{:S(2)}) collective-permute-start(f32[288,128]{1,0:T(8,128)S(1)} %get-tuple-element.65), channel_id=1, source_target_pairs={{0,16},{8,24},{16,0},{24,8},{1,17},{9,25},{17,1},{25,9},{2,18},{10... | collective-permute-start | bytes 442376 | tf_op jit(solution)/shard_map/ppermute | solution.py:45
  48.9 0.7 %collective-permute-start.11 = (f32[2,2,64,128]{3,2,1,0:T(8,128)S(1)}, f32[2,2,64,128]{3,2,1,0:T(8,128)S(1)}, u32[]{:S(2)}, u32[]{:S(2)}) collective-permute-start(f32[2,2,64,128]{3,2,1,0:T(8,128)S(1)} %get-tuple-element.61), channel_id=1, source_target_pairs={{0,4},{4,0},{8,12},{12,8},{16,20},{20,16},{24,28},{28,24},{1,5},{5... | collective-permute-start | bytes 393224 | tf_op jit(solution)/shard_map/ppermute | solution.py:37
  49.7 2.3 %collective-permute-start.12 = (f32[2,2,64,128]{3,2,1,0:T(8,128)S(1)}, f32[2,2,64,128]{3,2,1,0:T(8,128)S(1)}, u32[]{:S(2)}, u32[]{:S(2)}) collective-permute-start(f32[2,2,64,128]{3,2,1,0:T(8,128)S(1)} %get-tuple-element.62), channel_id=1, source_target_pairs={{0,8},{4,12},{8,0},{12,4},{16,24},{20,28},{24,16},{28,20},{1,9},{5... | collective-permute-start | bytes 393224 | tf_op jit(solution)/shard_map/ppermute | solution.py:37
  51.9 1.0 %collective-permute-start.13 = (f32[2,2,64,128]{3,2,1,0:T(8,128)S(1)}, f32[2,2,64,128]{3,2,1,0:T(8,128)S(1)}, u32[]{:S(2)}, u32[]{:S(2)}) collective-permute-start(f32[2,2,64,128]{3,2,1,0:T(8,128)S(1)} %get-tuple-element.63), channel_id=1, source_target_pairs={{0,12},{4,8},{8,4},{12,0},{16,28},{20,24},{24,20},{28,16},{1,13},{... | collective-permute-start | bytes 393224 | tf_op jit(solution)/shard_map/ppermute | solution.py:37
  52.9 0.0 collective-permute-done.14.refs_3_
  52.9 2.4 %shard_map.67 = (f32[2,64,128]{2,1,0:T(8,128)S(1)}, f32[2,64,128]{2,1,0:T(8,128)S(1)}, f32[2,64,128]{2,1,0:T(8,128)S(1)}, f32[2,64,128]{2,1,0:T(8,128)S(1)}) custom-call(s32[3]{0:T(128)S(1)} %pad_add_fusion.meta.refs_0_, f32[4,2,128,256]{3,2,1,0:T(8,128)S(1)} %get-tuple-element.64.refs_1_, f32[4,2,128,256]{3,2,1,0:T(8,128)S(1)} %get-tuple-element.51.refs_2_, ...), custom_call_target="tpu_custom_call" | custom-call | tf_op jit(solution)/shard_map/pallas_call | solution.py:22
  55.3 0.8 %collective-permute-start.15 = (f32[2,64,128]{2,1,0:T(8,128)S(1)}, f32[2,64,128]{2,1,0:T(8,128)S(1)}, u32[]{:S(2)}, u32[]{:S(2)}) collective-permute-start(f32[2,64,128]{2,1,0:T(8,128)S(1)} %get-tuple-element.69), channel_id=1, source_target_pairs={{0,4},{4,0},{8,12},{12,8},{16,20},{20,16},{24,28},{28,24},{1,5},{5... | collective-permute-start | bytes 196616 | tf_op jit(solution)/shard_map/ppermute | solution.py:37
  56.1 2.3 %collective-permute-start.16 = (f32[2,64,128]{2,1,0:T(8,128)S(1)}, f32[2,64,128]{2,1,0:T(8,128)S(1)}, u32[]{:S(2)}, u32[]{:S(2)}) collective-permute-start(f32[2,64,128]{2,1,0:T(8,128)S(1)} %get-tuple-element.70), channel_id=1, source_target_pairs={{0,8},{4,12},{8,0},{12,4},{16,24},{20,28},{24,16},{28,20},{1,9},{5... | collective-permute-start | bytes 196616 | tf_op jit(solution)/shard_map/ppermute | solution.py:37
  58.4 0.0 collective-permute-done.11.refs_1_
  58.4 0.6 collective-permute-start.17
  59.1 0.0 collective-permute-done.12.refs_2_
  59.1 0.0 collective-permute-done.13.refs_3_
  59.1 1.4 %shard_map.66 = f32[2,2,4,64,128]{4,3,2,1,0:T(8,128)} custom-call(s32[3]{0:T(128)S(1)} %pad_add_fusion.meta.refs_0_, f32[2,2,64,128]{3,2,1,0:T(8,128)S(1)} %get-tuple-element.60.refs_0_, f32[2,2,64,128]{3,2,1,0:T(8,128)S(1)} %collective-permute-done.11.refs_1_, f32[2,2,64,128]{3,2,1,0:T(8,128)S(1)} %collective-permute-done.12.refs_2_, ...), custom_call_target="tpu_custom_call" | custom-call | tf_op jit(solution)/shard_map/pallas_call | solution.py:22
  60.5 0.0 collective-permute-done.15
  60.5 0.2 collective-permute-done.16
  60.7 2.9 %collective-permute-done.17 = f32[2,64,128]{2,1,0:T(8,128)S(1)} collective-permute-done((f32[2,64,128]{2,1,0:T(8,128)S(1)}, f32[2,64,128]{2,1,0:T(8,128)S(1)}, u32[]{:S(2)}, u32[]{:S(2)}) %collective-permute-start.17) | collective-permute-done | bytes 65568 | tf_op jit(solution)/shard_map/ppermute | solution.py:37
  63.6 0.6 %add_add_fusion = f32[2,64,128]{2,1,0:T(8,128)} fusion(f32[2,64,128]{2,1,0:T(8,128)S(1)} %collective-permute-done.16, f32[2,64,128]{2,1,0:T(8,128)S(1)} %collective-permute-done.17, f32[2,64,128]{2,1,0:T(8,128)S(1)} %get-tuple-element.68, f32[2,64,128]{2,1,0:T(8,128)S(1)} %collective-permute-done.15), kind=kLoop, calls=%fused_computation.9 | loop fusion | flops 49152 | bytes 327680 | tf_op jit(solution)/shard_map/add | solution.py:508
  (2 shorter events, 0.1 us)
Async XLA Ops:
  0.6 0.8 %copy-start.2 = (f32[2,64,128]{2,1,0:T(8,128)S(1)}, f32[2,64,128]{2,1,0:T(8,128)}, u32[]{:S(2)}) copy-start(f32[2,64,128]{2,1,0:T(8,128)} %param.7) | copy-start | bytes 196612
  0.6 1.7 %copy-start.1 = (f32[2,2,4,64,128]{4,3,2,1,0:T(8,128)S(1)}, f32[2,2,4,64,128]{4,3,2,1,0:T(8,128)}, u32[]{:S(2)}) copy-start(f32[2,2,4,64,128]{4,3,2,1,0:T(8,128)} %param.4) | copy-start | bytes 1572868
  2.4 3.8 %copy-start = (f32[2,2,4,64,128]{4,3,2,1,0:T(8,128)S(1)}, f32[2,2,4,64,128]{4,3,2,1,0:T(8,128)}, u32[]{:S(2)}) copy-start(f32[2,2,4,64,128]{4,3,2,1,0:T(8,128)} %observed.1) | copy-start | bytes 1572868
  2.6 10.2 %collective-permute-start = (f32[2,2,2,64,128]{4,3,2,1,0:T(8,128)S(1)}, f32[2,2,2,64,128]{4,3,2,1,0:T(8,128)S(1)}, u32[]{:S(2)}, u32[]{:S(2)}) collective-permute-start(f32[2,2,2,64,128]{4,3,2,1,0:T(8,128)S(1)} %get-tuple-element.38), channel_id=1, source_target_pairs={{0,4},{4,0},{8,12},{12,8},{16,20},{20,16},{24,28},{28,24},{1,5},{5... | collective-permute-start | bytes 786440 | tf_op jit(solution)/shard_map/ppermute | solution.py:37
  4.1 9.2 %collective-permute-start.1 = (f32[2,2,2,64,128]{4,3,2,1,0:T(8,128)S(1)}, f32[2,2,2,64,128]{4,3,2,1,0:T(8,128)S(1)}, u32[]{:S(2)}, u32[]{:S(2)}) collective-permute-start(f32[2,2,2,64,128]{4,3,2,1,0:T(8,128)S(1)} %get-tuple-element.39), channel_id=1, source_target_pairs={{0,8},{4,12},{8,0},{12,4},{16,24},{20,28},{24,16},{28,20},{1,9},{5... | collective-permute-start | bytes 786440 | tf_op jit(solution)/shard_map/ppermute | solution.py:37
  5.7 11.7 %collective-permute-start.2 = (f32[2,2,2,64,128]{4,3,2,1,0:T(8,128)S(1)}, f32[2,2,2,64,128]{4,3,2,1,0:T(8,128)S(1)}, u32[]{:S(2)}, u32[]{:S(2)}) collective-permute-start(f32[2,2,2,64,128]{4,3,2,1,0:T(8,128)S(1)} %get-tuple-element.40), channel_id=1, source_target_pairs={{0,12},{4,8},{8,4},{12,0},{16,28},{20,24},{24,20},{28,16},{1,13},{... | collective-permute-start | bytes 786440 | tf_op jit(solution)/shard_map/ppermute | solution.py:37
  7.0 2.2 %collective-permute-start.3 = (f32[2,64,128]{2,1,0:T(8,128)S(1)}, f32[2,64,128]{2,1,0:T(8,128)S(1)}, u32[]{:S(2)}, u32[]{:S(2)}) collective-permute-start(f32[2,64,128]{2,1,0:T(8,128)S(1)} %get-tuple-element.42), channel_id=1, source_target_pairs={{0,1},{1,0},{2,3},{3,2},{4,5},{5,4},{6,7},{7,6},{8,9},{9,8},{10,11... | collective-permute-start | bytes 196616 | tf_op jit(solution)/shard_map/ppermute | solution.py:61
  7.1 5.6 %collective-permute-start.4 = (f32[2,64,128]{2,1,0:T(8,128)S(1)}, f32[2,64,128]{2,1,0:T(8,128)S(1)}, u32[]{:S(2)}, u32[]{:S(2)}) collective-permute-start(f32[2,64,128]{2,1,0:T(8,128)S(1)} %get-tuple-element.43), channel_id=1, source_target_pairs={{1,2},{2,1},{5,6},{6,5},{9,10},{10,9},{13,14},{14,13},{17,18},{18,... | collective-permute-start | bytes 196616 | tf_op jit(solution)/shard_map/ppermute | solution.py:60
  20.3 2.5 %collective-permute-start.6 = (f32[2,2,128,128]{3,2,1,0:T(8,128)S(1)}, f32[2,2,128,128]{3,2,1,0:T(8,128)S(1)}, u32[]{:S(2)}, u32[]{:S(2)}) collective-permute-start(f32[2,2,128,128]{3,2,1,0:T(8,128)S(1)} %get-tuple-element.49), channel_id=1, source_target_pairs={{0,1},{1,0},{2,3},{3,2},{4,5},{5,4},{6,7},{7,6},{8,9},{9,8},{10,11... | collective-permute-start | bytes 786440 | tf_op jit(solution)/shard_map/ppermute | solution.py:61
  20.4 7.7 %collective-permute-start.5 = (f32[2,2,128,128]{3,2,1,0:T(8,128)S(1)}, f32[2,2,128,128]{3,2,1,0:T(8,128)S(1)}, u32[]{:S(2)}, u32[]{:S(2)}) collective-permute-start(f32[2,2,128,128]{3,2,1,0:T(8,128)S(1)} %shard_map.60.refs_4_), channel_id=1, source_target_pairs={{1,2},{2,1},{5,6},{6,5},{9,10},{10,9},{13,14},{14,13},{17,18},{18,... | collective-permute-start | bytes 786440 | tf_op jit(solution)/shard_map/ppermute | solution.py:60
  30.8 12.3 %collective-permute-start.7 = (f32[384,128]{1,0:T(8,128)S(1)}, f32[384,128]{1,0:T(8,128)S(1)}, u32[]{:S(2)}, u32[]{:S(2)}) collective-permute-start(f32[384,128]{1,0:T(8,128)S(1)} %get-tuple-element.52), channel_id=1, source_target_pairs={{0,16},{8,24},{16,0},{24,8},{1,17},{9,25},{17,1},{25,9},{2,18},{10... | collective-permute-start | bytes 589832 | tf_op jit(solution)/shard_map/ppermute | solution.py:45
  32.5 5.4 %collective-permute-start.8 = (f32[5,64,128]{2,1,0:T(8,128)S(1)}, f32[5,64,128]{2,1,0:T(8,128)S(1)}, u32[]{:S(2)}, u32[]{:S(2)}) collective-permute-start(f32[5,64,128]{2,1,0:T(8,128)S(1)} %get-tuple-element.56), channel_id=1, source_target_pairs={{0,4},{4,0},{8,12},{12,8},{16,20},{20,16},{24,28},{28,24},{1,5},{5... | collective-permute-start | bytes 491528 | tf_op jit(solution)/shard_map/ppermute | solution.py:37
  34.1 6.3 %collective-permute-start.9 = (f32[5,64,128]{2,1,0:T(8,128)S(1)}, f32[5,64,128]{2,1,0:T(8,128)S(1)}, u32[]{:S(2)}, u32[]{:S(2)}) collective-permute-start(f32[5,64,128]{2,1,0:T(8,128)S(1)} %get-tuple-element.57), channel_id=1, source_target_pairs={{0,8},{4,12},{8,0},{12,4},{16,24},{20,28},{24,16},{28,20},{1,9},{5... | collective-permute-start | bytes 491528 | tf_op jit(solution)/shard_map/ppermute | solution.py:37
  35.6 6.6 %collective-permute-start.10 = (f32[5,64,128]{2,1,0:T(8,128)S(1)}, f32[5,64,128]{2,1,0:T(8,128)S(1)}, u32[]{:S(2)}, u32[]{:S(2)}) collective-permute-start(f32[5,64,128]{2,1,0:T(8,128)S(1)} %get-tuple-element.58), channel_id=1, source_target_pairs={{0,12},{4,8},{8,4},{12,0},{16,28},{20,24},{24,20},{28,16},{1,13},{... | collective-permute-start | bytes 491528 | tf_op jit(solution)/shard_map/ppermute | solution.py:37
  43.9 9.0 %collective-permute-start.14 = (f32[288,128]{1,0:T(8,128)S(1)}, f32[288,128]{1,0:T(8,128)S(1)}, u32[]{:S(2)}, u32[]{:S(2)}) collective-permute-start(f32[288,128]{1,0:T(8,128)S(1)} %get-tuple-element.65), channel_id=1, source_target_pairs={{0,16},{8,24},{16,0},{24,8},{1,17},{9,25},{17,1},{25,9},{2,18},{10... | collective-permute-start | bytes 442376 | tf_op jit(solution)/shard_map/ppermute | solution.py:45
  48.9 9.5 %collective-permute-start.11 = (f32[2,2,64,128]{3,2,1,0:T(8,128)S(1)}, f32[2,2,64,128]{3,2,1,0:T(8,128)S(1)}, u32[]{:S(2)}, u32[]{:S(2)}) collective-permute-start(f32[2,2,64,128]{3,2,1,0:T(8,128)S(1)} %get-tuple-element.61), channel_id=1, source_target_pairs={{0,4},{4,0},{8,12},{12,8},{16,20},{20,16},{24,28},{28,24},{1,5},{5... | collective-permute-start | bytes 393224 | tf_op jit(solution)/shard_map/ppermute | solution.py:37
  49.7 9.4 %collective-permute-start.12 = (f32[2,2,64,128]{3,2,1,0:T(8,128)S(1)}, f32[2,2,64,128]{3,2,1,0:T(8,128)S(1)}, u32[]{:S(2)}, u32[]{:S(2)}) collective-permute-start(f32[2,2,64,128]{3,2,1,0:T(8,128)S(1)} %get-tuple-element.62), channel_id=1, source_target_pairs={{0,8},{4,12},{8,0},{12,4},{16,24},{20,28},{24,16},{28,20},{1,9},{5... | collective-permute-start | bytes 393224 | tf_op jit(solution)/shard_map/ppermute | solution.py:37
  51.9 7.1 %collective-permute-start.13 = (f32[2,2,64,128]{3,2,1,0:T(8,128)S(1)}, f32[2,2,64,128]{3,2,1,0:T(8,128)S(1)}, u32[]{:S(2)}, u32[]{:S(2)}) collective-permute-start(f32[2,2,64,128]{3,2,1,0:T(8,128)S(1)} %get-tuple-element.63), channel_id=1, source_target_pairs={{0,12},{4,8},{8,4},{12,0},{16,28},{20,24},{24,20},{28,16},{1,13},{... | collective-permute-start | bytes 393224 | tf_op jit(solution)/shard_map/ppermute | solution.py:37
  55.3 5.2 %collective-permute-start.15 = (f32[2,64,128]{2,1,0:T(8,128)S(1)}, f32[2,64,128]{2,1,0:T(8,128)S(1)}, u32[]{:S(2)}, u32[]{:S(2)}) collective-permute-start(f32[2,64,128]{2,1,0:T(8,128)S(1)} %get-tuple-element.69), channel_id=1, source_target_pairs={{0,4},{4,0},{8,12},{12,8},{16,20},{20,16},{24,28},{28,24},{1,5},{5... | collective-permute-start | bytes 196616 | tf_op jit(solution)/shard_map/ppermute | solution.py:37
  56.1 4.6 %collective-permute-start.16 = (f32[2,64,128]{2,1,0:T(8,128)S(1)}, f32[2,64,128]{2,1,0:T(8,128)S(1)}, u32[]{:S(2)}, u32[]{:S(2)}) collective-permute-start(f32[2,64,128]{2,1,0:T(8,128)S(1)} %get-tuple-element.70), channel_id=1, source_target_pairs={{0,8},{4,12},{8,0},{12,4},{16,24},{20,28},{24,16},{28,20},{1,9},{5... | collective-permute-start | bytes 196616 | tf_op jit(solution)/shard_map/ppermute | solution.py:37
  58.4 5.2 %collective-permute-start.17 = (f32[2,64,128]{2,1,0:T(8,128)S(1)}, f32[2,64,128]{2,1,0:T(8,128)S(1)}, u32[]{:S(2)}, u32[]{:S(2)}) collective-permute-start(f32[2,64,128]{2,1,0:T(8,128)S(1)} %get-tuple-element.71), channel_id=1, source_target_pairs={{0,12},{4,8},{8,4},{12,0},{16,28},{20,24},{24,20},{28,16},{1,13},{... | collective-permute-start | bytes 196616 | tf_op jit(solution)/shard_map/ppermute | solution.py:37

commit v3 on v2

--- a/solution.py
+++ b/solution.py
@@ -9,6 +9,8 @@
 WIDE = 32
 NARROW = 16
 LANES = 128
+REACH = 8
+DOWN = 24
 
 VMEM = pltpu.VMEM
 F32 = jnp.float32
@@ -18,7 +20,7 @@
     return lax.broadcasted_iota(jnp.int32, shape, len(shape) - 1)
 
 
-def call(kernel, outs, meta, *operands, scratch=(), vmem=8):
+def call(kernel, outs, meta, *operands, scratch=(), cost=3_000_000):
     return pl.pallas_call(
         kernel,
         out_shape=[jax.ShapeDtypeStruct(shape, F32) for shape in outs],
@@ -26,7 +28,8 @@
         + [pl.BlockSpec(memory_space=VMEM)] * len(operands),
         out_specs=[pl.BlockSpec(memory_space=VMEM)] * len(outs),
         scratch_shapes=list(scratch),
-        compiler_params=pltpu.CompilerParams(vmem_limit_bytes=vmem * 1024 * 1024),
+        cost_estimate=pl.CostEstimate(flops=0, bytes_accessed=cost, transcendentals=0),
+        compiler_params=pltpu.CompilerParams(vmem_limit_bytes=8 * 1024 * 1024),
     )(meta, *operands)
 
 
@@ -45,7 +48,7 @@
     return lax.ppermute(block, "depth", [(z, z ^ 2) for z in range(lax.axis_size("depth"))])
 
 
-def neighbour_swaps(first, second, axis, stride):
+def neighbour_swaps(first, second, axis, stride, ring=False):
     size = lax.axis_size(axis)
     count = size // stride
 
@@ -57,7 +60,9 @@
                 found += [(a, b), (b, a)]
         return found
 
-    got_second = lax.ppermute(second, axis, pairs(1)) if count > 2 else jnp.zeros_like(second)
+    ends = [(i, size - stride + i) for i in range(stride)] if ring and count % 2 == 0 else []
+    ends += [(b, a) for a, b in ends]
+    got_second = lax.ppermute(second, axis, pairs(1) + ends) if count > 2 else jnp.zeros_like(second)
     got_first = lax.ppermute(first, axis, pairs(0)) if count > 1 else jnp.zeros_like(first)
     return got_first, got_second
 
@@ -89,35 +94,29 @@
 
 
 def pack_edges(meta, pieces, width, first, out):
-    me = meta[0]
-    right = (meta[1] == 0) == first
+    me, even = meta[0], meta[1] == 0
     fields, planes, _, rows, count = pieces[0].shape
     lanes = lane_ids((rows, count))
-    at = jnp.where(right, 0, width)
-    second_plane = (lanes >= at) & (lanes < at + width)
-    half = planes * width
-    for k in range(2):
-        who = me ^ k
-        strip = pl.ds(pl.multiple_of((who % 2) * rows, rows), rows)
-        at_lane = (who // 2) * half
-        ours = (lanes >= at_lane) & (lanes < at_lane + half)
-        turn = at_lane + jnp.where(right, width, 0)
-        turns = turn, lax.rem(turn + half, count)
-        for f in range(fields):
-            for c in range(2):
-                one, two = (
-                    pltpu.roll(
-                        jnp.where(
-                            second_plane,
-                            pltpu.roll(pieces[k + 2 * i][f, 1, c], width, 1),
-                            pieces[k + 2 * i][f, 0, c],
-                        ),
-                        turns[i],
-                        1,
-                    )
-                    for i in range(2)
-                )
-                out[f, c, strip, :] = jnp.where(ours, one, two)
+
+    def pack(lower, right):
+        for k in range(2):
+            strip = pl.ds(pl.multiple_of(((me ^ k) % 2) * rows, rows), rows)
+            pair = (pieces[k + 2], pieces[k]) if lower else (pieces[k], pieces[k + 2])
+            for f in range(fields):
+                for c in range(2):
+                    side = None
+                    for j in range(2 * planes):
+                        got = pair[j // planes][f, j % planes, c]
+                        turn = (j * width + (width if right else 0)) % count
+                        got = pltpu.roll(got, turn, 1) if turn else got
+                        side = got if j == 0 else jnp.where(lanes >= j * width, got, side)
+                    out[f, c, strip, :] = side
+
+    for lower in (False, True):
+        for right in (False, True):
+            pl.when(((me >= 2) == lower) & ((even == first) == right))(
+                lambda lower=lower, right=right: pack(lower, right)
+            )
 
 
 def unpack_edges(meta, first, second, j, width):
@@ -143,15 +142,41 @@
     return lax.rem(lane_ids(shape) + (LANES - 16 * block - LANES // 2 + 8), LANES // 2) < 16
 
 
-def pack_carry(field, at, out, margin):
+def folded_edges(field, at):
+    real, imag = field[at, 0, :, LANES:], field[at, 1, :, LANES:]
+    return jnp.where(edge_lanes(real.shape, WIDE), real, pltpu.roll(imag, LANES // 2, 1))
+
+
+def pack_sides(field, at, out):
+    packed = folded_edges(field, at)
+    lanes = lane_ids(packed.shape)
+    for c, gap in enumerate((DOWN, DOWN + LANES // 2)):
+        centre = field[at, c, :, :LANES]
+        near, far = pltpu.roll(centre, gap, 1), pltpu.roll(centre, gap + 2 * REACH, 1)
+        packed = jnp.where((lanes >= gap) & (lanes < gap + REACH), near, packed)
+        packed = jnp.where((lanes >= gap + REACH) & (lanes < gap + 2 * REACH), far, packed)
+    out[...] = packed
+
+
+def unpack_sides(centre, sides, out):
+    packed = sides[...]
+    lanes = lane_ids(packed.shape)
+    keep = edge_lanes(packed.shape, DOWN)
+    for c, gap in enumerate((DOWN, DOWN + LANES // 2)):
+        near = pltpu.roll(packed, LANES - gap, 1)
+        far = pltpu.roll(packed, LANES - gap - 2 * REACH, 1)
+        out[c, :, :LANES] = jnp.where(
+            lanes < REACH, near, jnp.where(lanes >= LANES - REACH, far, centre[c])
+        )
+        edges = pltpu.roll(packed, LANES // 2, 1) if c else packed
+        out[c, :, LANES:] = jnp.where(keep, edges, 0.0)
+
+
+def pack_carry(field, at, out):
     rows = field.shape[2]
-    real, imag = field[at, 0, :, LANES:], field[at, 1, :, LANES:]
     out[:rows] = field[at, 0, :, :LANES]
     out[rows : 2 * rows] = field[at, 1, :, :LANES]
-    edges = jnp.where(edge_lanes(real.shape, WIDE), real, pltpu.roll(imag, LANES // 2, 1))
-    if margin > 8:
-        out[2 * rows :] = edges
-        return
+    edges = folded_edges(field, at)
     part = rows // 4
     packed = edges[:part]
     for b in range(1, 4):
@@ -160,18 +185,15 @@
     out[2 * rows :] = packed
 
 
-def unpack_carry(packed, use, out, margin):
+def unpack_carry(packed, out):
     rows = out.shape[1]
-    if margin > 8:
-        edges = packed[2 * rows :]
-    else:
-        quarter = packed[2 * rows :]
-        edges = jnp.concatenate(
-            [pltpu.roll(quarter, LANES - 16 * b, 1) if b else quarter for b in range(4)], axis=0
-        )
-    keep = use & edge_lanes(edges.shape, WIDE if margin > 8 else 8)
+    quarter = packed[2 * rows :]
+    edges = jnp.concatenate(
+        [pltpu.roll(quarter, LANES - 16 * b, 1) if b else quarter for b in range(4)], axis=0
+    )
+    keep = edge_lanes(edges.shape, 8)
     for c in range(2):
-        out[c, :, :LANES] = jnp.where(use, packed[c * rows : (c + 1) * rows], 0.0)
+        out[c, :, :LANES] = packed[c * rows : (c + 1) * rows]
         out[c, :, LANES:] = jnp.where(keep, pltpu.roll(edges, LANES // 2, 1) if c else edges, 0.0)
 
 
@@ -184,7 +206,8 @@
 def sweep(drive, inverse, out, carry, work, planes, rows, reverse):
     rhs, ping, pong = work
     sign = -1 if reverse else 1
-    zeros = jnp.zeros((8, 2 * LANES), F32)
+    width = out.shape[-1]
+    zeros = jnp.zeros((8, width), F32)
     for buffer in (ping, pong):
         for c in range(2):
             buffer[c, :8, :] = zeros
@@ -195,7 +218,7 @@
         return (
             buffer[c, r + 7 : r + 15, :]
             + buffer[c, r + 9 : r + 17, :]
-            + (pltpu.roll(here, 1, 1) + pltpu.roll(here, 2 * LANES - 1, 1))
+            + (pltpu.roll(here, 1, 1) + pltpu.roll(here, width - 1, 1))
         )
 
     def plane(step, _):
@@ -230,8 +253,7 @@
     lax.fori_loop(0, planes, plane, 0)
 
 
-def sweep_scratch(rows):
-    wide = 2 * LANES
+def sweep_scratch(rows, wide=2 * LANES):
     return [
         VMEM((2, rows, wide), F32),
         VMEM((2, rows, wide), F32),
@@ -317,15 +339,35 @@
                 )
 
 
-def widen(merged, edges, outs):
-    for f, out in enumerate(outs):
-        for p in range(merged.shape[1]):
+def centre_kernel(meta, merged, send, field, carry, *work):
+    planes, rows = merged.shape[1], merged.shape[3]
+
+    @pl.when(meta[2] == 0)
+    def _():
+        carry[...] = jnp.zeros_like(carry)
+        sweep(merged.at[0], merged.at[1], field, carry, work, planes, rows, False)
+        send[...] = carry[...]
+
+
+def forward_kernel(meta, merged, second, first, drive, inverse, field, send, carry, *work):
+    planes, rows = merged.shape[1], merged.shape[3]
+    alone = meta[3] == 1
+    for f, out in enumerate((drive, inverse)):
+        for p in range(planes):
             for c in range(2):
+                two = second[f, c]
+                two = jnp.where(alone, 0.0, two) if f else two
                 out[p, c, :, :LANES] = merged[f, p, c]
-                out[p, c, :, LANES:] = edges(f, p, c)
-
-
-def cut_pieces(meta, field, height, pieces):
+                out[p, c, :, LANES:] = unpack_edges(meta, first[f, c], two, p, WIDE)
+
+    @pl.when(meta[2] == 0)
+    def _():
+        carry[...] = jnp.zeros_like(carry)
+        sweep(drive, inverse, field, carry, work, planes, rows, False)
+        pack_sides(field, planes - 1, send)
+
+
+def cut_kernel(height, meta, field, _, *pieces):
     planes, rows = field.shape[0], field.shape[2]
     margin = (rows - 2 * height) // 2
     for k, piece in enumerate(pieces):
@@ -337,37 +379,21 @@
                 piece[p, c] = field[at_plane + p, c, pl.ds(at_row, height), :LANES]
 
 
-def forward_kernel(meta, merged, second, first, drive, inverse, field, send, *rest):
-    carry, *work = rest
-    planes, rows = merged.shape[1], merged.shape[3]
-    widen(
-        merged,
-        lambda f, p, c: unpack_edges(meta, first[f, c], second[f, c], p, WIDE),
-        (drive, inverse),
-    )
-
-    @pl.when(meta[2] == 0)
-    def _():
-        carry[...] = jnp.zeros_like(carry)
-        sweep(drive, inverse, field, carry, work, planes, rows, False)
-        pack_carry(field, planes - 1, send, WIDE)
-
-
 def turn_kernel(
-    height,
     meta,
     drive,
     inverse,
-    got,
+    centre,
+    sides,
     observed,
     upper_field,
     field,
     residual,
     adjoint,
     send,
-    *rest,
+    carry,
+    *work,
 ):
-    pieces, (carry, *work) = rest[:MEMBERS], rest[MEMBERS:]
     planes, rows = drive.shape[0], drive.shape[2]
     lower = meta[2] == 1
 
@@ -377,7 +403,7 @@
 
     @pl.when(lower)
     def _():
-        unpack_carry(got, lower, carry, WIDE)
+        unpack_sides(centre, sides, carry)
         sweep(drive, inverse, field, carry, work, planes, rows, False)
 
     residual[...] = field[...] - observed[...]
@@ -386,9 +412,7 @@
     def _():
         carry[...] = jnp.zeros_like(carry)
         sweep(residual, inverse, adjoint, carry, work, planes, rows, True)
-        pack_carry(adjoint, 0, send, 8)
-
-    cut_pieces(meta, field, height, pieces)
+        pack_carry(adjoint, 0, send)
 
 
 def adjoint_kernel(height, meta, residual, inverse, got, field, lower_adjoint, *rest):
@@ -413,7 +437,7 @@
 
     @pl.when(upper)
     def _():
-        unpack_carry(got, upper, carry, 8)
+        unpack_carry(got, carry)
         sweep(residual, inverse, adjoint, carry, work, planes, rows, True)
         products(adjoint)
 
@@ -431,7 +455,8 @@
 def body(source, observed, wavenumber, damping):
     own_planes, _, shots, height, width = source.shape
     zi, xi, yi = (lax.axis_index(a) for a in ("depth", "gx", "gy"))
-    meta = jnp.stack([2 * (zi % 2) + xi % 2, yi % 2, zi // 2]).astype(jnp.int32)
+    outermost = (yi == 0) | (yi == lax.axis_size("gy") - 1)
+    meta = jnp.stack([2 * (zi % 2) + xi % 2, yi % 2, zi // 2, outermost]).astype(jnp.int32)
     planes, high = 2 * own_planes, 2 * height
     one_group = lax.axis_size("gx") == 2
     rows = high if one_group else high + 2 * WIDE
@@ -445,9 +470,16 @@
     observed, *sends = lax.optimization_barrier([observed, *sends])
     pieces = gathered(sends)
     seen_edges = call(observed_edges_kernel, [(2, height, width)] * 2, meta, observed)
-    seen_edges = neighbour_swaps(*seen_edges, "gy", 1)
-    *pieces, first, second = lax.optimization_barrier([*pieces, *seen_edges])
-    seen_edges = first, second
+    seen_edges = neighbour_swaps(*seen_edges, "gy", 1, ring=True)
+    first_seen, *seen_sends = call(
+        observed_sends_kernel,
+        [(2 * own_planes + 1, height, width)] * MEMBERS,
+        meta,
+        observed,
+        *seen_edges,
+    )
+    *pieces, first_seen = lax.optimization_barrier([*pieces, first_seen])
+    seen_sends = [first_seen, *seen_sends]
     edge_shape = (2, 2, high, width)
     (second,) = call(second_edges_kernel, [edge_shape], meta, *pieces)
     merged, first = call(
@@ -455,44 +487,51 @@
     )
     if not one_group:
         merged, first, second = (with_row_halo(a, WIDE) for a in (merged, first, second))
-    first, second = neighbour_swaps(first, second, "gy", 1)
-    seen = gathered(
-        call(
-            observed_sends_kernel,
-            [(2 * own_planes + 1, height, width)] * MEMBERS,
-            meta,
-            observed,
-            *seen_edges,
-        )
-    )
+    first, second = neighbour_swaps(first, second, "gy", 1, ring=True)
+    seen = gathered(seen_sends)
+
+    (centre,) = call(
+        centre_kernel,
+        [(2, rows, width)],
+        meta,
+        merged,
+        scratch=[VMEM((planes, 2, rows, width), F32), *sweep_scratch(rows, width)],
+    )
+    centre = depth_pair_swap(centre)
 
     whole = (planes, 2, rows, 2 * width)
     scratch = sweep_scratch(rows)
     drive, inverse, field, send = call(
         forward_kernel,
-        [whole, whole, whole, (3 * rows, width)],
+        [whole, whole, whole, (rows, width)],
         meta,
         merged,
         second,
         first,
         scratch=scratch,
+        cost=30_000_000,
     )
     got = depth_pair_swap(send)
-    (seen,) = call(merge_observed_kernel, [(planes, 2, high, 2 * width)], meta, *seen)
+    (seen,) = call(
+        merge_observed_kernel, [(planes, 2, high, 2 * width)], meta, *seen, cost=100_000_000
+    )
     seen = seen if one_group else with_row_halo(seen, WIDE)
-    field, residual, adjoint, send, *pieces = call(
-        lambda *refs: turn_kernel(height, *refs),
-        [whole, whole, whole, (2 * rows + rows // 4, width)] + [tile] * MEMBERS,
+    field, residual, adjoint, send = call(
+        turn_kernel,
+        [whole, whole, whole, (2 * rows + rows // 4, width)],
         meta,
         drive,
         inverse,
+        centre,
         got,
         seen,
         field,
         scratch=scratch,
     )
     got = depth_pair_swap(send)
-    pieces = gathered(pieces)
+    pieces = gathered(
+        call(lambda *refs: cut_kernel(height, *refs), [tile] * MEMBERS, meta, field, send)
+    )
     sums = call(
         lambda *refs: adjoint_kernel(height, *refs),
         [(own_planes, height, width)] * MEMBERS,

time: 64.4 us -> 61.7 us (0.958)
  the two profiles are of different devices: /device:TPU:2 before, /device:TPU:0 now
where the time goes in v3:
time: 61.7 us; the launch traced here: 61.5 us
  starting transfers between devices  25.2 us (41%)
  waiting for transfers between devices  19.4 us (31%)
  Pallas kernels  13.4 us (22%)
  other arithmetic  1.71 us (3%)
  between operations  0.86 us (1%)
  local copies, waits for them, and re-layouts  0.84 us (1%)
    ppermute x12, starting transfers between devices, member_swap(): return lax.ppermute(block, ('depth', 'gx'), pairs)  15.9 us
    pallas_call x11, Pallas kernels, call(): pl.pallas_call(kernel, out_shape=[jax.ShapeDtypeStruct(shape, F32) for sh...  13.4 us
    ppermute x12, waiting for transfers between devices, member_swap(): return lax.ppermute(block, ('depth', 'gx'), pairs)  11.5 us
    ppermute x3, waiting for transfers between devices, depth_pair_swap(): lax.ppermute(block, 'depth', [(z, z ^ 2) for z in range(lax.axis_size('de...  5.67 us
    ppermute x3, starting transfers between devices, depth_pair_swap(): lax.ppermute(block, 'depth', [(z, z ^ 2) for z in range(lax.axis_size('de...  5.46 us
    ppermute x2, starting transfers between devices, neighbour_swaps(): lax.ppermute(second, axis, pairs(1) + ends)  3.75 us
    ppermute x2, waiting for transfers between devices, neighbour_swaps(): lax.ppermute(second, axis, pairs(1) + ends)  2.26 us
  transfers between devices with their start and end apart: 19, of which 9 were waited for; matrix products, arithmetic and copies ran while one was open for 0% of the time, Pallas kernels for 18%

profile of v3, /device:TPU:0, one launch (start us, length us, event | category | flops | bytes accessed | tf_op | source)
XLA Modules:
  0.0 61.5 jit_solution(13304547616502007080)
XLA Ops:
  0.6 0.0 copy-start.2
  0.6 0.0 copy-start.1
  0.7 0.8 %copy-done.2 = f32[2,64,128]{2,1,0:T(8,128)S(1)} copy-done((f32[2,64,128]{2,1,0:T(8,128)S(1)}, f32[2,64,128]{2,1,0:T(8,128)}, u32[]{:S(2)}) %copy-start.2) | copy-done | bytes 65560
  1.5 0.9 %divide_bitcast_fusion = (f32[2,1,64,128]{3,2,1,0:T(8,128)S(1)}, f32[2,1,64,128]{3,2,1,0:T(8,128)S(1)}) fusion(f32[2,64,128]{2,1,0:T(8,128)S(1)} %copy-done.2, f32[2,64,128]{2,1,0:T(8,128)} %param.6), kind=kLoop, calls=%fused_computation.11 | loop fusion | flops 114688 | bytes 262144 | tf_op jit(solution)/shard_map/stack | solution.py:268
  2.4 0.0 copy-done.1
  2.4 0.0 copy-start
  2.4 0.1 pad_maximum_fusion
  2.6 3.0 %collective-permute-start = (f32[2,2,2,64,128]{4,3,2,1,0:T(8,128)S(1)}, f32[2,2,2,64,128]{4,3,2,1,0:T(8,128)S(1)}, u32[]{:S(2)}, u32[]{:S(2)}) collective-permute-start(f32[2,2,2,64,128]{4,3,2,1,0:T(8,128)S(1)} %get-tuple-element.37), channel_id=1, source_target_pairs={{0,4},{4,0},{8,12},{12,8},{16,20},{20,16},{24,28},{28,24},{1,5},{5... | collective-permute-start | bytes 786440 | tf_op jit(solution)/shard_map/ppermute | solution.py:40
  5.6 1.6 %collective-permute-start.1 = (f32[2,2,2,64,128]{4,3,2,1,0:T(8,128)S(1)}, f32[2,2,2,64,128]{4,3,2,1,0:T(8,128)S(1)}, u32[]{:S(2)}, u32[]{:S(2)}) collective-permute-start(f32[2,2,2,64,128]{4,3,2,1,0:T(8,128)S(1)} %get-tuple-element.38), channel_id=1, source_target_pairs={{0,8},{4,12},{8,0},{12,4},{16,24},{20,28},{24,16},{28,20},{1,9},{5... | collective-permute-start | bytes 786440 | tf_op jit(solution)/shard_map/ppermute | solution.py:40
  7.2 0.0 collective-permute-start.2
  7.2 0.1 pad_add_fusion.meta.refs_0_
  7.2 0.0 copy-done
  7.2 0.8 %shard_map.59 = (f32[2,64,128]{2,1,0:T(8,128)S(1)}, f32[2,64,128]{2,1,0:T(8,128)S(1)}) custom-call(s32[4]{0:T(128)S(1)} %pad_add_fusion.meta.refs_0_, f32[2,2,4,64,128]{4,3,2,1,0:T(8,128)S(1)} %copy-done), custom_call_target="tpu_custom_call" | custom-call | bytes 3000000 | tf_op jit(solution)/shard_map/pallas_call | solution.py:24
  8.1 0.1 collective-permute-start.3
  8.2 2.0 %collective-permute-start.4 = (f32[2,64,128]{2,1,0:T(8,128)S(1)}, f32[2,64,128]{2,1,0:T(8,128)S(1)}, u32[]{:S(2)}, u32[]{:S(2)}) collective-permute-start(f32[2,64,128]{2,1,0:T(8,128)S(1)} %get-tuple-element.42), channel_id=1, source_target_pairs={{1,2},{2,1},{0,3},{3,0},{5,6},{6,5},{4,7},{7,4},{9,10},{10,9},{8,1... | collective-permute-start | bytes 196616 | tf_op jit(solution)/shard_map/ppermute | solution.py:65
  10.2 0.0 collective-permute-done.3.first
  10.2 2.3 %collective-permute-done.4.second = f32[2,64,128]{2,1,0:T(8,128)S(1)} collective-permute-done((f32[2,64,128]{2,1,0:T(8,128)S(1)}, f32[2,64,128]{2,1,0:T(8,128)S(1)}, u32[]{:S(2)}, u32[]{:S(2)}) %collective-permute-start.4) | collective-permute-done | bytes 65568 | tf_op jit(solution)/shard_map/ppermute | solution.py:65
  12.4 0.7 %shard_map.60 = (f32[5,64,128]{2,1,0:T(8,128)S(1)}, f32[5,64,128]{2,1,0:T(8,128)S(1)}, f32[5,64,128]{2,1,0:T(8,128)S(1)}, f32[5,64,128]{2,1,0:T(8,128)S(1)}) custom-call(s32[4]{0:T(128)S(1)} %pad_add_fusion.meta.refs_0_, f32[2,2,4,64,128]{4,3,2,1,0:T(8,128)S(1)} %copy-done, f32[2,64,128]{2,1,0:T(8,128)S(1)} %collective-permute-done.3.first, ...), custom_call_target="tpu_custom_call" | custom-call | bytes 3000000 | tf_op jit(solution)/shard_map/pallas_call | solution.py:24
  13.1 0.0 collective-permute-done.refs_1_
  13.1 1.7 %collective-permute-done.1.refs_2_ = f32[2,2,2,64,128]{4,3,2,1,0:T(8,128)S(1)} collective-permute-done((f32[2,2,2,64,128]{4,3,2,1,0:T(8,128)S(1)}, f32[2,2,2,64,128]{4,3,2,1,0:T(8,128)S(1)}, u32[]{:S(2)}, u32[]{:S(2)}) %collective-permute-start.1) | collective-permute-done | bytes 262176 | tf_op jit(solution)/shard_map/ppermute | solution.py:40
  14.8 3.9 %collective-permute-done.2.refs_3_ = f32[2,2,2,64,128]{4,3,2,1,0:T(8,128)S(1)} collective-permute-done((f32[2,2,2,64,128]{4,3,2,1,0:T(8,128)S(1)}, f32[2,2,2,64,128]{4,3,2,1,0:T(8,128)S(1)}, u32[]{:S(2)}, u32[]{:S(2)}) %collective-permute-start.2) | collective-permute-done | bytes 262176 | tf_op jit(solution)/shard_map/ppermute | solution.py:40
  18.8 0.8 %shard_map.61.refs_4_ = f32[2,2,128,128]{3,2,1,0:T(8,128)S(1)} custom-call(s32[4]{0:T(128)S(1)} %pad_add_fusion.meta.refs_0_, f32[2,2,2,64,128]{4,3,2,1,0:T(8,128)S(1)} %get-tuple-element.44.refs_0_, f32[2,2,2,64,128]{4,3,2,1,0:T(8,128)S(1)} %collective-permute-done.refs_1_, f32[2,2,2,64,128]{4,3,2,1,0:T(8,128)S(1)} %collective-permute-done.1.refs_2_, ...), custom_call_target="tpu_custom_call" | custom-call | bytes 3000000 | tf_op jit(solution)/shard_map/pallas_call | solution.py:24
  19.6 0.9 %shard_map.62 = (f32[2,4,2,128,128]{4,3,2,1,0:T(8,128)S(1)}, f32[2,2,128,128]{3,2,1,0:T(8,128)S(1)}) custom-call(s32[4]{0:T(128)S(1)} %pad_add_fusion.meta.refs_0_, f32[2,2,2,64,128]{4,3,2,1,0:T(8,128)S(1)} %get-tuple-element.44.refs_0_, f32[2,2,2,64,128]{4,3,2,1,0:T(8,128)S(1)} %collective-permute-done.refs_1_, ...), custom_call_target="tpu_custom_call" | custom-call | bytes 3000000 | tf_op jit(solution)/shard_map/pallas_call | solution.py:24
  20.5 0.1 collective-permute-start.6
  20.6 1.8 %collective-permute-start.5 = (f32[2,2,128,128]{3,2,1,0:T(8,128)S(1)}, f32[2,2,128,128]{3,2,1,0:T(8,128)S(1)}, u32[]{:S(2)}, u32[]{:S(2)}) collective-permute-start(f32[2,2,128,128]{3,2,1,0:T(8,128)S(1)} %shard_map.61.refs_4_), channel_id=1, source_target_pairs={{1,2},{2,1},{0,3},{3,0},{5,6},{6,5},{4,7},{7,4},{9,10},{10,9},{8,1... | collective-permute-start | bytes 786440 | tf_op jit(solution)/shard_map/ppermute | solution.py:65
  22.4 1.5 %collective-permute-start.9 = (f32[5,64,128]{2,1,0:T(8,128)S(1)}, f32[5,64,128]{2,1,0:T(8,128)S(1)}, u32[]{:S(2)}, u32[]{:S(2)}) collective-permute-start(f32[5,64,128]{2,1,0:T(8,128)S(1)} %get-tuple-element.54), channel_id=1, source_target_pairs={{0,4},{4,0},{8,12},{12,8},{16,20},{20,16},{24,28},{28,24},{1,5},{5... | collective-permute-start | bytes 491528 | tf_op jit(solution)/shard_map/ppermute | solution.py:40
  23.9 1.6 %collective-permute-start.10 = (f32[5,64,128]{2,1,0:T(8,128)S(1)}, f32[5,64,128]{2,1,0:T(8,128)S(1)}, u32[]{:S(2)}, u32[]{:S(2)}) collective-permute-start(f32[5,64,128]{2,1,0:T(8,128)S(1)} %get-tuple-element.55), channel_id=1, source_target_pairs={{0,8},{4,12},{8,0},{12,4},{16,24},{20,28},{24,16},{28,20},{1,9},{5... | collective-permute-start | bytes 491528 | tf_op jit(solution)/shard_map/ppermute | solution.py:40
  25.5 0.4 collective-permute-start.11
  25.8 1.5 %shard_map.64 = f32[2,128,128]{2,1,0:T(8,128)S(1)} custom-call(s32[4]{0:T(128)S(1)} %pad_add_fusion.meta.refs_0_, f32[2,4,2,128,128]{4,3,2,1,0:T(8,128)S(1)} %get-tuple-element.48.merged), custom_call_target="tpu_custom_call" | custom-call | bytes 3000000 | tf_op jit(solution)/shard_map/pallas_call | solution.py:24
  27.3 0.0 collective-permute-done.6.first
  27.3 1.7 %collective-permute-start.7 = (f32[2,128,128]{2,1,0:T(8,128)S(1)}, f32[2,128,128]{2,1,0:T(8,128)S(1)}, u32[]{:S(2)}, u32[]{:S(2)}) collective-permute-start(f32[2,128,128]{2,1,0:T(8,128)S(1)} %shard_map.64), channel_id=1, source_target_pairs={{0,16},{8,24},{16,0},{24,8},{1,17},{9,25},{17,1},{25,9},{2,18},{10... | collective-permute-start | bytes 393224 | tf_op jit(solution)/shard_map/ppermute | solution.py:48
  29.1 0.0 collective-permute-done.5.second
  29.1 2.8 %shard_map.63 = (f32[4,2,128,256]{3,2,1,0:T(8,128)S(1)}, f32[4,2,128,256]{3,2,1,0:T(8,128)S(1)}, f32[4,2,128,256]{3,2,1,0:T(8,128)S(1)}, f32[128,128]{1,0:T(8,128)S(1)}) custom-call(s32[4]{0:T(128)S(1)} %pad_add_fusion.meta.refs_0_, f32[2,4,2,128,128]{4,3,2,1,0:T(8,128)S(1)} %get-tuple-element.48.merged, ...), custom_call_target="tpu_custom_call" | custom-call | bytes 30000000 | tf_op jit(solution)/shard_map/pallas_call | solution.py:24
  31.9 0.7 %collective-permute-start.8 = (f32[128,128]{1,0:T(8,128)S(1)}, f32[128,128]{1,0:T(8,128)S(1)}, u32[]{:S(2)}, u32[]{:S(2)}) collective-permute-start(f32[128,128]{1,0:T(8,128)S(1)} %get-tuple-element.52), channel_id=1, source_target_pairs={{0,16},{8,24},{16,0},{24,8},{1,17},{9,25},{17,1},{25,9},{2,18},{10... | collective-permute-start | bytes 196616 | tf_op jit(solution)/shard_map/ppermute | solution.py:48
  32.6 0.0 collective-permute-done.9.refs_1_
  32.6 1.2 %collective-permute-done.10.refs_2_ = f32[5,64,128]{2,1,0:T(8,128)S(1)} collective-permute-done((f32[5,64,128]{2,1,0:T(8,128)S(1)}, f32[5,64,128]{2,1,0:T(8,128)S(1)}, u32[]{:S(2)}, u32[]{:S(2)}) %collective-permute-start.10) | collective-permute-done | bytes 163872 | tf_op jit(solution)/shard_map/ppermute | solution.py:40
  33.8 2.2 %collective-permute-done.11.refs_3_ = f32[5,64,128]{2,1,0:T(8,128)S(1)} collective-permute-done((f32[5,64,128]{2,1,0:T(8,128)S(1)}, f32[5,64,128]{2,1,0:T(8,128)S(1)}, u32[]{:S(2)}, u32[]{:S(2)}) %collective-permute-start.11) | collective-permute-done | bytes 163872 | tf_op jit(solution)/shard_map/ppermute | solution.py:40
  36.0 0.8 %shard_map.65.observed = f32[4,2,128,256]{3,2,1,0:T(8,128)S(1)} custom-call(s32[4]{0:T(128)S(1)} %pad_add_fusion.meta.refs_0_, f32[5,64,128]{2,1,0:T(8,128)S(1)} %get-tuple-element.53.refs_0_, f32[5,64,128]{2,1,0:T(8,128)S(1)} %collective-permute-done.9.refs_1_, f32[5,64,128]{2,1,0:T(8,128)S(1)} %collective-permute-done.10.refs_2_, ...), custom_call_target="tpu_custom_call" | custom-call | bytes 100000000 | tf_op jit(solution)/shard_map/pallas_call | solution.py:24
  36.8 0.0 collective-permute-done.7.centre
  36.9 3.7 %collective-permute-done.8.sides = f32[128,128]{1,0:T(8,128)S(1)} collective-permute-done((f32[128,128]{1,0:T(8,128)S(1)}, f32[128,128]{1,0:T(8,128)S(1)}, u32[]{:S(2)}, u32[]{:S(2)}) %collective-permute-start.8) | collective-permute-done | bytes 65568 | tf_op jit(solution)/shard_map/ppermute | solution.py:48
  40.5 0.7 %shard_map.66 = (f32[4,2,128,256]{3,2,1,0:T(8,128)S(1)}, f32[4,2,128,256]{3,2,1,0:T(8,128)S(1)}, f32[4,2,128,256]{3,2,1,0:T(8,128)S(1)}, f32[288,128]{1,0:T(8,128)S(1)}) custom-call(s32[4]{0:T(128)S(1)} %pad_add_fusion.meta.refs_0_, f32[4,2,128,256]{3,2,1,0:T(8,128)S(1)} %get-tuple-element.50.drive, ...), custom_call_target="tpu_custom_call" | custom-call | bytes 3000000 | tf_op jit(solution)/shard_map/pallas_call | solution.py:24
  41.3 3.1 %collective-permute-start.15 = (f32[288,128]{1,0:T(8,128)S(1)}, f32[288,128]{1,0:T(8,128)S(1)}, u32[]{:S(2)}, u32[]{:S(2)}) collective-permute-start(f32[288,128]{1,0:T(8,128)S(1)} %get-tuple-element.59.refs_2_), channel_id=1, source_target_pairs={{0,16},{8,24},{16,0},{24,8},{1,17},{9,25},{17,1},{25,9},{2,18},{10... | collective-permute-start | bytes 442376 | tf_op jit(solution)/shard_map/ppermute | solution.py:48
  44.3 0.6 shard_map.67
  44.9 1.0 %collective-permute-start.12 = (f32[2,2,64,128]{3,2,1,0:T(8,128)S(1)}, f32[2,2,64,128]{3,2,1,0:T(8,128)S(1)}, u32[]{:S(2)}, u32[]{:S(2)}) collective-permute-start(f32[2,2,64,128]{3,2,1,0:T(8,128)S(1)} %get-tuple-element.61), channel_id=1, source_target_pairs={{0,4},{4,0},{8,12},{12,8},{16,20},{20,16},{24,28},{28,24},{1,5},{5... | collective-permute-start | bytes 393224 | tf_op jit(solution)/shard_map/ppermute | solution.py:40
  45.9 2.6 %collective-permute-start.13 = (f32[2,2,64,128]{3,2,1,0:T(8,128)S(1)}, f32[2,2,64,128]{3,2,1,0:T(8,128)S(1)}, u32[]{:S(2)}, u32[]{:S(2)}) collective-permute-start(f32[2,2,64,128]{3,2,1,0:T(8,128)S(1)} %get-tuple-element.62), channel_id=1, source_target_pairs={{0,8},{4,12},{8,0},{12,4},{16,24},{20,28},{24,16},{28,20},{1,9},{5... | collective-permute-start | bytes 393224 | tf_op jit(solution)/shard_map/ppermute | solution.py:40
  48.5 0.7 %collective-permute-start.14 = (f32[2,2,64,128]{3,2,1,0:T(8,128)S(1)}, f32[2,2,64,128]{3,2,1,0:T(8,128)S(1)}, u32[]{:S(2)}, u32[]{:S(2)}) collective-permute-start(f32[2,2,64,128]{3,2,1,0:T(8,128)S(1)} %get-tuple-element.63), channel_id=1, source_target_pairs={{0,12},{4,8},{8,4},{12,0},{16,28},{20,24},{24,20},{28,16},{1,13},{... | collective-permute-start | bytes 393224 | tf_op jit(solution)/shard_map/ppermute | solution.py:40
  49.1 2.0 %collective-permute-done.15.refs_3_ = f32[288,128]{1,0:T(8,128)S(1)} collective-permute-done((f32[288,128]{1,0:T(8,128)S(1)}, f32[288,128]{1,0:T(8,128)S(1)}, u32[]{:S(2)}, u32[]{:S(2)}) %collective-permute-start.15) | collective-permute-done | bytes 147488 | tf_op jit(solution)/shard_map/ppermute | solution.py:48
  51.1 2.4 %shard_map.69 = (f32[2,64,128]{2,1,0:T(8,128)S(1)}, f32[2,64,128]{2,1,0:T(8,128)S(1)}, f32[2,64,128]{2,1,0:T(8,128)S(1)}, f32[2,64,128]{2,1,0:T(8,128)S(1)}) custom-call(s32[4]{0:T(128)S(1)} %pad_add_fusion.meta.refs_0_, f32[4,2,128,256]{3,2,1,0:T(8,128)S(1)} %get-tuple-element.64.refs_1_, f32[4,2,128,256]{3,2,1,0:T(8,128)S(1)} %get-tuple-element.51.inverse.refs_2_, ...), custom_call_target="tpu_custom_call" | custom-call | bytes 3000000 | tf_op jit(solution)/shard_map/pallas_call | solution.py:24
  53.5 1.5 %collective-permute-start.16 = (f32[2,64,128]{2,1,0:T(8,128)S(1)}, f32[2,64,128]{2,1,0:T(8,128)S(1)}, u32[]{:S(2)}, u32[]{:S(2)}) collective-permute-start(f32[2,64,128]{2,1,0:T(8,128)S(1)} %get-tuple-element.67), channel_id=1, source_target_pairs={{0,4},{4,0},{8,12},{12,8},{16,20},{20,16},{24,28},{28,24},{1,5},{5... | collective-permute-start | bytes 196616 | tf_op jit(solution)/shard_map/ppermute | solution.py:40
  55.0 0.7 %collective-permute-start.17 = (f32[2,64,128]{2,1,0:T(8,128)S(1)}, f32[2,64,128]{2,1,0:T(8,128)S(1)}, u32[]{:S(2)}, u32[]{:S(2)}) collective-permute-start(f32[2,64,128]{2,1,0:T(8,128)S(1)} %get-tuple-element.68), channel_id=1, source_target_pairs={{0,8},{4,12},{8,0},{12,4},{16,24},{20,28},{24,16},{28,20},{1,9},{5... | collective-permute-start | bytes 196616 | tf_op jit(solution)/shard_map/ppermute | solution.py:40
  55.7 0.0 collective-permute-done.12.refs_1_
  55.7 1.4 %collective-permute-start.18 = (f32[2,64,128]{2,1,0:T(8,128)S(1)}, f32[2,64,128]{2,1,0:T(8,128)S(1)}, u32[]{:S(2)}, u32[]{:S(2)}) collective-permute-start(f32[2,64,128]{2,1,0:T(8,128)S(1)} %get-tuple-element.69), channel_id=1, source_target_pairs={{0,12},{4,8},{8,4},{12,0},{16,28},{20,24},{24,20},{28,16},{1,13},{... | collective-permute-start | bytes 196616 | tf_op jit(solution)/shard_map/ppermute | solution.py:40
  57.1 0.0 collective-permute-done.13.refs_2_
  57.1 0.0 collective-permute-done.14.refs_3_
  57.1 1.4 %shard_map.68 = f32[2,2,4,64,128]{4,3,2,1,0:T(8,128)} custom-call(s32[4]{0:T(128)S(1)} %pad_add_fusion.meta.refs_0_, f32[2,2,64,128]{3,2,1,0:T(8,128)S(1)} %get-tuple-element.60.refs_0_, f32[2,2,64,128]{3,2,1,0:T(8,128)S(1)} %collective-permute-done.12.refs_1_, f32[2,2,64,128]{3,2,1,0:T(8,128)S(1)} %collective-permute-done.13.refs_2_, ...), custom_call_target="tpu_custom_call" | custom-call | bytes 3000000 | tf_op jit(solution)/shard_map/pallas_call | solution.py:24
  58.4 0.0 collective-permute-done.16
  58.4 0.8 %collective-permute-done.17 = f32[2,64,128]{2,1,0:T(8,128)S(1)} collective-permute-done((f32[2,64,128]{2,1,0:T(8,128)S(1)}, f32[2,64,128]{2,1,0:T(8,128)S(1)}, u32[]{:S(2)}, u32[]{:S(2)}) %collective-permute-start.17) | collective-permute-done | bytes 65568 | tf_op jit(solution)/shard_map/ppermute | solution.py:40
  59.3 1.6 %collective-permute-done.18 = f32[2,64,128]{2,1,0:T(8,128)S(1)} collective-permute-done((f32[2,64,128]{2,1,0:T(8,128)S(1)}, f32[2,64,128]{2,1,0:T(8,128)S(1)}, u32[]{:S(2)}, u32[]{:S(2)}) %collective-permute-start.18) | collective-permute-done | bytes 65568 | tf_op jit(solution)/shard_map/ppermute | solution.py:40
  60.8 0.6 %add_add_fusion = f32[2,64,128]{2,1,0:T(8,128)} fusion(f32[2,64,128]{2,1,0:T(8,128)S(1)} %collective-permute-done.17, f32[2,64,128]{2,1,0:T(8,128)S(1)} %collective-permute-done.18, f32[2,64,128]{2,1,0:T(8,128)S(1)} %get-tuple-element.66, f32[2,64,128]{2,1,0:T(8,128)S(1)} %collective-permute-done.16), kind=kLoop, calls=%fused_computation.9 | loop fusion | flops 49152 | bytes 327680 | tf_op jit(solution)/shard_map/add | solution.py:547
  (2 shorter events, 0.1 us)
Async XLA Ops:
  0.6 0.8 %copy-start.2 = (f32[2,64,128]{2,1,0:T(8,128)S(1)}, f32[2,64,128]{2,1,0:T(8,128)}, u32[]{:S(2)}) copy-start(f32[2,64,128]{2,1,0:T(8,128)} %param.7) | copy-start | bytes 196612
  0.6 1.7 %copy-start.1 = (f32[2,2,4,64,128]{4,3,2,1,0:T(8,128)S(1)}, f32[2,2,4,64,128]{4,3,2,1,0:T(8,128)}, u32[]{:S(2)}) copy-start(f32[2,2,4,64,128]{4,3,2,1,0:T(8,128)} %param.4) | copy-start | bytes 1572868
  2.4 4.8 %copy-start = (f32[2,2,4,64,128]{4,3,2,1,0:T(8,128)S(1)}, f32[2,2,4,64,128]{4,3,2,1,0:T(8,128)}, u32[]{:S(2)}) copy-start(f32[2,2,4,64,128]{4,3,2,1,0:T(8,128)} %observed.1) | copy-start | bytes 1572868
  2.6 10.6 %collective-permute-start = (f32[2,2,2,64,128]{4,3,2,1,0:T(8,128)S(1)}, f32[2,2,2,64,128]{4,3,2,1,0:T(8,128)S(1)}, u32[]{:S(2)}, u32[]{:S(2)}) collective-permute-start(f32[2,2,2,64,128]{4,3,2,1,0:T(8,128)S(1)} %get-tuple-element.37), channel_id=1, source_target_pairs={{0,4},{4,0},{8,12},{12,8},{16,20},{20,16},{24,28},{28,24},{1,5},{5... | collective-permute-start | bytes 786440 | tf_op jit(solution)/shard_map/ppermute | solution.py:40
  5.6 9.2 %collective-permute-start.1 = (f32[2,2,2,64,128]{4,3,2,1,0:T(8,128)S(1)}, f32[2,2,2,64,128]{4,3,2,1,0:T(8,128)S(1)}, u32[]{:S(2)}, u32[]{:S(2)}) collective-permute-start(f32[2,2,2,64,128]{4,3,2,1,0:T(8,128)S(1)} %get-tuple-element.38), channel_id=1, source_target_pairs={{0,8},{4,12},{8,0},{12,4},{16,24},{20,28},{24,16},{28,20},{1,9},{5... | collective-permute-start | bytes 786440 | tf_op jit(solution)/shard_map/ppermute | solution.py:40
  7.2 11.6 %collective-permute-start.2 = (f32[2,2,2,64,128]{4,3,2,1,0:T(8,128)S(1)}, f32[2,2,2,64,128]{4,3,2,1,0:T(8,128)S(1)}, u32[]{:S(2)}, u32[]{:S(2)}) collective-permute-start(f32[2,2,2,64,128]{4,3,2,1,0:T(8,128)S(1)} %get-tuple-element.39), channel_id=1, source_target_pairs={{0,12},{4,8},{8,4},{12,0},{16,28},{20,24},{24,20},{28,16},{1,13},{... | collective-permute-start | bytes 786440 | tf_op jit(solution)/shard_map/ppermute | solution.py:40
  8.1 2.1 %collective-permute-start.3 = (f32[2,64,128]{2,1,0:T(8,128)S(1)}, f32[2,64,128]{2,1,0:T(8,128)S(1)}, u32[]{:S(2)}, u32[]{:S(2)}) collective-permute-start(f32[2,64,128]{2,1,0:T(8,128)S(1)} %get-tuple-element.41), channel_id=1, source_target_pairs={{0,1},{1,0},{2,3},{3,2},{4,5},{5,4},{6,7},{7,6},{8,9},{9,8},{10,11... | collective-permute-start | bytes 196616 | tf_op jit(solution)/shard_map/ppermute | solution.py:66
  8.2 4.3 %collective-permute-start.4 = (f32[2,64,128]{2,1,0:T(8,128)S(1)}, f32[2,64,128]{2,1,0:T(8,128)S(1)}, u32[]{:S(2)}, u32[]{:S(2)}) collective-permute-start(f32[2,64,128]{2,1,0:T(8,128)S(1)} %get-tuple-element.42), channel_id=1, source_target_pairs={{1,2},{2,1},{0,3},{3,0},{5,6},{6,5},{4,7},{7,4},{9,10},{10,9},{8,1... | collective-permute-start | bytes 196616 | tf_op jit(solution)/shard_map/ppermute | solution.py:65
  20.5 6.8 %collective-permute-start.6 = (f32[2,2,128,128]{3,2,1,0:T(8,128)S(1)}, f32[2,2,128,128]{3,2,1,0:T(8,128)S(1)}, u32[]{:S(2)}, u32[]{:S(2)}) collective-permute-start(f32[2,2,128,128]{3,2,1,0:T(8,128)S(1)} %get-tuple-element.49), channel_id=1, source_target_pairs={{0,1},{1,0},{2,3},{3,2},{4,5},{5,4},{6,7},{7,6},{8,9},{9,8},{10,11... | collective-permute-start | bytes 786440 | tf_op jit(solution)/shard_map/ppermute | solution.py:66
  20.6 8.5 %collective-permute-start.5 = (f32[2,2,128,128]{3,2,1,0:T(8,128)S(1)}, f32[2,2,128,128]{3,2,1,0:T(8,128)S(1)}, u32[]{:S(2)}, u32[]{:S(2)}) collective-permute-start(f32[2,2,128,128]{3,2,1,0:T(8,128)S(1)} %shard_map.61.refs_4_), channel_id=1, source_target_pairs={{1,2},{2,1},{0,3},{3,0},{5,6},{6,5},{4,7},{7,4},{9,10},{10,9},{8,1... | collective-permute-start | bytes 786440 | tf_op jit(solution)/shard_map/ppermute | solution.py:65
  22.4 10.2 %collective-permute-start.9 = (f32[5,64,128]{2,1,0:T(8,128)S(1)}, f32[5,64,128]{2,1,0:T(8,128)S(1)}, u32[]{:S(2)}, u32[]{:S(2)}) collective-permute-start(f32[5,64,128]{2,1,0:T(8,128)S(1)} %get-tuple-element.54), channel_id=1, source_target_pairs={{0,4},{4,0},{8,12},{12,8},{16,20},{20,16},{24,28},{28,24},{1,5},{5... | collective-permute-start | bytes 491528 | tf_op jit(solution)/shard_map/ppermute | solution.py:40
  23.9 9.9 %collective-permute-start.10 = (f32[5,64,128]{2,1,0:T(8,128)S(1)}, f32[5,64,128]{2,1,0:T(8,128)S(1)}, u32[]{:S(2)}, u32[]{:S(2)}) collective-permute-start(f32[5,64,128]{2,1,0:T(8,128)S(1)} %get-tuple-element.55), channel_id=1, source_target_pairs={{0,8},{4,12},{8,0},{12,4},{16,24},{20,28},{24,16},{28,20},{1,9},{5... | collective-permute-start | bytes 491528 | tf_op jit(solution)/shard_map/ppermute | solution.py:40
  25.5 10.6 %collective-permute-start.11 = (f32[5,64,128]{2,1,0:T(8,128)S(1)}, f32[5,64,128]{2,1,0:T(8,128)S(1)}, u32[]{:S(2)}, u32[]{:S(2)}) collective-permute-start(f32[5,64,128]{2,1,0:T(8,128)S(1)} %get-tuple-element.56), channel_id=1, source_target_pairs={{0,12},{4,8},{8,4},{12,0},{16,28},{20,24},{24,20},{28,16},{1,13},{... | collective-permute-start | bytes 491528 | tf_op jit(solution)/shard_map/ppermute | solution.py:40
  27.3 9.5 %collective-permute-start.7 = (f32[2,128,128]{2,1,0:T(8,128)S(1)}, f32[2,128,128]{2,1,0:T(8,128)S(1)}, u32[]{:S(2)}, u32[]{:S(2)}) collective-permute-start(f32[2,128,128]{2,1,0:T(8,128)S(1)} %shard_map.64), channel_id=1, source_target_pairs={{0,16},{8,24},{16,0},{24,8},{1,17},{9,25},{17,1},{25,9},{2,18},{10... | collective-permute-start | bytes 393224 | tf_op jit(solution)/shard_map/ppermute | solution.py:48
  31.9 8.7 %collective-permute-start.8 = (f32[128,128]{1,0:T(8,128)S(1)}, f32[128,128]{1,0:T(8,128)S(1)}, u32[]{:S(2)}, u32[]{:S(2)}) collective-permute-start(f32[128,128]{1,0:T(8,128)S(1)} %get-tuple-element.52), channel_id=1, source_target_pairs={{0,16},{8,24},{16,0},{24,8},{1,17},{9,25},{17,1},{25,9},{2,18},{10... | collective-permute-start | bytes 196616 | tf_op jit(solution)/shard_map/ppermute | solution.py:48
  41.3 9.8 %collective-permute-start.15 = (f32[288,128]{1,0:T(8,128)S(1)}, f32[288,128]{1,0:T(8,128)S(1)}, u32[]{:S(2)}, u32[]{:S(2)}) collective-permute-start(f32[288,128]{1,0:T(8,128)S(1)} %get-tuple-element.59.refs_2_), channel_id=1, source_target_pairs={{0,16},{8,24},{16,0},{24,8},{1,17},{9,25},{17,1},{25,9},{2,18},{10... | collective-permute-start | bytes 442376 | tf_op jit(solution)/shard_map/ppermute | solution.py:48
  44.9 10.7 %collective-permute-start.12 = (f32[2,2,64,128]{3,2,1,0:T(8,128)S(1)}, f32[2,2,64,128]{3,2,1,0:T(8,128)S(1)}, u32[]{:S(2)}, u32[]{:S(2)}) collective-permute-start(f32[2,2,64,128]{3,2,1,0:T(8,128)S(1)} %get-tuple-element.61), channel_id=1, source_target_pairs={{0,4},{4,0},{8,12},{12,8},{16,20},{20,16},{24,28},{28,24},{1,5},{5... | collective-permute-start | bytes 393224 | tf_op jit(solution)/shard_map/ppermute | solution.py:40
  45.9 11.2 %collective-permute-start.13 = (f32[2,2,64,128]{3,2,1,0:T(8,128)S(1)}, f32[2,2,64,128]{3,2,1,0:T(8,128)S(1)}, u32[]{:S(2)}, u32[]{:S(2)}) collective-permute-start(f32[2,2,64,128]{3,2,1,0:T(8,128)S(1)} %get-tuple-element.62), channel_id=1, source_target_pairs={{0,8},{4,12},{8,0},{12,4},{16,24},{20,28},{24,16},{28,20},{1,9},{5... | collective-permute-start | bytes 393224 | tf_op jit(solution)/shard_map/ppermute | solution.py:40
  48.5 8.6 %collective-permute-start.14 = (f32[2,2,64,128]{3,2,1,0:T(8,128)S(1)}, f32[2,2,64,128]{3,2,1,0:T(8,128)S(1)}, u32[]{:S(2)}, u32[]{:S(2)}) collective-permute-start(f32[2,2,64,128]{3,2,1,0:T(8,128)S(1)} %get-tuple-element.63), channel_id=1, source_target_pairs={{0,12},{4,8},{8,4},{12,0},{16,28},{20,24},{24,20},{28,16},{1,13},{... | collective-permute-start | bytes 393224 | tf_op jit(solution)/shard_map/ppermute | solution.py:40
  53.5 4.9 %collective-permute-start.16 = (f32[2,64,128]{2,1,0:T(8,128)S(1)}, f32[2,64,128]{2,1,0:T(8,128)S(1)}, u32[]{:S(2)}, u32[]{:S(2)}) collective-permute-start(f32[2,64,128]{2,1,0:T(8,128)S(1)} %get-tuple-element.67), channel_id=1, source_target_pairs={{0,4},{4,0},{8,12},{12,8},{16,20},{20,16},{24,28},{28,24},{1,5},{5... | collective-permute-start | bytes 196616 | tf_op jit(solution)/shard_map/ppermute | solution.py:40
  55.0 4.3 %collective-permute-start.17 = (f32[2,64,128]{2,1,0:T(8,128)S(1)}, f32[2,64,128]{2,1,0:T(8,128)S(1)}, u32[]{:S(2)}, u32[]{:S(2)}) collective-permute-start(f32[2,64,128]{2,1,0:T(8,128)S(1)} %get-tuple-element.68), channel_id=1, source_target_pairs={{0,8},{4,12},{8,0},{12,4},{16,24},{20,28},{24,16},{28,20},{1,9},{5... | collective-permute-start | bytes 196616 | tf_op jit(solution)/shard_map/ppermute | solution.py:40
  55.7 5.2 %collective-permute-start.18 = (f32[2,64,128]{2,1,0:T(8,128)S(1)}, f32[2,64,128]{2,1,0:T(8,128)S(1)}, u32[]{:S(2)}, u32[]{:S(2)}) collective-permute-start(f32[2,64,128]{2,1,0:T(8,128)S(1)} %get-tuple-element.69), channel_id=1, source_target_pairs={{0,12},{4,8},{8,4},{12,0},{16,28},{20,24},{24,20},{28,16},{1,13},{... | collective-permute-start | bytes 196616 | tf_op jit(solution)/shard_map/ppermute | solution.py:40

commit v4 on v3

--- a/solution.py
+++ b/solution.py
@@ -20,17 +20,22 @@
     return lax.broadcasted_iota(jnp.int32, shape, len(shape) - 1)
 
 
-def call(kernel, outs, meta, *operands, scratch=(), cost=3_000_000):
+def position():
+    zi, xi, yi = (lax.axis_index(a) for a in ("depth", "gx", "gy"))
+    outermost = (yi == 0) | (yi == lax.axis_size("gy") - 1)
+    return 2 * (zi % 2) + xi % 2, yi % 2, zi // 2, outermost
+
+
+def call(kernel, outs, *operands, scratch=(), cost=3_000_000):
     return pl.pallas_call(
-        kernel,
+        lambda *refs: kernel(position(), *refs),
         out_shape=[jax.ShapeDtypeStruct(shape, F32) for shape in outs],
-        in_specs=[pl.BlockSpec(memory_space=pltpu.SMEM)]
-        + [pl.BlockSpec(memory_space=VMEM)] * len(operands),
+        in_specs=[pl.BlockSpec(memory_space=VMEM)] * len(operands),
         out_specs=[pl.BlockSpec(memory_space=VMEM)] * len(outs),
         scratch_shapes=list(scratch),
         cost_estimate=pl.CostEstimate(flops=0, bytes_accessed=cost, transcendentals=0),
         compiler_params=pltpu.CompilerParams(vmem_limit_bytes=8 * 1024 * 1024),
-    )(meta, *operands)
+    )(*operands)
 
 
 def member_swap(block, offset):
@@ -119,13 +124,6 @@
             )
 
 
-def unpack_edges(meta, first, second, j, width):
-    even = meta[1] == 0
-    right, left = jnp.where(even, first, second), jnp.where(even, second, first)
-    at = j * width
-    return beside_tile(right, (LANES - at) % LANES, left, (LANES - width - at) % LANES, width)
-
-
 def beside_tile(right, right_turn, left, left_turn, width):
     lanes = lane_ids(right.shape)
     right = pltpu.roll(right, right_turn, 1) if right_turn else right
@@ -203,7 +201,16 @@
     return a * q_real + b * q_imag, b * q_real - a * q_imag
 
 
+def beside_each_other(refs):
+    def read(z, c, strip):
+        parts = [ref[z, c, strip, :] for ref in refs]
+        return parts[0] if len(parts) == 1 else jnp.concatenate(parts, axis=1)
+
+    return read
+
+
 def sweep(drive, inverse, out, carry, work, planes, rows, reverse):
+    drive, inverse = beside_each_other(drive), beside_each_other(inverse)
     rhs, ping, pong = work
     sign = -1 if reverse else 1
     width = out.shape[-1]
@@ -225,25 +232,25 @@
         z = planes - 1 - step if reverse else step
         for r in range(0, rows, 8):
             strip = slice(r, r + 8)
-            a = drive[z, 0, strip, :] + 2.5 * carry[0, strip, :]
-            b = drive[z, 1, strip, :] + 2.5 * carry[1, strip, :]
+            a = drive(z, 0, strip) + 2.5 * carry[0, strip, :]
+            b = drive(z, 1, strip) + 2.5 * carry[1, strip, :]
             rhs[0, strip, :] = a
             rhs[1, strip, :] = b
-            a, b = times(a, b, inverse[z, 0, strip, :], inverse[z, 1, strip, :], sign)
+            a, b = times(a, b, inverse(z, 0, strip), inverse(z, 1, strip), sign)
             ping[0, r + 8 : r + 16, :] = a
             ping[1, r + 8 : r + 16, :] = b
         for r in range(0, rows, 8):
             strip = slice(r, r + 8)
             a = rhs[0, strip, :] + beside(ping, 0, r)
             b = rhs[1, strip, :] + beside(ping, 1, r)
-            a, b = times(a, b, inverse[z, 0, strip, :], inverse[z, 1, strip, :], sign)
+            a, b = times(a, b, inverse(z, 0, strip), inverse(z, 1, strip), sign)
             pong[0, r + 8 : r + 16, :] = a
             pong[1, r + 8 : r + 16, :] = b
         for r in range(0, rows, 8):
             strip = slice(r, r + 8)
             a = rhs[0, strip, :] + beside(pong, 0, r)
             b = rhs[1, strip, :] + beside(pong, 1, r)
-            a, b = times(a, b, inverse[z, 0, strip, :], inverse[z, 1, strip, :], sign)
+            a, b = times(a, b, inverse(z, 0, strip), inverse(z, 1, strip), sign)
             out[z, 0, strip, :] = a
             out[z, 1, strip, :] = b
             carry[0, strip, :] = a
@@ -345,24 +352,30 @@
     @pl.when(meta[2] == 0)
     def _():
         carry[...] = jnp.zeros_like(carry)
-        sweep(merged.at[0], merged.at[1], field, carry, work, planes, rows, False)
+        sweep([merged.at[0]], [merged.at[1]], field, carry, work, planes, rows, False)
         send[...] = carry[...]
 
 
-def forward_kernel(meta, merged, second, first, drive, inverse, field, send, carry, *work):
+def forward_kernel(meta, merged, second, first, sides, field, send, carry, *work):
     planes, rows = merged.shape[1], merged.shape[3]
-    alone = meta[3] == 1
-    for f, out in enumerate((drive, inverse)):
-        for p in range(planes):
-            for c in range(2):
-                two = second[f, c]
+    even, alone = meta[1] == 0, meta[3]
+    for f in range(2):
+        for c in range(2):
+            for r in range(0, rows, 32):
+                strip = slice(r, r + 32)
+                one, two = first[f, c, strip, :], second[f, c, strip, :]
                 two = jnp.where(alone, 0.0, two) if f else two
-                out[p, c, :, :LANES] = merged[f, p, c]
-                out[p, c, :, LANES:] = unpack_edges(meta, first[f, c], two, p, WIDE)
+                right, left = jnp.where(even, one, two), jnp.where(even, two, one)
+                for p in range(planes):
+                    at = p * WIDE
+                    sides[f, p, c, strip, :] = beside_tile(
+                        right, (LANES - at) % LANES, left, (2 * LANES - WIDE - at) % LANES, WIDE
+                    )
 
     @pl.when(meta[2] == 0)
     def _():
         carry[...] = jnp.zeros_like(carry)
+        drive, inverse = ([merged.at[f], sides.at[f]] for f in range(2))
         sweep(drive, inverse, field, carry, work, planes, rows, False)
         pack_sides(field, planes - 1, send)
 
@@ -381,8 +394,8 @@
 
 def turn_kernel(
     meta,
-    drive,
-    inverse,
+    merged,
+    beside,
     centre,
     sides,
     observed,
@@ -394,7 +407,8 @@
     carry,
     *work,
 ):
-    planes, rows = drive.shape[0], drive.shape[2]
+    planes, rows = merged.shape[1], merged.shape[3]
+    drive, inverse = ([merged.at[f], beside.at[f]] for f in range(2))
     lower = meta[2] == 1
 
     @pl.when(jnp.logical_not(lower))
@@ -411,15 +425,16 @@
     @pl.when(lower)
     def _():
         carry[...] = jnp.zeros_like(carry)
-        sweep(residual, inverse, adjoint, carry, work, planes, rows, True)
+        sweep([residual], inverse, adjoint, carry, work, planes, rows, True)
         pack_carry(adjoint, 0, send)
 
 
-def adjoint_kernel(height, meta, residual, inverse, got, field, lower_adjoint, *rest):
+def adjoint_kernel(height, meta, residual, merged, beside, got, field, lower_adjoint, *rest):
     pieces, (adjoint, carry, *work) = rest[:MEMBERS], rest[MEMBERS:]
     planes, rows = residual.shape[0], residual.shape[2]
     margin = (rows - 2 * height) // 2
     upper = meta[2] == 0
+    inverse = [merged.at[1], beside.at[1]]
 
     def products(adjoint):
         for k, piece in enumerate(pieces):
@@ -438,7 +453,7 @@
     @pl.when(upper)
     def _():
         unpack_carry(got, carry)
-        sweep(residual, inverse, adjoint, carry, work, planes, rows, True)
+        sweep([residual], inverse, adjoint, carry, work, planes, rows, True)
         products(adjoint)
 
     @pl.when(jnp.logical_not(upper))
@@ -454,9 +469,7 @@
 
 def body(source, observed, wavenumber, damping):
     own_planes, _, shots, height, width = source.shape
-    zi, xi, yi = (lax.axis_index(a) for a in ("depth", "gx", "gy"))
-    outermost = (yi == 0) | (yi == lax.axis_size("gy") - 1)
-    meta = jnp.stack([2 * (zi % 2) + xi % 2, yi % 2, zi // 2, outermost]).astype(jnp.int32)
+    member = position()[0]
     planes, high = 2 * own_planes, 2 * height
     one_group = lax.axis_size("gx") == 2
     rows = high if one_group else high + 2 * WIDE
@@ -464,26 +477,25 @@
 
     inverse = inverses(wavenumber, damping)
     sends = [
-        jnp.stack([lax.dynamic_index_in_dim(source, meta[0] ^ k, 2, keepdims=False), inverse])
+        jnp.stack([lax.dynamic_index_in_dim(source, member ^ k, 2, keepdims=False), inverse])
         for k in range(MEMBERS)
     ]
     observed, *sends = lax.optimization_barrier([observed, *sends])
     pieces = gathered(sends)
-    seen_edges = call(observed_edges_kernel, [(2, height, width)] * 2, meta, observed)
+    seen_edges = call(observed_edges_kernel, [(2, height, width)] * 2, observed)
     seen_edges = neighbour_swaps(*seen_edges, "gy", 1, ring=True)
     first_seen, *seen_sends = call(
         observed_sends_kernel,
         [(2 * own_planes + 1, height, width)] * MEMBERS,
-        meta,
         observed,
         *seen_edges,
     )
     *pieces, first_seen = lax.optimization_barrier([*pieces, first_seen])
     seen_sends = [first_seen, *seen_sends]
     edge_shape = (2, 2, high, width)
-    (second,) = call(second_edges_kernel, [edge_shape], meta, *pieces)
+    (second,) = call(second_edges_kernel, [edge_shape], *pieces)
     merged, first = call(
-        merge_kernel, [(2, planes, 2, high, width), edge_shape], meta, *pieces, second
+        merge_kernel, [(2, planes, 2, high, width), edge_shape], *pieces, second
     )
     if not one_group:
         merged, first, second = (with_row_halo(a, WIDE) for a in (merged, first, second))
@@ -493,7 +505,6 @@
     (centre,) = call(
         centre_kernel,
         [(2, rows, width)],
-        meta,
         merged,
         scratch=[VMEM((planes, 2, rows, width), F32), *sweep_scratch(rows, width)],
     )
@@ -501,10 +512,9 @@
 
     whole = (planes, 2, rows, 2 * width)
     scratch = sweep_scratch(rows)
-    drive, inverse, field, send = call(
+    beside, field, send = call(
         forward_kernel,
-        [whole, whole, whole, (rows, width)],
-        meta,
+        [(2, planes, 2, rows, width), whole, (rows, width)],
         merged,
         second,
         first,
@@ -513,15 +523,14 @@
     )
     got = depth_pair_swap(send)
     (seen,) = call(
-        merge_observed_kernel, [(planes, 2, high, 2 * width)], meta, *seen, cost=100_000_000
+        merge_observed_kernel, [(planes, 2, high, 2 * width)], *seen, cost=100_000_000
     )
     seen = seen if one_group else with_row_halo(seen, WIDE)
     field, residual, adjoint, send = call(
         turn_kernel,
         [whole, whole, whole, (2 * rows + rows // 4, width)],
-        meta,
-        drive,
-        inverse,
+        merged,
+        beside,
         centre,
         got,
         seen,
@@ -530,14 +539,14 @@
     )
     got = depth_pair_swap(send)
     pieces = gathered(
-        call(lambda *refs: cut_kernel(height, *refs), [tile] * MEMBERS, meta, field, send)
+        call(lambda *refs: cut_kernel(height, *refs), [tile] * MEMBERS, field, send)
     )
     sums = call(
         lambda *refs: adjoint_kernel(height, *refs),
         [(own_planes, height, width)] * MEMBERS,
-        meta,
         residual,
-        inverse,
+        merged,
+        beside,
         got,
         field,
         adjoint,
@@ -545,7 +554,7 @@
     )
     sums = gathered(sums)
     gradient = (sums[0] + sums[1]) + (sums[2] + sums[3])
-    (forward_field,) = call(field_kernel, [source.shape], meta, *pieces)
+    (forward_field,) = call(field_kernel, [source.shape], *pieces)
     return forward_field, gradient
 
 

time: 61.7 us -> 58.9 us (0.955)
  Pallas kernels: 13.4 us -> 7.2 us
  waiting for transfers between devices: 19.4 us -> 22.8 us
    pallas_call x11, Pallas kernels: 13.4 us -> 7.2 us  [call(): pl.pallas_call(lambda *refs: kernel(position(), *refs), out_shape=[jax.Sh...]
    ppermute x12, waiting for transfers between devices: 11.5 us -> 13.5 us  [member_swap(): return lax.ppermute(block, ('depth', 'gx'), pairs)]
    ppermute x3, waiting for transfers between devices: 5.67 us -> 6.73 us  [depth_pair_swap(): lax.ppermute(block, 'depth', [(z, z ^ 2) for z in range(lax.axis_size('de...]
  transfers between devices with their start and end apart: 19 -> 19, of which waited for: 9 -> 10; matrix products, arithmetic and copies ran while one was open for 0% -> 0% of each run, Pallas kernels for 18% -> 11%
where the time goes in v4:
time: 58.9 us; the launch traced here: 58.8 us
  starting transfers between devices  25.5 us (43%)
  waiting for transfers between devices  22.8 us (39%)
  Pallas kernels  7.2 us (12%)
  other arithmetic  1.63 us (3%)
  between operations  0.85 us (1%)
  local copies, waits for them, and re-layouts  0.84 us (1%)
    ppermute x12, starting transfers between devices, member_swap(): return lax.ppermute(block, ('depth', 'gx'), pairs)  15.6 us
    ppermute x12, waiting for transfers between devices, member_swap(): return lax.ppermute(block, ('depth', 'gx'), pairs)  13.5 us
    pallas_call x11, Pallas kernels, call(): pl.pallas_call(lambda *refs: kernel(position(), *refs), out_shape=[jax.Sh...  7.2 us
    ppermute x3, waiting for transfers between devices, depth_pair_swap(): lax.ppermute(block, 'depth', [(z, z ^ 2) for z in range(lax.axis_size('de...  6.73 us
    ppermute x3, starting transfers between devices, depth_pair_swap(): lax.ppermute(block, 'depth', [(z, z ^ 2) for z in range(lax.axis_size('de...  5.95 us
    ppermute x2, starting transfers between devices, neighbour_swaps(): lax.ppermute(second, axis, pairs(1) + ends)  3.75 us
    ppermute x2, waiting for transfers between devices, neighbour_swaps(): lax.ppermute(second, axis, pairs(1) + ends)  2.52 us
  transfers between devices with their start and end apart: 19, of which 10 were waited for; matrix products, arithmetic and copies ran while one was open for 0% of the time, Pallas kernels for 11%

profile of v4, /device:TPU:0, one launch (start us, length us, event | category | flops | bytes accessed | tf_op | source)
XLA Modules:
  0.0 58.8 jit_solution(14042486149036372466)
XLA Ops:
  0.6 0.0 copy-start.2
  0.6 0.0 copy-start.1
  0.7 0.8 %copy-done.2 = f32[2,64,128]{2,1,0:T(8,128)S(1)} copy-done((f32[2,64,128]{2,1,0:T(8,128)S(1)}, f32[2,64,128]{2,1,0:T(8,128)}, u32[]{:S(2)}) %copy-start.2) | copy-done | bytes 65560
  1.5 0.9 %divide_bitcast_fusion = (f32[2,1,64,128]{3,2,1,0:T(8,128)S(1)}, f32[2,1,64,128]{3,2,1,0:T(8,128)S(1)}) fusion(f32[2,64,128]{2,1,0:T(8,128)S(1)} %copy-done.2, f32[2,64,128]{2,1,0:T(8,128)} %param.6), kind=kLoop, calls=%fused_computation.11 | loop fusion | flops 114688 | bytes 262144 | tf_op jit(solution)/shard_map/stack | solution.py:275
  2.4 0.0 copy-done.1
  2.4 0.0 copy-start
  2.4 0.1 pad_maximum_fusion
  2.6 3.0 %collective-permute-start = (f32[2,2,2,64,128]{4,3,2,1,0:T(8,128)S(1)}, f32[2,2,2,64,128]{4,3,2,1,0:T(8,128)S(1)}, u32[]{:S(2)}, u32[]{:S(2)}) collective-permute-start(f32[2,2,2,64,128]{4,3,2,1,0:T(8,128)S(1)} %get-tuple-element.36), channel_id=1, source_target_pairs={{0,4},{4,0},{8,12},{12,8},{16,20},{20,16},{24,28},{28,24},{1,5},{5... | collective-permute-start | bytes 786440 | tf_op jit(solution)/shard_map/ppermute | solution.py:45
  5.6 1.6 %collective-permute-start.1 = (f32[2,2,2,64,128]{4,3,2,1,0:T(8,128)S(1)}, f32[2,2,2,64,128]{4,3,2,1,0:T(8,128)S(1)}, u32[]{:S(2)}, u32[]{:S(2)}) collective-permute-start(f32[2,2,2,64,128]{4,3,2,1,0:T(8,128)S(1)} %get-tuple-element.37), channel_id=1, source_target_pairs={{0,8},{4,12},{8,0},{12,4},{16,24},{20,28},{24,16},{28,20},{1,9},{5... | collective-permute-start | bytes 786440 | tf_op jit(solution)/shard_map/ppermute | solution.py:45
  7.2 0.0 collective-permute-start.2
  7.2 0.0 copy-done
  7.2 0.3 shard_map.59
  7.5 0.1 collective-permute-start.3
  7.6 2.0 %collective-permute-start.4 = (f32[2,64,128]{2,1,0:T(8,128)S(1)}, f32[2,64,128]{2,1,0:T(8,128)S(1)}, u32[]{:S(2)}, u32[]{:S(2)}) collective-permute-start(f32[2,64,128]{2,1,0:T(8,128)S(1)} %get-tuple-element.41), channel_id=1, source_target_pairs={{1,2},{2,1},{0,3},{3,0},{5,6},{6,5},{4,7},{7,4},{9,10},{10,9},{8,1... | collective-permute-start | bytes 196616 | tf_op jit(solution)/shard_map/ppermute | solution.py:70
  9.6 0.0 collective-permute-done.3.refs_1_
  9.6 2.3 %collective-permute-done.4.refs_2_ = f32[2,64,128]{2,1,0:T(8,128)S(1)} collective-permute-done((f32[2,64,128]{2,1,0:T(8,128)S(1)}, f32[2,64,128]{2,1,0:T(8,128)S(1)}, u32[]{:S(2)}, u32[]{:S(2)}) %collective-permute-start.4) | collective-permute-done | bytes 65568 | tf_op jit(solution)/shard_map/ppermute | solution.py:70
  11.8 0.1 shard_map.60
  12.0 0.0 collective-permute-done.refs_1_
  12.0 2.8 %collective-permute-done.1.refs_2_ = f32[2,2,2,64,128]{4,3,2,1,0:T(8,128)S(1)} collective-permute-done((f32[2,2,2,64,128]{4,3,2,1,0:T(8,128)S(1)}, f32[2,2,2,64,128]{4,3,2,1,0:T(8,128)S(1)}, u32[]{:S(2)}, u32[]{:S(2)}) %collective-permute-start.1) | collective-permute-done | bytes 262176 | tf_op jit(solution)/shard_map/ppermute | solution.py:45
  14.8 3.9 %collective-permute-done.2.refs_3_ = f32[2,2,2,64,128]{4,3,2,1,0:T(8,128)S(1)} collective-permute-done((f32[2,2,2,64,128]{4,3,2,1,0:T(8,128)S(1)}, f32[2,2,2,64,128]{4,3,2,1,0:T(8,128)S(1)}, u32[]{:S(2)}, u32[]{:S(2)}) %collective-permute-start.2) | collective-permute-done | bytes 262176 | tf_op jit(solution)/shard_map/ppermute | solution.py:45
  18.8 0.3 shard_map.61.refs_4_
  19.1 0.4 shard_map.62
  19.4 0.1 collective-permute-start.6
  19.5 1.8 %collective-permute-start.5 = (f32[2,2,128,128]{3,2,1,0:T(8,128)S(1)}, f32[2,2,128,128]{3,2,1,0:T(8,128)S(1)}, u32[]{:S(2)}, u32[]{:S(2)}) collective-permute-start(f32[2,2,128,128]{3,2,1,0:T(8,128)S(1)} %shard_map.61.refs_4_), channel_id=1, source_target_pairs={{1,2},{2,1},{0,3},{3,0},{5,6},{6,5},{4,7},{7,4},{9,10},{10,9},{8,1... | collective-permute-start | bytes 786440 | tf_op jit(solution)/shard_map/ppermute | solution.py:70
  21.3 1.5 %collective-permute-start.9 = (f32[5,64,128]{2,1,0:T(8,128)S(1)}, f32[5,64,128]{2,1,0:T(8,128)S(1)}, u32[]{:S(2)}, u32[]{:S(2)}) collective-permute-start(f32[5,64,128]{2,1,0:T(8,128)S(1)} %get-tuple-element.52), channel_id=1, source_target_pairs={{0,4},{4,0},{8,12},{12,8},{16,20},{20,16},{24,28},{28,24},{1,5},{5... | collective-permute-start | bytes 491528 | tf_op jit(solution)/shard_map/ppermute | solution.py:45
  22.8 1.6 %collective-permute-start.10 = (f32[5,64,128]{2,1,0:T(8,128)S(1)}, f32[5,64,128]{2,1,0:T(8,128)S(1)}, u32[]{:S(2)}, u32[]{:S(2)}) collective-permute-start(f32[5,64,128]{2,1,0:T(8,128)S(1)} %get-tuple-element.53), channel_id=1, source_target_pairs={{0,8},{4,12},{8,0},{12,4},{16,24},{20,28},{24,16},{28,20},{1,9},{5... | collective-permute-start | bytes 491528 | tf_op jit(solution)/shard_map/ppermute | solution.py:45
  24.4 0.4 collective-permute-start.11
  24.8 0.9 %shard_map.64 = f32[2,128,128]{2,1,0:T(8,128)S(1)} custom-call(f32[2,4,2,128,128]{4,3,2,1,0:T(8,128)S(1)} %get-tuple-element.47.refs_0_.refs_1_), custom_call_target="tpu_custom_call" | custom-call | bytes 3000000 | tf_op jit(solution)/shard_map/pallas_call | solution.py:30
  25.7 0.0 collective-permute-done.6.refs_2_
  25.7 1.7 %collective-permute-start.7 = (f32[2,128,128]{2,1,0:T(8,128)S(1)}, f32[2,128,128]{2,1,0:T(8,128)S(1)}, u32[]{:S(2)}, u32[]{:S(2)}) collective-permute-start(f32[2,128,128]{2,1,0:T(8,128)S(1)} %shard_map.64), channel_id=1, source_target_pairs={{0,16},{8,24},{16,0},{24,8},{1,17},{9,25},{17,1},{25,9},{2,18},{10... | collective-permute-start | bytes 393224 | tf_op jit(solution)/shard_map/ppermute | solution.py:53
  27.4 0.3 collective-permute-done.5.refs_1_
  27.6 2.1 %shard_map.63 = (f32[2,4,2,128,128]{4,3,2,1,0:T(8,128)S(1)}, f32[4,2,128,256]{3,2,1,0:T(8,128)S(1)}, f32[128,128]{1,0:T(8,128)S(1)}) custom-call(f32[2,4,2,128,128]{4,3,2,1,0:T(8,128)S(1)} %get-tuple-element.47.refs_0_.refs_1_, f32[2,2,128,128]{3,2,1,0:T(8,128)S(1)} %collective-permute-done.5.refs_1_, f32[2,2,128,128]{3,2,1,0:T(8,128)S(1)} %collective-permute-done.6.refs_2_), custom_call_target="tpu_custom_call" | custom-call | bytes 30000000 | tf_op jit(solution)/shard_map/pallas_call | solution.py:30
  29.8 1.1 %collective-permute-start.8 = (f32[128,128]{1,0:T(8,128)S(1)}, f32[128,128]{1,0:T(8,128)S(1)}, u32[]{:S(2)}, u32[]{:S(2)}) collective-permute-start(f32[128,128]{1,0:T(8,128)S(1)} %get-tuple-element.50), channel_id=1, source_target_pairs={{0,16},{8,24},{16,0},{24,8},{1,17},{9,25},{17,1},{25,9},{2,18},{10... | collective-permute-start | bytes 196616 | tf_op jit(solution)/shard_map/ppermute | solution.py:53
  30.9 0.0 collective-permute-done.9.refs_1_
  30.9 1.8 %collective-permute-done.10.refs_2_ = f32[5,64,128]{2,1,0:T(8,128)S(1)} collective-permute-done((f32[5,64,128]{2,1,0:T(8,128)S(1)}, f32[5,64,128]{2,1,0:T(8,128)S(1)}, u32[]{:S(2)}, u32[]{:S(2)}) %collective-permute-start.10) | collective-permute-done | bytes 163872 | tf_op jit(solution)/shard_map/ppermute | solution.py:45
  32.7 2.2 %collective-permute-done.11.refs_3_ = f32[5,64,128]{2,1,0:T(8,128)S(1)} collective-permute-done((f32[5,64,128]{2,1,0:T(8,128)S(1)}, f32[5,64,128]{2,1,0:T(8,128)S(1)}, u32[]{:S(2)}, u32[]{:S(2)}) %collective-permute-start.11) | collective-permute-done | bytes 163872 | tf_op jit(solution)/shard_map/ppermute | solution.py:45
  34.9 0.3 shard_map.65.refs_4_
  35.2 0.0 collective-permute-done.7.refs_2_
  35.2 3.9 %collective-permute-done.8.refs_3_ = f32[128,128]{1,0:T(8,128)S(1)} collective-permute-done((f32[128,128]{1,0:T(8,128)S(1)}, f32[128,128]{1,0:T(8,128)S(1)}, u32[]{:S(2)}, u32[]{:S(2)}) %collective-permute-start.8) | collective-permute-done | bytes 65568 | tf_op jit(solution)/shard_map/ppermute | solution.py:53
  39.1 0.2 shard_map.66
  39.3 3.1 %collective-permute-start.15 = (f32[288,128]{1,0:T(8,128)S(1)}, f32[288,128]{1,0:T(8,128)S(1)}, u32[]{:S(2)}, u32[]{:S(2)}) collective-permute-start(f32[288,128]{1,0:T(8,128)S(1)} %get-tuple-element.57.refs_1_), channel_id=1, source_target_pairs={{0,16},{8,24},{16,0},{24,8},{1,17},{9,25},{17,1},{25,9},{2,18},{10... | collective-permute-start | bytes 442376 | tf_op jit(solution)/shard_map/ppermute | solution.py:53
  42.5 0.8 %collective-permute-start.12 = (f32[2,2,64,128]{3,2,1,0:T(8,128)S(1)}, f32[2,2,64,128]{3,2,1,0:T(8,128)S(1)}, u32[]{:S(2)}, u32[]{:S(2)}) collective-permute-start(f32[2,2,64,128]{3,2,1,0:T(8,128)S(1)} %get-tuple-element.59), channel_id=1, source_target_pairs={{0,4},{4,0},{8,12},{12,8},{16,20},{20,16},{24,28},{28,24},{1,5},{5... | collective-permute-start | bytes 393224 | tf_op jit(solution)/shard_map/ppermute | solution.py:45
  43.3 2.5 %collective-permute-start.13 = (f32[2,2,64,128]{3,2,1,0:T(8,128)S(1)}, f32[2,2,64,128]{3,2,1,0:T(8,128)S(1)}, u32[]{:S(2)}, u32[]{:S(2)}) collective-permute-start(f32[2,2,64,128]{3,2,1,0:T(8,128)S(1)} %get-tuple-element.60), channel_id=1, source_target_pairs={{0,8},{4,12},{8,0},{12,4},{16,24},{20,28},{24,16},{28,20},{1,9},{5... | collective-permute-start | bytes 393224 | tf_op jit(solution)/shard_map/ppermute | solution.py:45
  45.8 0.6 %collective-permute-start.14 = (f32[2,2,64,128]{3,2,1,0:T(8,128)S(1)}, f32[2,2,64,128]{3,2,1,0:T(8,128)S(1)}, u32[]{:S(2)}, u32[]{:S(2)}) collective-permute-start(f32[2,2,64,128]{3,2,1,0:T(8,128)S(1)} %get-tuple-element.61), channel_id=1, source_target_pairs={{0,12},{4,8},{8,4},{12,0},{16,28},{20,24},{24,20},{28,16},{1,13},{... | collective-permute-start | bytes 393224 | tf_op jit(solution)/shard_map/ppermute | solution.py:45
  46.4 2.8 %collective-permute-done.15.refs_3_ = f32[288,128]{1,0:T(8,128)S(1)} collective-permute-done((f32[288,128]{1,0:T(8,128)S(1)}, f32[288,128]{1,0:T(8,128)S(1)}, u32[]{:S(2)}, u32[]{:S(2)}) %collective-permute-start.15) | collective-permute-done | bytes 147488 | tf_op jit(solution)/shard_map/ppermute | solution.py:53
  49.3 1.7 %shard_map.69 = (f32[2,64,128]{2,1,0:T(8,128)S(1)}, f32[2,64,128]{2,1,0:T(8,128)S(1)}, f32[2,64,128]{2,1,0:T(8,128)S(1)}, f32[2,64,128]{2,1,0:T(8,128)S(1)}) custom-call(f32[4,2,128,256]{3,2,1,0:T(8,128)S(1)} %get-tuple-element.62.refs_0_, f32[2,4,2,128,128]{4,3,2,1,0:T(8,128)S(1)} %get-tuple-element.47.refs_0_.refs_1_, ...), custom_call_target="tpu_custom_call" | custom-call | bytes 3000000 | tf_op jit(solution)/shard_map/pallas_call | solution.py:30
  51.0 1.3 %collective-permute-start.16 = (f32[2,64,128]{2,1,0:T(8,128)S(1)}, f32[2,64,128]{2,1,0:T(8,128)S(1)}, u32[]{:S(2)}, u32[]{:S(2)}) collective-permute-start(f32[2,64,128]{2,1,0:T(8,128)S(1)} %get-tuple-element.65), channel_id=1, source_target_pairs={{0,4},{4,0},{8,12},{12,8},{16,20},{20,16},{24,28},{28,24},{1,5},{5... | collective-permute-start | bytes 196616 | tf_op jit(solution)/shard_map/ppermute | solution.py:45
  52.3 0.7 %collective-permute-start.17 = (f32[2,64,128]{2,1,0:T(8,128)S(1)}, f32[2,64,128]{2,1,0:T(8,128)S(1)}, u32[]{:S(2)}, u32[]{:S(2)}) collective-permute-start(f32[2,64,128]{2,1,0:T(8,128)S(1)} %get-tuple-element.66), channel_id=1, source_target_pairs={{0,8},{4,12},{8,0},{12,4},{16,24},{20,28},{24,16},{28,20},{1,9},{5... | collective-permute-start | bytes 196616 | tf_op jit(solution)/shard_map/ppermute | solution.py:45
  52.9 0.0 collective-permute-done.12.refs_1_
  52.9 1.6 %collective-permute-start.18 = (f32[2,64,128]{2,1,0:T(8,128)S(1)}, f32[2,64,128]{2,1,0:T(8,128)S(1)}, u32[]{:S(2)}, u32[]{:S(2)}) collective-permute-start(f32[2,64,128]{2,1,0:T(8,128)S(1)} %get-tuple-element.67), channel_id=1, source_target_pairs={{0,12},{4,8},{8,4},{12,0},{16,28},{20,24},{24,20},{28,16},{1,13},{... | collective-permute-start | bytes 196616 | tf_op jit(solution)/shard_map/ppermute | solution.py:45
  54.6 0.0 collective-permute-done.13.refs_2_
  54.6 0.0 collective-permute-done.14.refs_3_
  54.6 0.9 %shard_map.68 = f32[2,2,4,64,128]{4,3,2,1,0:T(8,128)} custom-call(f32[2,2,64,128]{3,2,1,0:T(8,128)S(1)} %get-tuple-element.58.refs_0_, f32[2,2,64,128]{3,2,1,0:T(8,128)S(1)} %collective-permute-done.12.refs_1_, f32[2,2,64,128]{3,2,1,0:T(8,128)S(1)} %collective-permute-done.13.refs_2_, f32[2,2,64,128]{3,2,1,0:T(8,128)S(1)} %collective-permute-done.14.refs_3_), custom_call_target="tpu_custom_call" | custom-call | bytes 3000000 | tf_op jit(solution)/shard_map/pallas_call | solution.py:30
  55.4 0.0 collective-permute-done.16
  55.4 1.2 %collective-permute-done.17 = f32[2,64,128]{2,1,0:T(8,128)S(1)} collective-permute-done((f32[2,64,128]{2,1,0:T(8,128)S(1)}, f32[2,64,128]{2,1,0:T(8,128)S(1)}, u32[]{:S(2)}, u32[]{:S(2)}) %collective-permute-start.17) | collective-permute-done | bytes 65568 | tf_op jit(solution)/shard_map/ppermute | solution.py:45
  56.6 1.5 %collective-permute-done.18 = f32[2,64,128]{2,1,0:T(8,128)S(1)} collective-permute-done((f32[2,64,128]{2,1,0:T(8,128)S(1)}, f32[2,64,128]{2,1,0:T(8,128)S(1)}, u32[]{:S(2)}, u32[]{:S(2)}) %collective-permute-start.18) | collective-permute-done | bytes 65568 | tf_op jit(solution)/shard_map/ppermute | solution.py:45
  58.1 0.6 %add_add_fusion = f32[2,64,128]{2,1,0:T(8,128)} fusion(f32[2,64,128]{2,1,0:T(8,128)S(1)} %collective-permute-done.17, f32[2,64,128]{2,1,0:T(8,128)S(1)} %collective-permute-done.18, f32[2,64,128]{2,1,0:T(8,128)S(1)} %get-tuple-element.64, f32[2,64,128]{2,1,0:T(8,128)S(1)} %collective-permute-done.16), kind=kLoop, calls=%fused_computation.9 | loop fusion | flops 49152 | bytes 327680 | tf_op jit(solution)/shard_map/add | solution.py:556
  (3 shorter events, 0.1 us)
Async XLA Ops:
  0.6 0.8 %copy-start.2 = (f32[2,64,128]{2,1,0:T(8,128)S(1)}, f32[2,64,128]{2,1,0:T(8,128)}, u32[]{:S(2)}) copy-start(f32[2,64,128]{2,1,0:T(8,128)} %param.7) | copy-start | bytes 196612
  0.6 1.7 %copy-start.1 = (f32[2,2,4,64,128]{4,3,2,1,0:T(8,128)S(1)}, f32[2,2,4,64,128]{4,3,2,1,0:T(8,128)}, u32[]{:S(2)}) copy-start(f32[2,2,4,64,128]{4,3,2,1,0:T(8,128)} %param.4) | copy-start | bytes 1572868
  2.4 4.7 %copy-start = (f32[2,2,4,64,128]{4,3,2,1,0:T(8,128)S(1)}, f32[2,2,4,64,128]{4,3,2,1,0:T(8,128)}, u32[]{:S(2)}) copy-start(f32[2,2,4,64,128]{4,3,2,1,0:T(8,128)} %refs_0_.1) | copy-start | bytes 1572868
  2.6 9.4 %collective-permute-start = (f32[2,2,2,64,128]{4,3,2,1,0:T(8,128)S(1)}, f32[2,2,2,64,128]{4,3,2,1,0:T(8,128)S(1)}, u32[]{:S(2)}, u32[]{:S(2)}) collective-permute-start(f32[2,2,2,64,128]{4,3,2,1,0:T(8,128)S(1)} %get-tuple-element.36), channel_id=1, source_target_pairs={{0,4},{4,0},{8,12},{12,8},{16,20},{20,16},{24,28},{28,24},{1,5},{5... | collective-permute-start | bytes 786440 | tf_op jit(solution)/shard_map/ppermute | solution.py:45
  5.6 9.2 %collective-permute-start.1 = (f32[2,2,2,64,128]{4,3,2,1,0:T(8,128)S(1)}, f32[2,2,2,64,128]{4,3,2,1,0:T(8,128)S(1)}, u32[]{:S(2)}, u32[]{:S(2)}) collective-permute-start(f32[2,2,2,64,128]{4,3,2,1,0:T(8,128)S(1)} %get-tuple-element.37), channel_id=1, source_target_pairs={{0,8},{4,12},{8,0},{12,4},{16,24},{20,28},{24,16},{28,20},{1,9},{5... | collective-permute-start | bytes 786440 | tf_op jit(solution)/shard_map/ppermute | solution.py:45
  7.2 11.6 %collective-permute-start.2 = (f32[2,2,2,64,128]{4,3,2,1,0:T(8,128)S(1)}, f32[2,2,2,64,128]{4,3,2,1,0:T(8,128)S(1)}, u32[]{:S(2)}, u32[]{:S(2)}) collective-permute-start(f32[2,2,2,64,128]{4,3,2,1,0:T(8,128)S(1)} %get-tuple-element.38), channel_id=1, source_target_pairs={{0,12},{4,8},{8,4},{12,0},{16,28},{20,24},{24,20},{28,16},{1,13},{... | collective-permute-start | bytes 786440 | tf_op jit(solution)/shard_map/ppermute | solution.py:45
  7.5 2.1 %collective-permute-start.3 = (f32[2,64,128]{2,1,0:T(8,128)S(1)}, f32[2,64,128]{2,1,0:T(8,128)S(1)}, u32[]{:S(2)}, u32[]{:S(2)}) collective-permute-start(f32[2,64,128]{2,1,0:T(8,128)S(1)} %get-tuple-element.40), channel_id=1, source_target_pairs={{0,1},{1,0},{2,3},{3,2},{4,5},{5,4},{6,7},{7,6},{8,9},{9,8},{10,11... | collective-permute-start | bytes 196616 | tf_op jit(solution)/shard_map/ppermute | solution.py:71
  7.6 4.3 %collective-permute-start.4 = (f32[2,64,128]{2,1,0:T(8,128)S(1)}, f32[2,64,128]{2,1,0:T(8,128)S(1)}, u32[]{:S(2)}, u32[]{:S(2)}) collective-permute-start(f32[2,64,128]{2,1,0:T(8,128)S(1)} %get-tuple-element.41), channel_id=1, source_target_pairs={{1,2},{2,1},{0,3},{3,0},{5,6},{6,5},{4,7},{7,4},{9,10},{10,9},{8,1... | collective-permute-start | bytes 196616 | tf_op jit(solution)/shard_map/ppermute | solution.py:70
  19.4 6.2 %collective-permute-start.6 = (f32[2,2,128,128]{3,2,1,0:T(8,128)S(1)}, f32[2,2,128,128]{3,2,1,0:T(8,128)S(1)}, u32[]{:S(2)}, u32[]{:S(2)}) collective-permute-start(f32[2,2,128,128]{3,2,1,0:T(8,128)S(1)} %get-tuple-element.48), channel_id=1, source_target_pairs={{0,1},{1,0},{2,3},{3,2},{4,5},{5,4},{6,7},{7,6},{8,9},{9,8},{10,11... | collective-permute-start | bytes 786440 | tf_op jit(solution)/shard_map/ppermute | solution.py:71
  19.5 8.1 %collective-permute-start.5 = (f32[2,2,128,128]{3,2,1,0:T(8,128)S(1)}, f32[2,2,128,128]{3,2,1,0:T(8,128)S(1)}, u32[]{:S(2)}, u32[]{:S(2)}) collective-permute-start(f32[2,2,128,128]{3,2,1,0:T(8,128)S(1)} %shard_map.61.refs_4_), channel_id=1, source_target_pairs={{1,2},{2,1},{0,3},{3,0},{5,6},{6,5},{4,7},{7,4},{9,10},{10,9},{8,1... | collective-permute-start | bytes 786440 | tf_op jit(solution)/shard_map/ppermute | solution.py:70
  21.3 9.6 %collective-permute-start.9 = (f32[5,64,128]{2,1,0:T(8,128)S(1)}, f32[5,64,128]{2,1,0:T(8,128)S(1)}, u32[]{:S(2)}, u32[]{:S(2)}) collective-permute-start(f32[5,64,128]{2,1,0:T(8,128)S(1)} %get-tuple-element.52), channel_id=1, source_target_pairs={{0,4},{4,0},{8,12},{12,8},{16,20},{20,16},{24,28},{28,24},{1,5},{5... | collective-permute-start | bytes 491528 | tf_op jit(solution)/shard_map/ppermute | solution.py:45
  22.8 9.9 %collective-permute-start.10 = (f32[5,64,128]{2,1,0:T(8,128)S(1)}, f32[5,64,128]{2,1,0:T(8,128)S(1)}, u32[]{:S(2)}, u32[]{:S(2)}) collective-permute-start(f32[5,64,128]{2,1,0:T(8,128)S(1)} %get-tuple-element.53), channel_id=1, source_target_pairs={{0,8},{4,12},{8,0},{12,4},{16,24},{20,28},{24,16},{28,20},{1,9},{5... | collective-permute-start | bytes 491528 | tf_op jit(solution)/shard_map/ppermute | solution.py:45
  24.4 10.6 %collective-permute-start.11 = (f32[5,64,128]{2,1,0:T(8,128)S(1)}, f32[5,64,128]{2,1,0:T(8,128)S(1)}, u32[]{:S(2)}, u32[]{:S(2)}) collective-permute-start(f32[5,64,128]{2,1,0:T(8,128)S(1)} %get-tuple-element.54), channel_id=1, source_target_pairs={{0,12},{4,8},{8,4},{12,0},{16,28},{20,24},{24,20},{28,16},{1,13},{... | collective-permute-start | bytes 491528 | tf_op jit(solution)/shard_map/ppermute | solution.py:45
  25.7 9.5 %collective-permute-start.7 = (f32[2,128,128]{2,1,0:T(8,128)S(1)}, f32[2,128,128]{2,1,0:T(8,128)S(1)}, u32[]{:S(2)}, u32[]{:S(2)}) collective-permute-start(f32[2,128,128]{2,1,0:T(8,128)S(1)} %shard_map.64), channel_id=1, source_target_pairs={{0,16},{8,24},{16,0},{24,8},{1,17},{9,25},{17,1},{25,9},{2,18},{10... | collective-permute-start | bytes 393224 | tf_op jit(solution)/shard_map/ppermute | solution.py:53
  29.8 9.4 %collective-permute-start.8 = (f32[128,128]{1,0:T(8,128)S(1)}, f32[128,128]{1,0:T(8,128)S(1)}, u32[]{:S(2)}, u32[]{:S(2)}) collective-permute-start(f32[128,128]{1,0:T(8,128)S(1)} %get-tuple-element.50), channel_id=1, source_target_pairs={{0,16},{8,24},{16,0},{24,8},{1,17},{9,25},{17,1},{25,9},{2,18},{10... | collective-permute-start | bytes 196616 | tf_op jit(solution)/shard_map/ppermute | solution.py:53
  39.3 10.0 %collective-permute-start.15 = (f32[288,128]{1,0:T(8,128)S(1)}, f32[288,128]{1,0:T(8,128)S(1)}, u32[]{:S(2)}, u32[]{:S(2)}) collective-permute-start(f32[288,128]{1,0:T(8,128)S(1)} %get-tuple-element.57.refs_1_), channel_id=1, source_target_pairs={{0,16},{8,24},{16,0},{24,8},{1,17},{9,25},{17,1},{25,9},{2,18},{10... | collective-permute-start | bytes 442376 | tf_op jit(solution)/shard_map/ppermute | solution.py:53
  42.5 10.5 %collective-permute-start.12 = (f32[2,2,64,128]{3,2,1,0:T(8,128)S(1)}, f32[2,2,64,128]{3,2,1,0:T(8,128)S(1)}, u32[]{:S(2)}, u32[]{:S(2)}) collective-permute-start(f32[2,2,64,128]{3,2,1,0:T(8,128)S(1)} %get-tuple-element.59), channel_id=1, source_target_pairs={{0,4},{4,0},{8,12},{12,8},{16,20},{20,16},{24,28},{28,24},{1,5},{5... | collective-permute-start | bytes 393224 | tf_op jit(solution)/shard_map/ppermute | solution.py:45
  43.3 11.2 %collective-permute-start.13 = (f32[2,2,64,128]{3,2,1,0:T(8,128)S(1)}, f32[2,2,64,128]{3,2,1,0:T(8,128)S(1)}, u32[]{:S(2)}, u32[]{:S(2)}) collective-permute-start(f32[2,2,64,128]{3,2,1,0:T(8,128)S(1)} %get-tuple-element.60), channel_id=1, source_target_pairs={{0,8},{4,12},{8,0},{12,4},{16,24},{20,28},{24,16},{28,20},{1,9},{5... | collective-permute-start | bytes 393224 | tf_op jit(solution)/shard_map/ppermute | solution.py:45
  45.8 8.8 %collective-permute-start.14 = (f32[2,2,64,128]{3,2,1,0:T(8,128)S(1)}, f32[2,2,64,128]{3,2,1,0:T(8,128)S(1)}, u32[]{:S(2)}, u32[]{:S(2)}) collective-permute-start(f32[2,2,64,128]{3,2,1,0:T(8,128)S(1)} %get-tuple-element.61), channel_id=1, source_target_pairs={{0,12},{4,8},{8,4},{12,0},{16,28},{20,24},{24,20},{28,16},{1,13},{... | collective-permute-start | bytes 393224 | tf_op jit(solution)/shard_map/ppermute | solution.py:45
  51.0 4.4 %collective-permute-start.16 = (f32[2,64,128]{2,1,0:T(8,128)S(1)}, f32[2,64,128]{2,1,0:T(8,128)S(1)}, u32[]{:S(2)}, u32[]{:S(2)}) collective-permute-start(f32[2,64,128]{2,1,0:T(8,128)S(1)} %get-tuple-element.65), channel_id=1, source_target_pairs={{0,4},{4,0},{8,12},{12,8},{16,20},{20,16},{24,28},{28,24},{1,5},{5... | collective-permute-start | bytes 196616 | tf_op jit(solution)/shard_map/ppermute | solution.py:45
  52.3 4.4 %collective-permute-start.17 = (f32[2,64,128]{2,1,0:T(8,128)S(1)}, f32[2,64,128]{2,1,0:T(8,128)S(1)}, u32[]{:S(2)}, u32[]{:S(2)}) collective-permute-start(f32[2,64,128]{2,1,0:T(8,128)S(1)} %get-tuple-element.66), channel_id=1, source_target_pairs={{0,8},{4,12},{8,0},{12,4},{16,24},{20,28},{24,16},{28,20},{1,9},{5... | collective-permute-start | bytes 196616 | tf_op jit(solution)/shard_map/ppermute | solution.py:45
  52.9 5.2 %collective-permute-start.18 = (f32[2,64,128]{2,1,0:T(8,128)S(1)}, f32[2,64,128]{2,1,0:T(8,128)S(1)}, u32[]{:S(2)}, u32[]{:S(2)}) collective-permute-start(f32[2,64,128]{2,1,0:T(8,128)S(1)} %get-tuple-element.67), channel_id=1, source_target_pairs={{0,12},{4,8},{8,4},{12,0},{16,28},{20,24},{24,20},{28,16},{1,13},{... | collective-permute-start | bytes 196616 | tf_op jit(solution)/shard_map/ppermute | solution.py:45

commit v5 on v4

--- a/solution.py
+++ b/solution.py
@@ -9,6 +9,7 @@
 WIDE = 32
 NARROW = 16
 LANES = 128
+ALONG, ACROSS = (0, 1), (2, 3)
 REACH = 8
 DOWN = 24
 
@@ -46,7 +47,7 @@
 
 
 def gathered(sends):
-    return [sends[0]] + [member_swap(sends[k], k) for k in range(1, MEMBERS)]
+    return [member_swap(sends[k], k) for k in (3, 2, 1)] + [sends[0]]
 
 
 def depth_pair_swap(block):
@@ -276,13 +277,19 @@
 
 
 def second_edges_kernel(meta, *refs):
-    pack_edges(meta, refs[:MEMBERS], WIDE, False, refs[MEMBERS])
+    pack_edges(meta, refs[MEMBERS - 1 :: -1], WIDE, False, refs[MEMBERS])
 
 
 def merge_kernel(meta, *refs):
-    pieces, (_, merged, out) = refs[:MEMBERS], refs[MEMBERS:]
+    pieces, (_, merged, out) = refs[MEMBERS - 1 :: -1], refs[MEMBERS:]
     pack_edges(meta, pieces, WIDE, True, out)
     merge_members(meta, pieces, merged)
+
+
+def prepare_kernel(ks, meta, source, inverse, *refs):
+    for k, send in zip(ks, refs[-len(ks) :]):
+        send[0] = source[:, :, meta[0] ^ k]
+        send[1] = inverse[...]
 
 
 def observed_edges_kernel(meta, observed, first, second):
@@ -307,11 +314,11 @@
                     second[tile] = jnp.where(even, sides["left"], sides["right"])
 
 
-def observed_sends_kernel(meta, observed, first, second, *sends):
+def observed_sends_kernel(ks, meta, observed, first, second, *refs):
     even = meta[1] == 0
     planes, _, _, rows, count = observed.shape
     lanes = lane_ids((rows, count))
-    for k, send in enumerate(sends):
+    for k, send in zip(ks, refs[-len(ks) :]):
         shot = meta[0] ^ k
         for p in range(planes):
             for c in range(2):
@@ -325,7 +332,7 @@
 
 
 def merge_observed_kernel(meta, *refs):
-    pieces, out = refs[:MEMBERS], refs[MEMBERS]
+    pieces, out = refs[MEMBERS - 1 :: -1], refs[MEMBERS]
     planes = out.shape[0] // 2
     _, rows, count = pieces[0].shape
     for k, piece in enumerate(pieces):
@@ -463,33 +470,35 @@
 
 def field_kernel(meta, *refs):
     out = refs[MEMBERS]
-    for k, piece in enumerate(refs[:MEMBERS]):
+    for k, piece in enumerate(refs[MEMBERS - 1 :: -1]):
         out[:, :, meta[0] ^ k] = piece[...]
 
 
 def body(source, observed, wavenumber, damping):
     own_planes, _, shots, height, width = source.shape
-    member = position()[0]
     planes, high = 2 * own_planes, 2 * height
     one_group = lax.axis_size("gx") == 2
     rows = high if one_group else high + 2 * WIDE
     tile = (own_planes, 2, height, width)
 
     inverse = inverses(wavenumber, damping)
-    sends = [
-        jnp.stack([lax.dynamic_index_in_dim(source, member ^ k, 2, keepdims=False), inverse])
-        for k in range(MEMBERS)
-    ]
+    far = call(
+        lambda *refs: prepare_kernel(ACROSS, *refs), [(2, *tile)] * 2, source, inverse
+    )
+    near = call(
+        lambda *refs: prepare_kernel(ALONG, *refs), [(2, *tile)] * 2, source, inverse, far[0]
+    )
+    sends = [*near, *far]
     observed, *sends = lax.optimization_barrier([observed, *sends])
     pieces = gathered(sends)
     seen_edges = call(observed_edges_kernel, [(2, height, width)] * 2, observed)
     seen_edges = neighbour_swaps(*seen_edges, "gy", 1, ring=True)
-    first_seen, *seen_sends = call(
-        observed_sends_kernel,
-        [(2 * own_planes + 1, height, width)] * MEMBERS,
-        observed,
-        *seen_edges,
-    )
+    shape = [(2 * own_planes + 1, height, width)] * 2
+    far = call(lambda *refs: observed_sends_kernel(ACROSS, *refs), shape, observed, *seen_edges)
+    near = call(
+        lambda *refs: observed_sends_kernel(ALONG, *refs), shape, observed, *seen_edges, far[0]
+    )
+    first_seen, *seen_sends = *near, *far
     *pieces, first_seen = lax.optimization_barrier([*pieces, first_seen])
     seen_sends = [first_seen, *seen_sends]
     edge_shape = (2, 2, high, width)

time: 58.9 us -> 57.9 us (0.983)
  local copies, waits for them, and re-layouts: 0.84 us -> 0.13 us
  starting transfers between devices: 25.5 us -> 24.8 us
    unnamed x6 -> x4, local copies, waits for them, and re-layouts: 0.79 us -> 0.13 us
    pallas_call x11 -> x14, Pallas kernels: 7.2 us -> 7.36 us  [call(): pl.pallas_call(lambda *refs: kernel(position(), *refs), out_shape=[jax.Sh...]
where the time goes in v5:
time: 57.9 us; the launch traced here: 57.7 us
  starting transfers between devices  24.8 us (43%)
  waiting for transfers between devices  23 us (40%)
  Pallas kernels  7.36 us (13%)
  other arithmetic  1.61 us (3%)
  between operations  0.79 us (1%)
    ppermute x12, starting transfers between devices, member_swap(): return lax.ppermute(block, ('depth', 'gx'), pairs)  15.6 us
    ppermute x12, waiting for transfers between devices, member_swap(): return lax.ppermute(block, ('depth', 'gx'), pairs)  13.3 us
    pallas_call x14, Pallas kernels, call(): pl.pallas_call(lambda *refs: kernel(position(), *refs), out_shape=[jax.Sh...  7.36 us
    ppermute x3, waiting for transfers between devices, depth_pair_swap(): lax.ppermute(block, 'depth', [(z, z ^ 2) for z in range(lax.axis_size('de...  7.14 us
    ppermute x3, starting transfers between devices, depth_pair_swap(): lax.ppermute(block, 'depth', [(z, z ^ 2) for z in range(lax.axis_size('de...  5.52 us
    ppermute x2, starting transfers between devices, neighbour_swaps(): lax.ppermute(second, axis, pairs(1) + ends)  3.53 us
    ppermute x2, waiting for transfers between devices, neighbour_swaps(): lax.ppermute(second, axis, pairs(1) + ends)  2.58 us
  transfers between devices with their start and end apart: 19, of which 10 were waited for; matrix products, arithmetic and copies ran while one was open for 0% of the time, Pallas kernels for 11%

profile of v5, /device:TPU:0, one launch (start us, length us, event | category | flops | bytes accessed | tf_op | source)
XLA Modules:
  0.0 57.7 jit_solution(1099423667467033864)
XLA Ops:
  0.6 0.0 copy-start.1
  0.6 1.0 %divide_bitcast_fusion = (f32[2,1,64,128]{3,2,1,0:T(8,128)S(1)}, f32[2,1,64,128]{3,2,1,0:T(8,128)S(1)}) fusion(f32[2,64,128]{2,1,0:T(8,128)} %param.7, f32[2,64,128]{2,1,0:T(8,128)} %param.6), kind=kLoop, calls=%fused_computation.3 | loop fusion | flops 114688 | bytes 262144 | tf_op jit(solution)/shard_map/stack | solution.py:276
  1.6 0.1 copy-done.1
  1.8 0.0 copy-start
  1.8 4.0 %collective-permute-start = (f32[2,2,2,64,128]{4,3,2,1,0:T(8,128)S(1)}, f32[2,2,2,64,128]{4,3,2,1,0:T(8,128)S(1)}, u32[]{:S(2)}, u32[]{:S(2)}) collective-permute-start(f32[2,2,2,64,128]{4,3,2,1,0:T(8,128)S(1)} %get-tuple-element.43), channel_id=1, source_target_pairs={{0,12},{4,8},{8,4},{12,0},{16,28},{20,24},{24,20},{28,16},{1,13},{... | collective-permute-start | bytes 786440 | tf_op jit(solution)/shard_map/ppermute | solution.py:46
  5.9 0.4 collective-permute-start.1
  6.3 0.2 collective-permute-start.2
  6.5 0.0 copy-done
  6.5 0.3 shard_map.61
  6.8 0.1 collective-permute-start.3
  6.9 1.9 %collective-permute-start.4 = (f32[2,64,128]{2,1,0:T(8,128)S(1)}, f32[2,64,128]{2,1,0:T(8,128)S(1)}, u32[]{:S(2)}, u32[]{:S(2)}) collective-permute-start(f32[2,64,128]{2,1,0:T(8,128)S(1)} %get-tuple-element.49), channel_id=1, source_target_pairs={{1,2},{2,1},{0,3},{3,0},{5,6},{6,5},{4,7},{7,4},{9,10},{10,9},{8,1... | collective-permute-start | bytes 196616 | tf_op jit(solution)/shard_map/ppermute | solution.py:71
  8.8 0.0 collective-permute-done.3.refs_1_
  8.8 2.2 %collective-permute-done.4.refs_2_ = f32[2,64,128]{2,1,0:T(8,128)S(1)} collective-permute-done((f32[2,64,128]{2,1,0:T(8,128)S(1)}, f32[2,64,128]{2,1,0:T(8,128)S(1)}, u32[]{:S(2)}, u32[]{:S(2)}) %collective-permute-start.4) | collective-permute-done | bytes 65568 | tf_op jit(solution)/shard_map/ppermute | solution.py:71
  11.0 0.1 shard_map.62
  11.1 0.1 shard_map.63
  11.2 1.8 %collective-permute-done.refs_0_ = f32[2,2,2,64,128]{4,3,2,1,0:T(8,128)S(1)} collective-permute-done((f32[2,2,2,64,128]{4,3,2,1,0:T(8,128)S(1)}, f32[2,2,2,64,128]{4,3,2,1,0:T(8,128)S(1)}, u32[]{:S(2)}, u32[]{:S(2)}) %collective-permute-start) | collective-permute-done | bytes 262176 | tf_op jit(solution)/shard_map/ppermute | solution.py:46
  13.1 5.0 %collective-permute-done.1.refs_1_ = f32[2,2,2,64,128]{4,3,2,1,0:T(8,128)S(1)} collective-permute-done((f32[2,2,2,64,128]{4,3,2,1,0:T(8,128)S(1)}, f32[2,2,2,64,128]{4,3,2,1,0:T(8,128)S(1)}, u32[]{:S(2)}, u32[]{:S(2)}) %collective-permute-start.1) | collective-permute-done | bytes 262176 | tf_op jit(solution)/shard_map/ppermute | solution.py:46
  18.0 0.0 collective-permute-done.2.refs_2_
  18.0 0.3 shard_map.64.refs_4_
  18.3 0.4 shard_map.65
  18.7 0.1 collective-permute-start.6
  18.8 1.6 %collective-permute-start.5 = (f32[2,2,128,128]{3,2,1,0:T(8,128)S(1)}, f32[2,2,128,128]{3,2,1,0:T(8,128)S(1)}, u32[]{:S(2)}, u32[]{:S(2)}) collective-permute-start(f32[2,2,128,128]{3,2,1,0:T(8,128)S(1)} %shard_map.64.refs_4_), channel_id=1, source_target_pairs={{1,2},{2,1},{0,3},{3,0},{5,6},{6,5},{4,7},{7,4},{9,10},{10,9},{8,1... | collective-permute-start | bytes 786440 | tf_op jit(solution)/shard_map/ppermute | solution.py:71
  20.4 1.6 %collective-permute-start.10 = (f32[5,64,128]{2,1,0:T(8,128)S(1)}, f32[5,64,128]{2,1,0:T(8,128)S(1)}, u32[]{:S(2)}, u32[]{:S(2)}) collective-permute-start(f32[5,64,128]{2,1,0:T(8,128)S(1)} %get-tuple-element.50.refs_3_), channel_id=1, source_target_pairs={{0,8},{4,12},{8,0},{12,4},{16,24},{20,28},{24,16},{28,20},{1,9},{5... | collective-permute-start | bytes 491528 | tf_op jit(solution)/shard_map/ppermute | solution.py:46
  21.9 1.3 %collective-permute-start.9 = (f32[5,64,128]{2,1,0:T(8,128)S(1)}, f32[5,64,128]{2,1,0:T(8,128)S(1)}, u32[]{:S(2)}, u32[]{:S(2)}) collective-permute-start(f32[5,64,128]{2,1,0:T(8,128)S(1)} %get-tuple-element.60), channel_id=1, source_target_pairs={{0,12},{4,8},{8,4},{12,0},{16,28},{20,24},{24,20},{28,16},{1,13},{... | collective-permute-start | bytes 491528 | tf_op jit(solution)/shard_map/ppermute | solution.py:46
  23.2 0.6 %collective-permute-start.11 = (f32[5,64,128]{2,1,0:T(8,128)S(1)}, f32[5,64,128]{2,1,0:T(8,128)S(1)}, u32[]{:S(2)}, u32[]{:S(2)}) collective-permute-start(f32[5,64,128]{2,1,0:T(8,128)S(1)} %get-tuple-element.61), channel_id=1, source_target_pairs={{0,4},{4,0},{8,12},{12,8},{16,20},{20,16},{24,28},{28,24},{1,5},{5... | collective-permute-start | bytes 491528 | tf_op jit(solution)/shard_map/ppermute | solution.py:46
  23.9 0.9 %shard_map.67 = f32[2,128,128]{2,1,0:T(8,128)S(1)} custom-call(f32[2,4,2,128,128]{4,3,2,1,0:T(8,128)S(1)} %get-tuple-element.56.refs_0_.refs_1_), custom_call_target="tpu_custom_call" | custom-call | bytes 3000000 | tf_op jit(solution)/shard_map/pallas_call | solution.py:31
  24.8 0.0 collective-permute-done.6.refs_2_
  24.8 1.7 %collective-permute-start.7 = (f32[2,128,128]{2,1,0:T(8,128)S(1)}, f32[2,128,128]{2,1,0:T(8,128)S(1)}, u32[]{:S(2)}, u32[]{:S(2)}) collective-permute-start(f32[2,128,128]{2,1,0:T(8,128)S(1)} %shard_map.67), channel_id=1, source_target_pairs={{0,16},{8,24},{16,0},{24,8},{1,17},{9,25},{17,1},{25,9},{2,18},{10... | collective-permute-start | bytes 393224 | tf_op jit(solution)/shard_map/ppermute | solution.py:54
  26.5 0.4 collective-permute-done.5.refs_1_
  26.9 2.1 %shard_map.66 = (f32[2,4,2,128,128]{4,3,2,1,0:T(8,128)S(1)}, f32[4,2,128,256]{3,2,1,0:T(8,128)S(1)}, f32[128,128]{1,0:T(8,128)S(1)}) custom-call(f32[2,4,2,128,128]{4,3,2,1,0:T(8,128)S(1)} %get-tuple-element.56.refs_0_.refs_1_, f32[2,2,128,128]{3,2,1,0:T(8,128)S(1)} %collective-permute-done.5.refs_1_, f32[2,2,128,128]{3,2,1,0:T(8,128)S(1)} %collective-permute-done.6.refs_2_), custom_call_target="tpu_custom_call" | custom-call | bytes 30000000 | tf_op jit(solution)/shard_map/pallas_call | solution.py:31
  29.0 1.0 %collective-permute-start.8 = (f32[128,128]{1,0:T(8,128)S(1)}, f32[128,128]{1,0:T(8,128)S(1)}, u32[]{:S(2)}, u32[]{:S(2)}) collective-permute-start(f32[128,128]{1,0:T(8,128)S(1)} %get-tuple-element.59), channel_id=1, source_target_pairs={{0,16},{8,24},{16,0},{24,8},{1,17},{9,25},{17,1},{25,9},{2,18},{10... | collective-permute-start | bytes 196616 | tf_op jit(solution)/shard_map/ppermute | solution.py:54
  30.0 3.7 %collective-permute-done.9.refs_0_ = f32[5,64,128]{2,1,0:T(8,128)S(1)} collective-permute-done((f32[5,64,128]{2,1,0:T(8,128)S(1)}, f32[5,64,128]{2,1,0:T(8,128)S(1)}, u32[]{:S(2)}, u32[]{:S(2)}) %collective-permute-start.9) | collective-permute-done | bytes 163872 | tf_op jit(solution)/shard_map/ppermute | solution.py:46
  33.7 0.0 collective-permute-done.10.refs_1_
  33.7 0.0 collective-permute-done.11.refs_2_
  33.7 0.3 shard_map.68.refs_4_
  34.0 0.0 collective-permute-done.7.refs_2_
  34.0 3.7 %collective-permute-done.8.refs_3_ = f32[128,128]{1,0:T(8,128)S(1)} collective-permute-done((f32[128,128]{1,0:T(8,128)S(1)}, f32[128,128]{1,0:T(8,128)S(1)}, u32[]{:S(2)}, u32[]{:S(2)}) %collective-permute-start.8) | collective-permute-done | bytes 65568 | tf_op jit(solution)/shard_map/ppermute | solution.py:54
  37.7 0.2 shard_map.69
  37.9 2.8 %collective-permute-start.15 = (f32[288,128]{1,0:T(8,128)S(1)}, f32[288,128]{1,0:T(8,128)S(1)}, u32[]{:S(2)}, u32[]{:S(2)}) collective-permute-start(f32[288,128]{1,0:T(8,128)S(1)} %get-tuple-element.65.refs_1_), channel_id=1, source_target_pairs={{0,16},{8,24},{16,0},{24,8},{1,17},{9,25},{17,1},{25,9},{2,18},{10... | collective-permute-start | bytes 442376 | tf_op jit(solution)/shard_map/ppermute | solution.py:54
  40.8 3.3 %collective-permute-start.12 = (f32[2,2,64,128]{3,2,1,0:T(8,128)S(1)}, f32[2,2,64,128]{3,2,1,0:T(8,128)S(1)}, u32[]{:S(2)}, u32[]{:S(2)}) collective-permute-start(f32[2,2,64,128]{3,2,1,0:T(8,128)S(1)} %get-tuple-element.66), channel_id=1, source_target_pairs={{0,12},{4,8},{8,4},{12,0},{16,28},{20,24},{24,20},{28,16},{1,13},{... | collective-permute-start | bytes 393224 | tf_op jit(solution)/shard_map/ppermute | solution.py:46
  44.1 0.0 collective-permute-start.13
  44.1 0.6 %collective-permute-start.14 = (f32[2,2,64,128]{3,2,1,0:T(8,128)S(1)}, f32[2,2,64,128]{3,2,1,0:T(8,128)S(1)}, u32[]{:S(2)}, u32[]{:S(2)}) collective-permute-start(f32[2,2,64,128]{3,2,1,0:T(8,128)S(1)} %get-tuple-element.68), channel_id=1, source_target_pairs={{0,4},{4,0},{8,12},{12,8},{16,20},{20,16},{24,28},{28,24},{1,5},{5... | collective-permute-start | bytes 393224 | tf_op jit(solution)/shard_map/ppermute | solution.py:46
  44.7 3.4 %collective-permute-done.15.refs_3_ = f32[288,128]{1,0:T(8,128)S(1)} collective-permute-done((f32[288,128]{1,0:T(8,128)S(1)}, f32[288,128]{1,0:T(8,128)S(1)}, u32[]{:S(2)}, u32[]{:S(2)}) %collective-permute-start.15) | collective-permute-done | bytes 147488 | tf_op jit(solution)/shard_map/ppermute | solution.py:54
  48.1 1.7 %shard_map.72 = (f32[2,64,128]{2,1,0:T(8,128)S(1)}, f32[2,64,128]{2,1,0:T(8,128)S(1)}, f32[2,64,128]{2,1,0:T(8,128)S(1)}, f32[2,64,128]{2,1,0:T(8,128)S(1)}) custom-call(f32[4,2,128,256]{3,2,1,0:T(8,128)S(1)} %get-tuple-element.70.refs_0_, f32[2,4,2,128,128]{4,3,2,1,0:T(8,128)S(1)} %get-tuple-element.56.refs_0_.refs_1_, ...), custom_call_target="tpu_custom_call" | custom-call | bytes 3000000 | tf_op jit(solution)/shard_map/pallas_call | solution.py:31
  49.9 1.6 %collective-permute-start.16 = (f32[2,64,128]{2,1,0:T(8,128)S(1)}, f32[2,64,128]{2,1,0:T(8,128)S(1)}, u32[]{:S(2)}, u32[]{:S(2)}) collective-permute-start(f32[2,64,128]{2,1,0:T(8,128)S(1)} %get-tuple-element.72), channel_id=1, source_target_pairs={{0,12},{4,8},{8,4},{12,0},{16,28},{20,24},{24,20},{28,16},{1,13},{... | collective-permute-start | bytes 196616 | tf_op jit(solution)/shard_map/ppermute | solution.py:46
  51.4 1.4 %collective-permute-start.17 = (f32[2,64,128]{2,1,0:T(8,128)S(1)}, f32[2,64,128]{2,1,0:T(8,128)S(1)}, u32[]{:S(2)}, u32[]{:S(2)}) collective-permute-start(f32[2,64,128]{2,1,0:T(8,128)S(1)} %get-tuple-element.73), channel_id=1, source_target_pairs={{0,8},{4,12},{8,0},{12,4},{16,24},{20,28},{24,16},{28,20},{1,9},{5... | collective-permute-start | bytes 196616 | tf_op jit(solution)/shard_map/ppermute | solution.py:46
  52.8 0.0 collective-permute-done.12.refs_0_
  52.8 0.6 %collective-permute-start.18 = (f32[2,64,128]{2,1,0:T(8,128)S(1)}, f32[2,64,128]{2,1,0:T(8,128)S(1)}, u32[]{:S(2)}, u32[]{:S(2)}) collective-permute-start(f32[2,64,128]{2,1,0:T(8,128)S(1)} %get-tuple-element.74), channel_id=1, source_target_pairs={{0,4},{4,0},{8,12},{12,8},{16,20},{20,16},{24,28},{28,24},{1,5},{5... | collective-permute-start | bytes 196616 | tf_op jit(solution)/shard_map/ppermute | solution.py:46
  53.4 0.0 collective-permute-done.13.refs_1_
  53.4 0.0 collective-permute-done.14.refs_2_
  53.4 0.9 %shard_map.71 = f32[2,2,4,64,128]{4,3,2,1,0:T(8,128)} custom-call(f32[2,2,64,128]{3,2,1,0:T(8,128)S(1)} %collective-permute-done.12.refs_0_, f32[2,2,64,128]{3,2,1,0:T(8,128)S(1)} %collective-permute-done.13.refs_1_, f32[2,2,64,128]{3,2,1,0:T(8,128)S(1)} %collective-permute-done.14.refs_2_, f32[2,2,64,128]{3,2,1,0:T(8,128)S(1)} %get-tuple-element.69.refs_3_), custom_call_target="tpu_custom_call" | custom-call | bytes 3000000 | tf_op jit(solution)/shard_map/pallas_call | solution.py:31
  54.3 1.0 %collective-permute-done.16 = f32[2,64,128]{2,1,0:T(8,128)S(1)} collective-permute-done((f32[2,64,128]{2,1,0:T(8,128)S(1)}, f32[2,64,128]{2,1,0:T(8,128)S(1)}, u32[]{:S(2)}, u32[]{:S(2)}) %collective-permute-start.16) | collective-permute-done | bytes 65568 | tf_op jit(solution)/shard_map/ppermute | solution.py:46
  55.3 0.6 %collective-permute-done.17 = f32[2,64,128]{2,1,0:T(8,128)S(1)} collective-permute-done((f32[2,64,128]{2,1,0:T(8,128)S(1)}, f32[2,64,128]{2,1,0:T(8,128)S(1)}, u32[]{:S(2)}, u32[]{:S(2)}) %collective-permute-start.17) | collective-permute-done | bytes 65568 | tf_op jit(solution)/shard_map/ppermute | solution.py:46
  55.9 1.2 %collective-permute-done.18 = f32[2,64,128]{2,1,0:T(8,128)S(1)} collective-permute-done((f32[2,64,128]{2,1,0:T(8,128)S(1)}, f32[2,64,128]{2,1,0:T(8,128)S(1)}, u32[]{:S(2)}, u32[]{:S(2)}) %collective-permute-start.18) | collective-permute-done | bytes 65568 | tf_op jit(solution)/shard_map/ppermute | solution.py:46
  57.1 0.6 %add_add_fusion = f32[2,64,128]{2,1,0:T(8,128)} fusion(f32[2,64,128]{2,1,0:T(8,128)S(1)} %collective-permute-done.18, f32[2,64,128]{2,1,0:T(8,128)S(1)} %get-tuple-element.75, f32[2,64,128]{2,1,0:T(8,128)S(1)} %collective-permute-done.16, f32[2,64,128]{2,1,0:T(8,128)S(1)} %collective-permute-done.17), kind=kLoop, calls=%fused_computation.1 | loop fusion | flops 49152 | bytes 327680 | tf_op jit(solution)/shard_map/add | solution.py:565
  (4 shorter events, 0.1 us)
Async XLA Ops:
  0.6 1.1 %copy-start.1 = (f32[2,2,4,64,128]{4,3,2,1,0:T(8,128)S(1)}, f32[2,2,4,64,128]{4,3,2,1,0:T(8,128)}, u32[]{:S(2)}) copy-start(f32[2,2,4,64,128]{4,3,2,1,0:T(8,128)} %refs_0_.3) | copy-start | bytes 1572868
  1.8 4.7 %copy-start = (f32[2,2,4,64,128]{4,3,2,1,0:T(8,128)S(1)}, f32[2,2,4,64,128]{4,3,2,1,0:T(8,128)}, u32[]{:S(2)}) copy-start(f32[2,2,4,64,128]{4,3,2,1,0:T(8,128)} %refs_0_.6) | copy-start | bytes 1572868
  1.8 11.2 %collective-permute-start = (f32[2,2,2,64,128]{4,3,2,1,0:T(8,128)S(1)}, f32[2,2,2,64,128]{4,3,2,1,0:T(8,128)S(1)}, u32[]{:S(2)}, u32[]{:S(2)}) collective-permute-start(f32[2,2,2,64,128]{4,3,2,1,0:T(8,128)S(1)} %get-tuple-element.43), channel_id=1, source_target_pairs={{0,12},{4,8},{8,4},{12,0},{16,28},{20,24},{24,20},{28,16},{1,13},{... | collective-permute-start | bytes 786440 | tf_op jit(solution)/shard_map/ppermute | solution.py:46
  5.9 12.1 %collective-permute-start.1 = (f32[2,2,2,64,128]{4,3,2,1,0:T(8,128)S(1)}, f32[2,2,2,64,128]{4,3,2,1,0:T(8,128)S(1)}, u32[]{:S(2)}, u32[]{:S(2)}) collective-permute-start(f32[2,2,2,64,128]{4,3,2,1,0:T(8,128)S(1)} %get-tuple-element.44.refs_2_), channel_id=1, source_target_pairs={{0,8},{4,12},{8,0},{12,4},{16,24},{20,28},{24,16},{28,20},{1,9},{5... | collective-permute-start | bytes 786440 | tf_op jit(solution)/shard_map/ppermute | solution.py:46
  6.3 11.7 %collective-permute-start.2 = (f32[2,2,2,64,128]{4,3,2,1,0:T(8,128)S(1)}, f32[2,2,2,64,128]{4,3,2,1,0:T(8,128)S(1)}, u32[]{:S(2)}, u32[]{:S(2)}) collective-permute-start(f32[2,2,2,64,128]{4,3,2,1,0:T(8,128)S(1)} %get-tuple-element.45), channel_id=1, source_target_pairs={{0,4},{4,0},{8,12},{12,8},{16,20},{20,16},{24,28},{28,24},{1,5},{5... | collective-permute-start | bytes 786440 | tf_op jit(solution)/shard_map/ppermute | solution.py:46
  6.8 2.0 %collective-permute-start.3 = (f32[2,64,128]{2,1,0:T(8,128)S(1)}, f32[2,64,128]{2,1,0:T(8,128)S(1)}, u32[]{:S(2)}, u32[]{:S(2)}) collective-permute-start(f32[2,64,128]{2,1,0:T(8,128)S(1)} %get-tuple-element.48), channel_id=1, source_target_pairs={{0,1},{1,0},{2,3},{3,2},{4,5},{5,4},{6,7},{7,6},{8,9},{9,8},{10,11... | collective-permute-start | bytes 196616 | tf_op jit(solution)/shard_map/ppermute | solution.py:72
  6.9 4.1 %collective-permute-start.4 = (f32[2,64,128]{2,1,0:T(8,128)S(1)}, f32[2,64,128]{2,1,0:T(8,128)S(1)}, u32[]{:S(2)}, u32[]{:S(2)}) collective-permute-start(f32[2,64,128]{2,1,0:T(8,128)S(1)} %get-tuple-element.49), channel_id=1, source_target_pairs={{1,2},{2,1},{0,3},{3,0},{5,6},{6,5},{4,7},{7,4},{9,10},{10,9},{8,1... | collective-permute-start | bytes 196616 | tf_op jit(solution)/shard_map/ppermute | solution.py:71
  18.7 6.1 %collective-permute-start.6 = (f32[2,2,128,128]{3,2,1,0:T(8,128)S(1)}, f32[2,2,128,128]{3,2,1,0:T(8,128)S(1)}, u32[]{:S(2)}, u32[]{:S(2)}) collective-permute-start(f32[2,2,128,128]{3,2,1,0:T(8,128)S(1)} %get-tuple-element.57), channel_id=1, source_target_pairs={{0,1},{1,0},{2,3},{3,2},{4,5},{5,4},{6,7},{7,6},{8,9},{9,8},{10,11... | collective-permute-start | bytes 786440 | tf_op jit(solution)/shard_map/ppermute | solution.py:72
  18.8 8.1 %collective-permute-start.5 = (f32[2,2,128,128]{3,2,1,0:T(8,128)S(1)}, f32[2,2,128,128]{3,2,1,0:T(8,128)S(1)}, u32[]{:S(2)}, u32[]{:S(2)}) collective-permute-start(f32[2,2,128,128]{3,2,1,0:T(8,128)S(1)} %shard_map.64.refs_4_), channel_id=1, source_target_pairs={{1,2},{2,1},{0,3},{3,0},{5,6},{6,5},{4,7},{7,4},{9,10},{10,9},{8,1... | collective-permute-start | bytes 786440 | tf_op jit(solution)/shard_map/ppermute | solution.py:71
  20.4 13.3 %collective-permute-start.10 = (f32[5,64,128]{2,1,0:T(8,128)S(1)}, f32[5,64,128]{2,1,0:T(8,128)S(1)}, u32[]{:S(2)}, u32[]{:S(2)}) collective-permute-start(f32[5,64,128]{2,1,0:T(8,128)S(1)} %get-tuple-element.50.refs_3_), channel_id=1, source_target_pairs={{0,8},{4,12},{8,0},{12,4},{16,24},{20,28},{24,16},{28,20},{1,9},{5... | collective-permute-start | bytes 491528 | tf_op jit(solution)/shard_map/ppermute | solution.py:46
  21.9 11.8 %collective-permute-start.9 = (f32[5,64,128]{2,1,0:T(8,128)S(1)}, f32[5,64,128]{2,1,0:T(8,128)S(1)}, u32[]{:S(2)}, u32[]{:S(2)}) collective-permute-start(f32[5,64,128]{2,1,0:T(8,128)S(1)} %get-tuple-element.60), channel_id=1, source_target_pairs={{0,12},{4,8},{8,4},{12,0},{16,28},{20,24},{24,20},{28,16},{1,13},{... | collective-permute-start | bytes 491528 | tf_op jit(solution)/shard_map/ppermute | solution.py:46
  23.2 10.5 %collective-permute-start.11 = (f32[5,64,128]{2,1,0:T(8,128)S(1)}, f32[5,64,128]{2,1,0:T(8,128)S(1)}, u32[]{:S(2)}, u32[]{:S(2)}) collective-permute-start(f32[5,64,128]{2,1,0:T(8,128)S(1)} %get-tuple-element.61), channel_id=1, source_target_pairs={{0,4},{4,0},{8,12},{12,8},{16,20},{20,16},{24,28},{28,24},{1,5},{5... | collective-permute-start | bytes 491528 | tf_op jit(solution)/shard_map/ppermute | solution.py:46
  24.8 9.2 %collective-permute-start.7 = (f32[2,128,128]{2,1,0:T(8,128)S(1)}, f32[2,128,128]{2,1,0:T(8,128)S(1)}, u32[]{:S(2)}, u32[]{:S(2)}) collective-permute-start(f32[2,128,128]{2,1,0:T(8,128)S(1)} %shard_map.67), channel_id=1, source_target_pairs={{0,16},{8,24},{16,0},{24,8},{1,17},{9,25},{17,1},{25,9},{2,18},{10... | collective-permute-start | bytes 393224 | tf_op jit(solution)/shard_map/ppermute | solution.py:54
  29.0 8.7 %collective-permute-start.8 = (f32[128,128]{1,0:T(8,128)S(1)}, f32[128,128]{1,0:T(8,128)S(1)}, u32[]{:S(2)}, u32[]{:S(2)}) collective-permute-start(f32[128,128]{1,0:T(8,128)S(1)} %get-tuple-element.59), channel_id=1, source_target_pairs={{0,16},{8,24},{16,0},{24,8},{1,17},{9,25},{17,1},{25,9},{2,18},{10... | collective-permute-start | bytes 196616 | tf_op jit(solution)/shard_map/ppermute | solution.py:54
  37.9 10.2 %collective-permute-start.15 = (f32[288,128]{1,0:T(8,128)S(1)}, f32[288,128]{1,0:T(8,128)S(1)}, u32[]{:S(2)}, u32[]{:S(2)}) collective-permute-start(f32[288,128]{1,0:T(8,128)S(1)} %get-tuple-element.65.refs_1_), channel_id=1, source_target_pairs={{0,16},{8,24},{16,0},{24,8},{1,17},{9,25},{17,1},{25,9},{2,18},{10... | collective-permute-start | bytes 442376 | tf_op jit(solution)/shard_map/ppermute | solution.py:54
  40.8 12.0 %collective-permute-start.12 = (f32[2,2,64,128]{3,2,1,0:T(8,128)S(1)}, f32[2,2,64,128]{3,2,1,0:T(8,128)S(1)}, u32[]{:S(2)}, u32[]{:S(2)}) collective-permute-start(f32[2,2,64,128]{3,2,1,0:T(8,128)S(1)} %get-tuple-element.66), channel_id=1, source_target_pairs={{0,12},{4,8},{8,4},{12,0},{16,28},{20,24},{24,20},{28,16},{1,13},{... | collective-permute-start | bytes 393224 | tf_op jit(solution)/shard_map/ppermute | solution.py:46
  44.1 9.4 %collective-permute-start.13 = (f32[2,2,64,128]{3,2,1,0:T(8,128)S(1)}, f32[2,2,64,128]{3,2,1,0:T(8,128)S(1)}, u32[]{:S(2)}, u32[]{:S(2)}) collective-permute-start(f32[2,2,64,128]{3,2,1,0:T(8,128)S(1)} %get-tuple-element.67), channel_id=1, source_target_pairs={{0,8},{4,12},{8,0},{12,4},{16,24},{20,28},{24,16},{28,20},{1,9},{5... | collective-permute-start | bytes 393224 | tf_op jit(solution)/shard_map/ppermute | solution.py:46
  44.1 9.4 %collective-permute-start.14 = (f32[2,2,64,128]{3,2,1,0:T(8,128)S(1)}, f32[2,2,64,128]{3,2,1,0:T(8,128)S(1)}, u32[]{:S(2)}, u32[]{:S(2)}) collective-permute-start(f32[2,2,64,128]{3,2,1,0:T(8,128)S(1)} %get-tuple-element.68), channel_id=1, source_target_pairs={{0,4},{4,0},{8,12},{12,8},{16,20},{20,16},{24,28},{28,24},{1,5},{5... | collective-permute-start | bytes 393224 | tf_op jit(solution)/shard_map/ppermute | solution.py:46
  49.9 5.4 %collective-permute-start.16 = (f32[2,64,128]{2,1,0:T(8,128)S(1)}, f32[2,64,128]{2,1,0:T(8,128)S(1)}, u32[]{:S(2)}, u32[]{:S(2)}) collective-permute-start(f32[2,64,128]{2,1,0:T(8,128)S(1)} %get-tuple-element.72), channel_id=1, source_target_pairs={{0,12},{4,8},{8,4},{12,0},{16,28},{20,24},{24,20},{28,16},{1,13},{... | collective-permute-start | bytes 196616 | tf_op jit(solution)/shard_map/ppermute | solution.py:46
  51.4 4.5 %collective-permute-start.17 = (f32[2,64,128]{2,1,0:T(8,128)S(1)}, f32[2,64,128]{2,1,0:T(8,128)S(1)}, u32[]{:S(2)}, u32[]{:S(2)}) collective-permute-start(f32[2,64,128]{2,1,0:T(8,128)S(1)} %get-tuple-element.73), channel_id=1, source_target_pairs={{0,8},{4,12},{8,0},{12,4},{16,24},{20,28},{24,16},{28,20},{1,9},{5... | collective-permute-start | bytes 196616 | tf_op jit(solution)/shard_map/ppermute | solution.py:46
  52.8 4.3 %collective-permute-start.18 = (f32[2,64,128]{2,1,0:T(8,128)S(1)}, f32[2,64,128]{2,1,0:T(8,128)S(1)}, u32[]{:S(2)}, u32[]{:S(2)}) collective-permute-start(f32[2,64,128]{2,1,0:T(8,128)S(1)} %get-tuple-element.74), channel_id=1, source_target_pairs={{0,4},{4,0},{8,12},{12,8},{16,20},{20,16},{24,28},{28,24},{1,5},{5... | collective-permute-start | bytes 196616 | tf_op jit(solution)/shard_map/ppermute | solution.py:46

commit v6 on v5

--- a/solution.py
+++ b/solution.py
@@ -54,7 +54,7 @@
     return lax.ppermute(block, "depth", [(z, z ^ 2) for z in range(lax.axis_size("depth"))])
 
 
-def neighbour_swaps(first, second, axis, stride, ring=False):
+def neighbour_swaps(first, second, axis, stride):
     size = lax.axis_size(axis)
     count = size // stride
 
@@ -66,10 +66,23 @@
                 found += [(a, b), (b, a)]
         return found
 
-    ends = [(i, size - stride + i) for i in range(stride)] if ring and count % 2 == 0 else []
-    ends += [(b, a) for a, b in ends]
-    got_second = lax.ppermute(second, axis, pairs(1) + ends) if count > 2 else jnp.zeros_like(second)
+    got_second = lax.ppermute(second, axis, pairs(1)) if count > 2 else jnp.zeros_like(second)
     got_first = lax.ppermute(first, axis, pairs(0)) if count > 1 else jnp.zeros_like(first)
+    return got_first, got_second
+
+
+def side_swaps(first, second):
+    nx, ny = lax.axis_size("gx"), lax.axis_size("gy")
+    if ny % 2 or ny == 2:
+        return neighbour_swaps(first, second, "gy", 1)
+    pairs = []
+    for x in range(nx):
+        for low in range(1, ny - 1, 2):
+            a, b = x * ny + low, x * ny + low + 1
+            pairs += [(a, b), (b, a)]
+        pairs += [(x * ny + end, (x ^ 1) * ny + end) for end in (0, ny - 1)]
+    got_second = lax.ppermute(second, ("gx", "gy"), pairs)
+    got_first = lax.ppermute(first, "gy", [(y, y ^ 1) for y in range(ny)])
     return got_first, got_second
 
 
@@ -276,14 +289,12 @@
     return jnp.stack([real_diag / denom, -(damping / denom)], axis=1)
 
 
-def second_edges_kernel(meta, *refs):
-    pack_edges(meta, refs[MEMBERS - 1 :: -1], WIDE, False, refs[MEMBERS])
+def edges_kernel(first, meta, *refs):
+    pack_edges(meta, refs[MEMBERS - 1 :: -1], WIDE, first, refs[-1])
 
 
 def merge_kernel(meta, *refs):
-    pieces, (_, merged, out) = refs[MEMBERS - 1 :: -1], refs[MEMBERS:]
-    pack_edges(meta, pieces, WIDE, True, out)
-    merge_members(meta, pieces, merged)
+    merge_members(meta, refs[MEMBERS - 1 :: -1], refs[MEMBERS])
 
 
 def prepare_kernel(ks, meta, source, inverse, *refs):
@@ -332,7 +343,7 @@
 
 
 def merge_observed_kernel(meta, *refs):
-    pieces, out = refs[MEMBERS - 1 :: -1], refs[MEMBERS]
+    pieces, out = refs[MEMBERS - 1 :: -1], refs[-1]
     planes = out.shape[0] // 2
     _, rows, count = pieces[0].shape
     for k, piece in enumerate(pieces):
@@ -492,32 +503,31 @@
     observed, *sends = lax.optimization_barrier([observed, *sends])
     pieces = gathered(sends)
     seen_edges = call(observed_edges_kernel, [(2, height, width)] * 2, observed)
-    seen_edges = neighbour_swaps(*seen_edges, "gy", 1, ring=True)
-    shape = [(2 * own_planes + 1, height, width)] * 2
-    far = call(lambda *refs: observed_sends_kernel(ACROSS, *refs), shape, observed, *seen_edges)
-    near = call(
-        lambda *refs: observed_sends_kernel(ALONG, *refs), shape, observed, *seen_edges, far[0]
-    )
-    first_seen, *seen_sends = *near, *far
-    *pieces, first_seen = lax.optimization_barrier([*pieces, first_seen])
-    seen_sends = [first_seen, *seen_sends]
+    seen_edges = side_swaps(*seen_edges)
+    *pieces, one, two = lax.optimization_barrier([*pieces, *seen_edges])
     edge_shape = (2, 2, high, width)
-    (second,) = call(second_edges_kernel, [edge_shape], *pieces)
-    merged, first = call(
-        merge_kernel, [(2, planes, 2, high, width), edge_shape], *pieces, second
-    )
+    (second,) = call(lambda *refs: edges_kernel(False, *refs), [edge_shape], *pieces)
+    (merged,) = call(merge_kernel, [(2, planes, 2, high, width)], *pieces)
     if not one_group:
-        merged, first, second = (with_row_halo(a, WIDE) for a in (merged, first, second))
-    first, second = neighbour_swaps(first, second, "gy", 1, ring=True)
-    seen = gathered(seen_sends)
-
+        merged = with_row_halo(merged, WIDE)
     (centre,) = call(
         centre_kernel,
         [(2, rows, width)],
         merged,
         scratch=[VMEM((planes, 2, rows, width), F32), *sweep_scratch(rows, width)],
     )
+    (first,) = call(lambda *refs: edges_kernel(True, *refs), [edge_shape], *pieces, centre)
+    packed = first
+    if not one_group:
+        first, second = (with_row_halo(a, WIDE) for a in (first, second))
+    first, second = side_swaps(first, second)
     centre = depth_pair_swap(centre)
+    shape = [(2 * own_planes + 1, height, width)] * 2
+    far = call(lambda *refs: observed_sends_kernel(ACROSS, *refs), shape, observed, one, two, packed)
+    near = call(
+        lambda *refs: observed_sends_kernel(ALONG, *refs), shape, observed, one, two, far[0]
+    )
+    seen = gathered([*near, *far])
 
     whole = (planes, 2, rows, 2 * width)
     scratch = sweep_scratch(rows)
@@ -532,7 +542,7 @@
     )
     got = depth_pair_swap(send)
     (seen,) = call(
-        merge_observed_kernel, [(planes, 2, high, 2 * width)], *seen, cost=100_000_000
+        merge_observed_kernel, [(planes, 2, high, 2 * width)], *seen, centre, cost=3_000_000
     )
     seen = seen if one_group else with_row_halo(seen, WIDE)
     field, residual, adjoint, send = call(

time: 57.9 us -> 57.1 us (0.986)
  waiting for transfers between devices: 23 us -> 21.5 us
  starting transfers between devices: 24.8 us -> 25.5 us
    ppermute x12, waiting for transfers between devices: 13.3 us -> 3.36 us  [member_swap(): return lax.ppermute(block, ('depth', 'gx'), pairs)]
    ppermute x4, waiting for transfers between devices: 2.58 us -> 9.7 us  [the longest x2 9.69 us: side_swaps(): got_second = lax.ppermute(second, ('gx', 'gy'), pairs)]
    ppermute x3, waiting for transfers between devices: 7.14 us -> 8.44 us  [depth_pair_swap(): lax.ppermute(block, 'depth', [(z, z ^ 2) for z in range(lax.axis_size('de...]
    ppermute x3, starting transfers between devices: 5.52 us -> 6.25 us  [depth_pair_swap(): lax.ppermute(block, 'depth', [(z, z ^ 2) for z in range(lax.axis_size('de...]
    pallas_call x14 -> x15, Pallas kernels: 7.36 us -> 7.42 us  [call(): pl.pallas_call(lambda *refs: kernel(position(), *refs), out_shape=[jax.Sh...]
  transfers between devices with their start and end apart: 19 -> 19, of which waited for: 10 -> 7; matrix products, arithmetic and copies ran while one was open for 0% -> 0% of each run, Pallas kernels for 11% -> 12%
where the time goes in v6:
time: 57.1 us; the launch traced here: 56.9 us
  starting transfers between devices  25.5 us (45%)
  waiting for transfers between devices  21.5 us (38%)
  Pallas kernels  7.42 us (13%)
  other arithmetic  1.61 us (3%)
  between operations  0.79 us (1%)
    ppermute x12, starting transfers between devices, member_swap(): return lax.ppermute(block, ('depth', 'gx'), pairs)  15.5 us
    ppermute x2, waiting for transfers between devices, side_swaps(): got_second = lax.ppermute(second, ('gx', 'gy'), pairs)  9.69 us
    ppermute x3, waiting for transfers between devices, depth_pair_swap(): lax.ppermute(block, 'depth', [(z, z ^ 2) for z in range(lax.axis_size('de...  8.44 us
    pallas_call x15, Pallas kernels, call(): pl.pallas_call(lambda *refs: kernel(position(), *refs), out_shape=[jax.Sh...  7.42 us
    ppermute x3, starting transfers between devices, depth_pair_swap(): lax.ppermute(block, 'depth', [(z, z ^ 2) for z in range(lax.axis_size('de...  6.25 us
    ppermute x2, starting transfers between devices, side_swaps(): got_second = lax.ppermute(second, ('gx', 'gy'), pairs)  3.59 us
    ppermute x12, waiting for transfers between devices, member_swap(): return lax.ppermute(block, ('depth', 'gx'), pairs)  3.36 us
  transfers between devices with their start and end apart: 19, of which 7 were waited for; matrix products, arithmetic and copies ran while one was open for 0% of the time, Pallas kernels for 12%

profile of v6, /device:TPU:0, one launch (start us, length us, event | category | flops | bytes accessed | tf_op | source)
XLA Modules:
  0.0 56.9 jit_solution(11412745682310528857)
XLA Ops:
  0.6 0.0 copy-start.1
  0.6 1.0 %divide_bitcast_fusion = (f32[2,1,64,128]{3,2,1,0:T(8,128)S(1)}, f32[2,1,64,128]{3,2,1,0:T(8,128)S(1)}) fusion(f32[2,64,128]{2,1,0:T(8,128)} %param.7, f32[2,64,128]{2,1,0:T(8,128)} %param.6), kind=kLoop, calls=%fused_computation.3 | loop fusion | flops 114688 | bytes 262144 | tf_op jit(solution)/shard_map/stack | solution.py:289
  1.6 0.1 copy-done.1
  1.8 0.0 copy-start
  1.8 4.0 %collective-permute-start = (f32[2,2,2,64,128]{4,3,2,1,0:T(8,128)S(1)}, f32[2,2,2,64,128]{4,3,2,1,0:T(8,128)S(1)}, u32[]{:S(2)}, u32[]{:S(2)}) collective-permute-start(f32[2,2,2,64,128]{4,3,2,1,0:T(8,128)S(1)} %get-tuple-element.42), channel_id=1, source_target_pairs={{0,12},{4,8},{8,4},{12,0},{16,28},{20,24},{24,20},{28,16},{1,13},{... | collective-permute-start | bytes 786440 | tf_op jit(solution)/shard_map/ppermute | solution.py:46
  5.9 0.4 collective-permute-start.1
  6.3 0.2 collective-permute-start.2
  6.5 0.0 copy-done
  6.5 0.3 shard_map.61
  6.8 0.1 collective-permute-start.3
  6.9 1.9 %collective-permute-start.4 = (f32[2,64,128]{2,1,0:T(8,128)S(1)}, f32[2,64,128]{2,1,0:T(8,128)S(1)}, u32[]{:S(2)}, u32[]{:S(2)}) collective-permute-start(f32[2,64,128]{2,1,0:T(8,128)S(1)} %get-tuple-element.48), channel_id=1, source_target_pairs={{1,2},{2,1},{0,4},{3,7},{5,6},{6,5},{4,0},{7,3},{9,10},{10,9},{8,1... | collective-permute-start | bytes 196616 | tf_op jit(solution)/shard_map/ppermute | solution.py:84
  8.8 0.0 collective-permute-done.3.refs_1_
  8.8 9.7 %collective-permute-done.4.refs_2_ = f32[2,64,128]{2,1,0:T(8,128)S(1)} collective-permute-done((f32[2,64,128]{2,1,0:T(8,128)S(1)}, f32[2,64,128]{2,1,0:T(8,128)S(1)}, u32[]{:S(2)}, u32[]{:S(2)}) %collective-permute-start.4) | collective-permute-done | bytes 65568 | tf_op jit(solution)/shard_map/ppermute | solution.py:84
  18.5 0.0 collective-permute-done.refs_0_
  18.5 0.0 collective-permute-done.1.refs_1_
  18.5 0.0 collective-permute-done.2.refs_2_
  18.5 0.3 shard_map.63
  18.8 1.7 %collective-permute-start.5 = (f32[2,2,128,128]{3,2,1,0:T(8,128)S(1)}, f32[2,2,128,128]{3,2,1,0:T(8,128)S(1)}, u32[]{:S(2)}, u32[]{:S(2)}) collective-permute-start(f32[2,2,128,128]{3,2,1,0:T(8,128)S(1)} %shard_map.63), channel_id=1, source_target_pairs={{1,2},{2,1},{0,4},{3,7},{5,6},{6,5},{4,0},{7,3},{9,10},{10,9},{8,1... | collective-permute-start | bytes 786440 | tf_op jit(solution)/shard_map/ppermute | solution.py:84
  20.5 0.1 shard_map.62.refs_0_.refs_1_
  20.6 0.9 %shard_map.64.refs_4_ = f32[2,128,128]{2,1,0:T(8,128)S(1)} custom-call(f32[2,4,2,128,128]{4,3,2,1,0:T(8,128)S(1)} %shard_map.62.refs_0_.refs_1_), custom_call_target="tpu_custom_call" | custom-call | bytes 3000000 | tf_op jit(solution)/shard_map/pallas_call | solution.py:31
  21.5 0.3 shard_map.65.refs_3_
  21.8 0.1 collective-permute-start.6
  21.9 0.1 shard_map.67
  22.1 1.6 %collective-permute-start.10 = (f32[5,64,128]{2,1,0:T(8,128)S(1)}, f32[5,64,128]{2,1,0:T(8,128)S(1)}, u32[]{:S(2)}, u32[]{:S(2)}) collective-permute-start(f32[5,64,128]{2,1,0:T(8,128)S(1)} %get-tuple-element.58.refs_3_), channel_id=1, source_target_pairs={{0,8},{4,12},{8,0},{12,4},{16,24},{20,28},{24,16},{28,20},{1,9},{5... | collective-permute-start | bytes 491528 | tf_op jit(solution)/shard_map/ppermute | solution.py:46
  23.7 0.1 shard_map.68
  23.8 0.9 %collective-permute-start.9 = (f32[5,64,128]{2,1,0:T(8,128)S(1)}, f32[5,64,128]{2,1,0:T(8,128)S(1)}, u32[]{:S(2)}, u32[]{:S(2)}) collective-permute-start(f32[5,64,128]{2,1,0:T(8,128)S(1)} %get-tuple-element.57), channel_id=1, source_target_pairs={{0,12},{4,8},{8,4},{12,0},{16,28},{20,24},{24,20},{28,16},{1,13},{... | collective-permute-start | bytes 491528 | tf_op jit(solution)/shard_map/ppermute | solution.py:46
  24.7 1.1 %collective-permute-start.11 = (f32[5,64,128]{2,1,0:T(8,128)S(1)}, f32[5,64,128]{2,1,0:T(8,128)S(1)}, u32[]{:S(2)}, u32[]{:S(2)}) collective-permute-start(f32[5,64,128]{2,1,0:T(8,128)S(1)} %get-tuple-element.59), channel_id=1, source_target_pairs={{0,4},{4,0},{8,12},{12,8},{16,20},{20,16},{24,28},{28,24},{1,5},{5... | collective-permute-start | bytes 491528 | tf_op jit(solution)/shard_map/ppermute | solution.py:46
  25.8 0.0 collective-permute-done.5.refs_1_
  25.8 2.2 %collective-permute-start.7 = (f32[2,128,128]{2,1,0:T(8,128)S(1)}, f32[2,128,128]{2,1,0:T(8,128)S(1)}, u32[]{:S(2)}, u32[]{:S(2)}) collective-permute-start(f32[2,128,128]{2,1,0:T(8,128)S(1)} %shard_map.64.refs_4_), channel_id=1, source_target_pairs={{0,16},{8,24},{16,0},{24,8},{1,17},{9,25},{17,1},{25,9},{2,18},{10... | collective-permute-start | bytes 393224 | tf_op jit(solution)/shard_map/ppermute | solution.py:54
  28.0 0.0 collective-permute-done.6.refs_2_
  28.0 2.1 %shard_map.66 = (f32[2,4,2,128,128]{4,3,2,1,0:T(8,128)S(1)}, f32[4,2,128,256]{3,2,1,0:T(8,128)S(1)}, f32[128,128]{1,0:T(8,128)S(1)}) custom-call(f32[2,4,2,128,128]{4,3,2,1,0:T(8,128)S(1)} %shard_map.62.refs_0_.refs_1_, f32[2,2,128,128]{3,2,1,0:T(8,128)S(1)} %collective-permute-done.5.refs_1_, f32[2,2,128,128]{3,2,1,0:T(8,128)S(1)} %collective-permute-done.6.refs_2_), custom_call_target="tpu_custom_call" | custom-call | bytes 30000000 | tf_op jit(solution)/shard_map/pallas_call | solution.py:31
  30.1 0.1 collective-permute-start.8
  30.2 4.4 %collective-permute-done.7.refs_4_.refs_2_ = f32[2,128,128]{2,1,0:T(8,128)S(1)} collective-permute-done((f32[2,128,128]{2,1,0:T(8,128)S(1)}, f32[2,128,128]{2,1,0:T(8,128)S(1)}, u32[]{:S(2)}, u32[]{:S(2)}) %collective-permute-start.7) | collective-permute-done | bytes 131104 | tf_op jit(solution)/shard_map/ppermute | solution.py:54
  34.6 0.9 %collective-permute-done.9.refs_0_ = f32[5,64,128]{2,1,0:T(8,128)S(1)} collective-permute-done((f32[5,64,128]{2,1,0:T(8,128)S(1)}, f32[5,64,128]{2,1,0:T(8,128)S(1)}, u32[]{:S(2)}, u32[]{:S(2)}) %collective-permute-start.9) | collective-permute-done | bytes 163872 | tf_op jit(solution)/shard_map/ppermute | solution.py:46
  35.5 0.0 collective-permute-done.10.refs_1_
  35.5 0.0 collective-permute-done.11.refs_2_
  35.5 0.3 shard_map.69.refs_4_
  35.8 2.5 %collective-permute-done.8.refs_3_ = f32[128,128]{1,0:T(8,128)S(1)} collective-permute-done((f32[128,128]{1,0:T(8,128)S(1)}, f32[128,128]{1,0:T(8,128)S(1)}, u32[]{:S(2)}, u32[]{:S(2)}) %collective-permute-start.8) | collective-permute-done | bytes 65568 | tf_op jit(solution)/shard_map/ppermute | solution.py:54
  38.3 0.2 shard_map.70
  38.5 4.0 %collective-permute-start.15 = (f32[288,128]{1,0:T(8,128)S(1)}, f32[288,128]{1,0:T(8,128)S(1)}, u32[]{:S(2)}, u32[]{:S(2)}) collective-permute-start(f32[288,128]{1,0:T(8,128)S(1)} %get-tuple-element.63.refs_1_), channel_id=1, source_target_pairs={{0,16},{8,24},{16,0},{24,8},{1,17},{9,25},{17,1},{25,9},{2,18},{10... | collective-permute-start | bytes 442376 | tf_op jit(solution)/shard_map/ppermute | solution.py:54
  42.5 3.0 %collective-permute-start.12 = (f32[2,2,64,128]{3,2,1,0:T(8,128)S(1)}, f32[2,2,64,128]{3,2,1,0:T(8,128)S(1)}, u32[]{:S(2)}, u32[]{:S(2)}) collective-permute-start(f32[2,2,64,128]{3,2,1,0:T(8,128)S(1)} %get-tuple-element.64), channel_id=1, source_target_pairs={{0,12},{4,8},{8,4},{12,0},{16,28},{20,24},{24,20},{28,16},{1,13},{... | collective-permute-start | bytes 393224 | tf_op jit(solution)/shard_map/ppermute | solution.py:46
  45.5 0.0 collective-permute-start.13
  45.5 0.6 %collective-permute-start.14 = (f32[2,2,64,128]{3,2,1,0:T(8,128)S(1)}, f32[2,2,64,128]{3,2,1,0:T(8,128)S(1)}, u32[]{:S(2)}, u32[]{:S(2)}) collective-permute-start(f32[2,2,64,128]{3,2,1,0:T(8,128)S(1)} %get-tuple-element.66), channel_id=1, source_target_pairs={{0,4},{4,0},{8,12},{12,8},{16,20},{20,16},{24,28},{28,24},{1,5},{5... | collective-permute-start | bytes 393224 | tf_op jit(solution)/shard_map/ppermute | solution.py:46
  46.2 1.5 %collective-permute-done.15.refs_3_ = f32[288,128]{1,0:T(8,128)S(1)} collective-permute-done((f32[288,128]{1,0:T(8,128)S(1)}, f32[288,128]{1,0:T(8,128)S(1)}, u32[]{:S(2)}, u32[]{:S(2)}) %collective-permute-start.15) | collective-permute-done | bytes 147488 | tf_op jit(solution)/shard_map/ppermute | solution.py:54
  47.6 1.7 %shard_map.73 = (f32[2,64,128]{2,1,0:T(8,128)S(1)}, f32[2,64,128]{2,1,0:T(8,128)S(1)}, f32[2,64,128]{2,1,0:T(8,128)S(1)}, f32[2,64,128]{2,1,0:T(8,128)S(1)}) custom-call(f32[4,2,128,256]{3,2,1,0:T(8,128)S(1)} %get-tuple-element.68.refs_0_, f32[2,4,2,128,128]{4,3,2,1,0:T(8,128)S(1)} %shard_map.62.refs_0_.refs_1_, ...), custom_call_target="tpu_custom_call" | custom-call | bytes 3000000 | tf_op jit(solution)/shard_map/pallas_call | solution.py:31
  49.4 2.6 %collective-permute-start.16 = (f32[2,64,128]{2,1,0:T(8,128)S(1)}, f32[2,64,128]{2,1,0:T(8,128)S(1)}, u32[]{:S(2)}, u32[]{:S(2)}) collective-permute-start(f32[2,64,128]{2,1,0:T(8,128)S(1)} %get-tuple-element.70), channel_id=1, source_target_pairs={{0,12},{4,8},{8,4},{12,0},{16,28},{20,24},{24,20},{28,16},{1,13},{... | collective-permute-start | bytes 196616 | tf_op jit(solution)/shard_map/ppermute | solution.py:46
  52.0 0.0 collective-permute-start.17
  52.0 0.0 collective-permute-done.12.refs_0_
  52.0 0.9 %collective-permute-start.18 = (f32[2,64,128]{2,1,0:T(8,128)S(1)}, f32[2,64,128]{2,1,0:T(8,128)S(1)}, u32[]{:S(2)}, u32[]{:S(2)}) collective-permute-start(f32[2,64,128]{2,1,0:T(8,128)S(1)} %get-tuple-element.72), channel_id=1, source_target_pairs={{0,4},{4,0},{8,12},{12,8},{16,20},{20,16},{24,28},{28,24},{1,5},{5... | collective-permute-start | bytes 196616 | tf_op jit(solution)/shard_map/ppermute | solution.py:46
  52.9 0.0 collective-permute-done.13.refs_1_
  52.9 0.0 collective-permute-done.14.refs_2_
  53.0 0.9 %shard_map.72 = f32[2,2,4,64,128]{4,3,2,1,0:T(8,128)} custom-call(f32[2,2,64,128]{3,2,1,0:T(8,128)S(1)} %collective-permute-done.12.refs_0_, f32[2,2,64,128]{3,2,1,0:T(8,128)S(1)} %collective-permute-done.13.refs_1_, f32[2,2,64,128]{3,2,1,0:T(8,128)S(1)} %collective-permute-done.14.refs_2_, f32[2,2,64,128]{3,2,1,0:T(8,128)S(1)} %get-tuple-element.67.refs_3_), custom_call_target="tpu_custom_call" | custom-call | bytes 3000000 | tf_op jit(solution)/shard_map/pallas_call | solution.py:31
  53.8 0.8 %collective-permute-done.16 = f32[2,64,128]{2,1,0:T(8,128)S(1)} collective-permute-done((f32[2,64,128]{2,1,0:T(8,128)S(1)}, f32[2,64,128]{2,1,0:T(8,128)S(1)}, u32[]{:S(2)}, u32[]{:S(2)}) %collective-permute-start.16) | collective-permute-done | bytes 65568 | tf_op jit(solution)/shard_map/ppermute | solution.py:46
  54.6 1.7 %collective-permute-done.17 = f32[2,64,128]{2,1,0:T(8,128)S(1)} collective-permute-done((f32[2,64,128]{2,1,0:T(8,128)S(1)}, f32[2,64,128]{2,1,0:T(8,128)S(1)}, u32[]{:S(2)}, u32[]{:S(2)}) %collective-permute-start.17) | collective-permute-done | bytes 65568 | tf_op jit(solution)/shard_map/ppermute | solution.py:46
  56.3 0.0 collective-permute-done.18
  56.3 0.6 %add_add_fusion = f32[2,64,128]{2,1,0:T(8,128)} fusion(f32[2,64,128]{2,1,0:T(8,128)S(1)} %collective-permute-done.18, f32[2,64,128]{2,1,0:T(8,128)S(1)} %get-tuple-element.73, f32[2,64,128]{2,1,0:T(8,128)S(1)} %collective-permute-done.16, f32[2,64,128]{2,1,0:T(8,128)S(1)} %collective-permute-done.17), kind=kLoop, calls=%fused_computation.1 | loop fusion | flops 49152 | bytes 327680 | tf_op jit(solution)/shard_map/add | solution.py:575
  (4 shorter events, 0.1 us)
Async XLA Ops:
  0.6 1.1 %copy-start.1 = (f32[2,2,4,64,128]{4,3,2,1,0:T(8,128)S(1)}, f32[2,2,4,64,128]{4,3,2,1,0:T(8,128)}, u32[]{:S(2)}) copy-start(f32[2,2,4,64,128]{4,3,2,1,0:T(8,128)} %refs_0_.3) | copy-start | bytes 1572868
  1.8 4.7 %copy-start = (f32[2,2,4,64,128]{4,3,2,1,0:T(8,128)S(1)}, f32[2,2,4,64,128]{4,3,2,1,0:T(8,128)}, u32[]{:S(2)}) copy-start(f32[2,2,4,64,128]{4,3,2,1,0:T(8,128)} %refs_0_.6) | copy-start | bytes 1572868
  1.8 16.7 %collective-permute-start = (f32[2,2,2,64,128]{4,3,2,1,0:T(8,128)S(1)}, f32[2,2,2,64,128]{4,3,2,1,0:T(8,128)S(1)}, u32[]{:S(2)}, u32[]{:S(2)}) collective-permute-start(f32[2,2,2,64,128]{4,3,2,1,0:T(8,128)S(1)} %get-tuple-element.42), channel_id=1, source_target_pairs={{0,12},{4,8},{8,4},{12,0},{16,28},{20,24},{24,20},{28,16},{1,13},{... | collective-permute-start | bytes 786440 | tf_op jit(solution)/shard_map/ppermute | solution.py:46
  5.9 12.6 %collective-permute-start.1 = (f32[2,2,2,64,128]{4,3,2,1,0:T(8,128)S(1)}, f32[2,2,2,64,128]{4,3,2,1,0:T(8,128)S(1)}, u32[]{:S(2)}, u32[]{:S(2)}) collective-permute-start(f32[2,2,2,64,128]{4,3,2,1,0:T(8,128)S(1)} %get-tuple-element.43.refs_2_), channel_id=1, source_target_pairs={{0,8},{4,12},{8,0},{12,4},{16,24},{20,28},{24,16},{28,20},{1,9},{5... | collective-permute-start | bytes 786440 | tf_op jit(solution)/shard_map/ppermute | solution.py:46
  6.3 12.2 %collective-permute-start.2 = (f32[2,2,2,64,128]{4,3,2,1,0:T(8,128)S(1)}, f32[2,2,2,64,128]{4,3,2,1,0:T(8,128)S(1)}, u32[]{:S(2)}, u32[]{:S(2)}) collective-permute-start(f32[2,2,2,64,128]{4,3,2,1,0:T(8,128)S(1)} %get-tuple-element.44), channel_id=1, source_target_pairs={{0,4},{4,0},{8,12},{12,8},{16,20},{20,16},{24,28},{28,24},{1,5},{5... | collective-permute-start | bytes 786440 | tf_op jit(solution)/shard_map/ppermute | solution.py:46
  6.8 2.0 %collective-permute-start.3 = (f32[2,64,128]{2,1,0:T(8,128)S(1)}, f32[2,64,128]{2,1,0:T(8,128)S(1)}, u32[]{:S(2)}, u32[]{:S(2)}) collective-permute-start(f32[2,64,128]{2,1,0:T(8,128)S(1)} %get-tuple-element.47), channel_id=1, source_target_pairs={{0,1},{1,0},{2,3},{3,2},{4,5},{5,4},{6,7},{7,6},{8,9},{9,8},{10,11... | collective-permute-start | bytes 196616 | tf_op jit(solution)/shard_map/ppermute | solution.py:85
  6.9 11.6 %collective-permute-start.4 = (f32[2,64,128]{2,1,0:T(8,128)S(1)}, f32[2,64,128]{2,1,0:T(8,128)S(1)}, u32[]{:S(2)}, u32[]{:S(2)}) collective-permute-start(f32[2,64,128]{2,1,0:T(8,128)S(1)} %get-tuple-element.48), channel_id=1, source_target_pairs={{1,2},{2,1},{0,4},{3,7},{5,6},{6,5},{4,0},{7,3},{9,10},{10,9},{8,1... | collective-permute-start | bytes 196616 | tf_op jit(solution)/shard_map/ppermute | solution.py:84
  18.8 7.0 %collective-permute-start.5 = (f32[2,2,128,128]{3,2,1,0:T(8,128)S(1)}, f32[2,2,128,128]{3,2,1,0:T(8,128)S(1)}, u32[]{:S(2)}, u32[]{:S(2)}) collective-permute-start(f32[2,2,128,128]{3,2,1,0:T(8,128)S(1)} %shard_map.63), channel_id=1, source_target_pairs={{1,2},{2,1},{0,4},{3,7},{5,6},{6,5},{4,0},{7,3},{9,10},{10,9},{8,1... | collective-permute-start | bytes 786440 | tf_op jit(solution)/shard_map/ppermute | solution.py:84
  21.8 6.1 %collective-permute-start.6 = (f32[2,2,128,128]{3,2,1,0:T(8,128)S(1)}, f32[2,2,128,128]{3,2,1,0:T(8,128)S(1)}, u32[]{:S(2)}, u32[]{:S(2)}) collective-permute-start(f32[2,2,128,128]{3,2,1,0:T(8,128)S(1)} %shard_map.65.refs_3_), channel_id=1, source_target_pairs={{0,1},{1,0},{2,3},{3,2},{4,5},{5,4},{6,7},{7,6},{8,9},{9,8},{10,11... | collective-permute-start | bytes 786440 | tf_op jit(solution)/shard_map/ppermute | solution.py:85
  22.1 13.4 %collective-permute-start.10 = (f32[5,64,128]{2,1,0:T(8,128)S(1)}, f32[5,64,128]{2,1,0:T(8,128)S(1)}, u32[]{:S(2)}, u32[]{:S(2)}) collective-permute-start(f32[5,64,128]{2,1,0:T(8,128)S(1)} %get-tuple-element.58.refs_3_), channel_id=1, source_target_pairs={{0,8},{4,12},{8,0},{12,4},{16,24},{20,28},{24,16},{28,20},{1,9},{5... | collective-permute-start | bytes 491528 | tf_op jit(solution)/shard_map/ppermute | solution.py:46
  23.8 11.7 %collective-permute-start.9 = (f32[5,64,128]{2,1,0:T(8,128)S(1)}, f32[5,64,128]{2,1,0:T(8,128)S(1)}, u32[]{:S(2)}, u32[]{:S(2)}) collective-permute-start(f32[5,64,128]{2,1,0:T(8,128)S(1)} %get-tuple-element.57), channel_id=1, source_target_pairs={{0,12},{4,8},{8,4},{12,0},{16,28},{20,24},{24,20},{28,16},{1,13},{... | collective-permute-start | bytes 491528 | tf_op jit(solution)/shard_map/ppermute | solution.py:46
  24.7 10.8 %collective-permute-start.11 = (f32[5,64,128]{2,1,0:T(8,128)S(1)}, f32[5,64,128]{2,1,0:T(8,128)S(1)}, u32[]{:S(2)}, u32[]{:S(2)}) collective-permute-start(f32[5,64,128]{2,1,0:T(8,128)S(1)} %get-tuple-element.59), channel_id=1, source_target_pairs={{0,4},{4,0},{8,12},{12,8},{16,20},{20,16},{24,28},{28,24},{1,5},{5... | collective-permute-start | bytes 491528 | tf_op jit(solution)/shard_map/ppermute | solution.py:46
  25.8 8.8 %collective-permute-start.7 = (f32[2,128,128]{2,1,0:T(8,128)S(1)}, f32[2,128,128]{2,1,0:T(8,128)S(1)}, u32[]{:S(2)}, u32[]{:S(2)}) collective-permute-start(f32[2,128,128]{2,1,0:T(8,128)S(1)} %shard_map.64.refs_4_), channel_id=1, source_target_pairs={{0,16},{8,24},{16,0},{24,8},{1,17},{9,25},{17,1},{25,9},{2,18},{10... | collective-permute-start | bytes 393224 | tf_op jit(solution)/shard_map/ppermute | solution.py:54
  30.1 8.2 %collective-permute-start.8 = (f32[128,128]{1,0:T(8,128)S(1)}, f32[128,128]{1,0:T(8,128)S(1)}, u32[]{:S(2)}, u32[]{:S(2)}) collective-permute-start(f32[128,128]{1,0:T(8,128)S(1)} %get-tuple-element.54), channel_id=1, source_target_pairs={{0,16},{8,24},{16,0},{24,8},{1,17},{9,25},{17,1},{25,9},{2,18},{10... | collective-permute-start | bytes 196616 | tf_op jit(solution)/shard_map/ppermute | solution.py:54
  38.5 9.2 %collective-permute-start.15 = (f32[288,128]{1,0:T(8,128)S(1)}, f32[288,128]{1,0:T(8,128)S(1)}, u32[]{:S(2)}, u32[]{:S(2)}) collective-permute-start(f32[288,128]{1,0:T(8,128)S(1)} %get-tuple-element.63.refs_1_), channel_id=1, source_target_pairs={{0,16},{8,24},{16,0},{24,8},{1,17},{9,25},{17,1},{25,9},{2,18},{10... | collective-permute-start | bytes 442376 | tf_op jit(solution)/shard_map/ppermute | solution.py:54
  42.5 9.5 %collective-permute-start.12 = (f32[2,2,64,128]{3,2,1,0:T(8,128)S(1)}, f32[2,2,64,128]{3,2,1,0:T(8,128)S(1)}, u32[]{:S(2)}, u32[]{:S(2)}) collective-permute-start(f32[2,2,64,128]{3,2,1,0:T(8,128)S(1)} %get-tuple-element.64), channel_id=1, source_target_pairs={{0,12},{4,8},{8,4},{12,0},{16,28},{20,24},{24,20},{28,16},{1,13},{... | collective-permute-start | bytes 393224 | tf_op jit(solution)/shard_map/ppermute | solution.py:46
  45.5 7.4 %collective-permute-start.13 = (f32[2,2,64,128]{3,2,1,0:T(8,128)S(1)}, f32[2,2,64,128]{3,2,1,0:T(8,128)S(1)}, u32[]{:S(2)}, u32[]{:S(2)}) collective-permute-start(f32[2,2,64,128]{3,2,1,0:T(8,128)S(1)} %get-tuple-element.65), channel_id=1, source_target_pairs={{0,8},{4,12},{8,0},{12,4},{16,24},{20,28},{24,16},{28,20},{1,9},{5... | collective-permute-start | bytes 393224 | tf_op jit(solution)/shard_map/ppermute | solution.py:46
  45.5 7.4 %collective-permute-start.14 = (f32[2,2,64,128]{3,2,1,0:T(8,128)S(1)}, f32[2,2,64,128]{3,2,1,0:T(8,128)S(1)}, u32[]{:S(2)}, u32[]{:S(2)}) collective-permute-start(f32[2,2,64,128]{3,2,1,0:T(8,128)S(1)} %get-tuple-element.66), channel_id=1, source_target_pairs={{0,4},{4,0},{8,12},{12,8},{16,20},{20,16},{24,28},{28,24},{1,5},{5... | collective-permute-start | bytes 393224 | tf_op jit(solution)/shard_map/ppermute | solution.py:46
  49.4 5.2 %collective-permute-start.16 = (f32[2,64,128]{2,1,0:T(8,128)S(1)}, f32[2,64,128]{2,1,0:T(8,128)S(1)}, u32[]{:S(2)}, u32[]{:S(2)}) collective-permute-start(f32[2,64,128]{2,1,0:T(8,128)S(1)} %get-tuple-element.70), channel_id=1, source_target_pairs={{0,12},{4,8},{8,4},{12,0},{16,28},{20,24},{24,20},{28,16},{1,13},{... | collective-permute-start | bytes 196616 | tf_op jit(solution)/shard_map/ppermute | solution.py:46
  52.0 4.3 %collective-permute-start.17 = (f32[2,64,128]{2,1,0:T(8,128)S(1)}, f32[2,64,128]{2,1,0:T(8,128)S(1)}, u32[]{:S(2)}, u32[]{:S(2)}) collective-permute-start(f32[2,64,128]{2,1,0:T(8,128)S(1)} %get-tuple-element.71), channel_id=1, source_target_pairs={{0,8},{4,12},{8,0},{12,4},{16,24},{20,28},{24,16},{28,20},{1,9},{5... | collective-permute-start | bytes 196616 | tf_op jit(solution)/shard_map/ppermute | solution.py:46
  52.0 4.3 %collective-permute-start.18 = (f32[2,64,128]{2,1,0:T(8,128)S(1)}, f32[2,64,128]{2,1,0:T(8,128)S(1)}, u32[]{:S(2)}, u32[]{:S(2)}) collective-permute-start(f32[2,64,128]{2,1,0:T(8,128)S(1)} %get-tuple-element.72), channel_id=1, source_target_pairs={{0,4},{4,0},{8,12},{12,8},{16,20},{20,16},{24,28},{28,24},{1,5},{5... | collective-permute-start | bytes 196616 | tf_op jit(solution)/shard_map/ppermute | solution.py:46

commit v7 on v6

--- a/solution.py
+++ b/solution.py
@@ -223,8 +223,13 @@
     return read
 
 
+def difference(one, two):
+    return lambda z, c, strip: one[z, c, strip, :] - two[z, c, strip, :]
+
+
 def sweep(drive, inverse, out, carry, work, planes, rows, reverse):
-    drive, inverse = beside_each_other(drive), beside_each_other(inverse)
+    drive = drive if callable(drive) else beside_each_other(drive)
+    inverse = beside_each_other(inverse)
     rhs, ping, pong = work
     sign = -1 if reverse else 1
     width = out.shape[-1]
@@ -235,33 +240,33 @@
             buffer[c, rows + 8 : rows + 16, :] = zeros
 
     def beside(buffer, c, r):
-        here = buffer[c, r + 8 : r + 16, :]
+        here = buffer[c, r + 8 : r + 24, :]
         return (
-            buffer[c, r + 7 : r + 15, :]
-            + buffer[c, r + 9 : r + 17, :]
+            buffer[c, r + 7 : r + 23, :]
+            + buffer[c, r + 9 : r + 25, :]
             + (pltpu.roll(here, 1, 1) + pltpu.roll(here, width - 1, 1))
         )
 
     def plane(step, _):
         z = planes - 1 - step if reverse else step
-        for r in range(0, rows, 8):
-            strip = slice(r, r + 8)
+        for r in range(0, rows, 16):
+            strip = slice(r, r + 16)
             a = drive(z, 0, strip) + 2.5 * carry[0, strip, :]
             b = drive(z, 1, strip) + 2.5 * carry[1, strip, :]
             rhs[0, strip, :] = a
             rhs[1, strip, :] = b
             a, b = times(a, b, inverse(z, 0, strip), inverse(z, 1, strip), sign)
-            ping[0, r + 8 : r + 16, :] = a
-            ping[1, r + 8 : r + 16, :] = b
-        for r in range(0, rows, 8):
-            strip = slice(r, r + 8)
+            ping[0, r + 8 : r + 24, :] = a
+            ping[1, r + 8 : r + 24, :] = b
+        for r in range(0, rows, 16):
+            strip = slice(r, r + 16)
             a = rhs[0, strip, :] + beside(ping, 0, r)
             b = rhs[1, strip, :] + beside(ping, 1, r)
             a, b = times(a, b, inverse(z, 0, strip), inverse(z, 1, strip), sign)
-            pong[0, r + 8 : r + 16, :] = a
-            pong[1, r + 8 : r + 16, :] = b
-        for r in range(0, rows, 8):
-            strip = slice(r, r + 8)
+            pong[0, r + 8 : r + 24, :] = a
+            pong[1, r + 8 : r + 24, :] = b
+        for r in range(0, rows, 16):
+            strip = slice(r, r + 16)
             a = rhs[0, strip, :] + beside(pong, 0, r)
             b = rhs[1, strip, :] + beside(pong, 1, r)
             a, b = times(a, b, inverse(z, 0, strip), inverse(z, 1, strip), sign)
@@ -419,7 +424,6 @@
     observed,
     upper_field,
     field,
-    residual,
     adjoint,
     send,
     carry,
@@ -437,19 +441,14 @@
     def _():
         unpack_sides(centre, sides, carry)
         sweep(drive, inverse, field, carry, work, planes, rows, False)
-
-    residual[...] = field[...] - observed[...]
-
-    @pl.when(lower)
-    def _():
         carry[...] = jnp.zeros_like(carry)
-        sweep([residual], inverse, adjoint, carry, work, planes, rows, True)
+        sweep(difference(field, observed), inverse, adjoint, carry, work, planes, rows, True)
         pack_carry(adjoint, 0, send)
 
 
-def adjoint_kernel(height, meta, residual, merged, beside, got, field, lower_adjoint, *rest):
+def adjoint_kernel(height, meta, observed, merged, beside, got, field, lower_adjoint, *rest):
     pieces, (adjoint, carry, *work) = rest[:MEMBERS], rest[MEMBERS:]
-    planes, rows = residual.shape[0], residual.shape[2]
+    planes, rows = field.shape[0], field.shape[2]
     margin = (rows - 2 * height) // 2
     upper = meta[2] == 0
     inverse = [merged.at[1], beside.at[1]]
@@ -471,12 +470,16 @@
     @pl.when(upper)
     def _():
         unpack_carry(got, carry)
-        sweep([residual], inverse, adjoint, carry, work, planes, rows, True)
+        sweep(difference(field, observed), inverse, adjoint, carry, work, planes, rows, True)
         products(adjoint)
 
     @pl.when(jnp.logical_not(upper))
     def _():
         products(lower_adjoint)
+
+
+def sum_kernel(meta, one, two, three, four, out):
+    out[...] = (one[...] + two[...]) + (three[...] + four[...])
 
 
 def field_kernel(meta, *refs):
@@ -545,9 +548,9 @@
         merge_observed_kernel, [(planes, 2, high, 2 * width)], *seen, centre, cost=3_000_000
     )
     seen = seen if one_group else with_row_halo(seen, WIDE)
-    field, residual, adjoint, send = call(
+    field, adjoint, send = call(
         turn_kernel,
-        [whole, whole, whole, (2 * rows + rows // 4, width)],
+        [whole, whole, (2 * rows + rows // 4, width)],
         merged,
         beside,
         centre,
@@ -563,7 +566,7 @@
     sums = call(
         lambda *refs: adjoint_kernel(height, *refs),
         [(own_planes, height, width)] * MEMBERS,
-        residual,
+        seen,
         merged,
         beside,
         got,
@@ -572,7 +575,7 @@
         scratch=[VMEM(whole, F32), *scratch],
     )
     sums = gathered(sums)
-    gradient = (sums[0] + sums[1]) + (sums[2] + sums[3])
+    (gradient,) = call(sum_kernel, [wavenumber.shape], *sums)
     (forward_field,) = call(field_kernel, [source.shape], *pieces)
     return forward_field, gradient
 

time: 57.1 us -> 56.9 us (level)
  other arithmetic: 1.61 us -> 0.96 us
    add x1 -> x0, other arithmetic: 0.65 us -> none  [body(): gradient = sums[0] + sums[1] + (sums[2] + sums[3])]
    pallas_call x15 -> x16, Pallas kernels: 7.42 us -> 7.93 us  [call(): pl.pallas_call(lambda *refs: kernel(position(), *refs), out_shape=[jax.Sh...]
where the time goes in v7:
time: 56.9 us; the launch traced here: 56.8 us
  starting transfers between devices  25.5 us (45%)
  waiting for transfers between devices  21.5 us (38%)
  Pallas kernels  7.93 us (14%)
  other arithmetic  0.96 us (2%)
  between operations  0.8 us (1%)
    ppermute x12, starting transfers between devices, member_swap(): return lax.ppermute(block, ('depth', 'gx'), pairs)  15.5 us
    ppermute x2, waiting for transfers between devices, side_swaps(): got_second = lax.ppermute(second, ('gx', 'gy'), pairs)  9.69 us
    ppermute x3, waiting for transfers between devices, depth_pair_swap(): lax.ppermute(block, 'depth', [(z, z ^ 2) for z in range(lax.axis_size('de...  8.46 us
    pallas_call x16, Pallas kernels, call(): pl.pallas_call(lambda *refs: kernel(position(), *refs), out_shape=[jax.Sh...  7.93 us
    ppermute x3, starting transfers between devices, depth_pair_swap(): lax.ppermute(block, 'depth', [(z, z ^ 2) for z in range(lax.axis_size('de...  6.24 us
    ppermute x2, starting transfers between devices, side_swaps(): got_second = lax.ppermute(second, ('gx', 'gy'), pairs)  3.59 us
    ppermute x12, waiting for transfers between devices, member_swap(): return lax.ppermute(block, ('depth', 'gx'), pairs)  3.35 us
  transfers between devices with their start and end apart: 19, of which 7 were waited for; matrix products, arithmetic and copies ran while one was open for 0% of the time, Pallas kernels for 12%

profile of v7, /device:TPU:0, one launch (start us, length us, event | category | flops | bytes accessed | tf_op | source)
XLA Modules:
  0.0 56.8 jit_solution(2028926254174426603)
XLA Ops:
  0.6 0.0 copy-start.1
  0.6 1.0 %divide_bitcast_fusion = (f32[2,1,64,128]{3,2,1,0:T(8,128)S(1)}, f32[2,1,64,128]{3,2,1,0:T(8,128)S(1)}) fusion(f32[2,64,128]{2,1,0:T(8,128)} %param.7, f32[2,64,128]{2,1,0:T(8,128)} %param.6), kind=kLoop, calls=%fused_computation.2 | loop fusion | flops 114688 | bytes 262144 | tf_op jit(solution)/shard_map/stack | solution.py:294
  1.6 0.1 copy-done.1
  1.8 0.0 copy-start
  1.8 4.0 %collective-permute-start = (f32[2,2,2,64,128]{4,3,2,1,0:T(8,128)S(1)}, f32[2,2,2,64,128]{4,3,2,1,0:T(8,128)S(1)}, u32[]{:S(2)}, u32[]{:S(2)}) collective-permute-start(f32[2,2,2,64,128]{4,3,2,1,0:T(8,128)S(1)} %get-tuple-element.41), channel_id=1, source_target_pairs={{0,12},{4,8},{8,4},{12,0},{16,28},{20,24},{24,20},{28,16},{1,13},{... | collective-permute-start | bytes 786440 | tf_op jit(solution)/shard_map/ppermute | solution.py:46
  5.9 0.4 collective-permute-start.1
  6.3 0.2 collective-permute-start.2
  6.5 0.0 copy-done
  6.5 0.3 shard_map.61
  6.8 0.1 collective-permute-start.3
  6.9 1.9 %collective-permute-start.4 = (f32[2,64,128]{2,1,0:T(8,128)S(1)}, f32[2,64,128]{2,1,0:T(8,128)S(1)}, u32[]{:S(2)}, u32[]{:S(2)}) collective-permute-start(f32[2,64,128]{2,1,0:T(8,128)S(1)} %get-tuple-element.47), channel_id=1, source_target_pairs={{1,2},{2,1},{0,4},{3,7},{5,6},{6,5},{4,0},{7,3},{9,10},{10,9},{8,1... | collective-permute-start | bytes 196616 | tf_op jit(solution)/shard_map/ppermute | solution.py:84
  8.8 0.0 collective-permute-done.3.refs_1_
  8.8 9.7 %collective-permute-done.4.refs_2_ = f32[2,64,128]{2,1,0:T(8,128)S(1)} collective-permute-done((f32[2,64,128]{2,1,0:T(8,128)S(1)}, f32[2,64,128]{2,1,0:T(8,128)S(1)}, u32[]{:S(2)}, u32[]{:S(2)}) %collective-permute-start.4) | collective-permute-done | bytes 65568 | tf_op jit(solution)/shard_map/ppermute | solution.py:84
  18.5 0.0 collective-permute-done.refs_0_
  18.5 0.0 collective-permute-done.1.refs_1_
  18.5 0.0 collective-permute-done.2.refs_2_
  18.5 0.3 shard_map.63
  18.8 1.7 %collective-permute-start.5 = (f32[2,2,128,128]{3,2,1,0:T(8,128)S(1)}, f32[2,2,128,128]{3,2,1,0:T(8,128)S(1)}, u32[]{:S(2)}, u32[]{:S(2)}) collective-permute-start(f32[2,2,128,128]{3,2,1,0:T(8,128)S(1)} %shard_map.63), channel_id=1, source_target_pairs={{1,2},{2,1},{0,4},{3,7},{5,6},{6,5},{4,0},{7,3},{9,10},{10,9},{8,1... | collective-permute-start | bytes 786440 | tf_op jit(solution)/shard_map/ppermute | solution.py:84
  20.5 0.1 shard_map.62.refs_0_.refs_1_
  20.6 0.9 %shard_map.64.refs_4_ = f32[2,128,128]{2,1,0:T(8,128)S(1)} custom-call(f32[2,4,2,128,128]{4,3,2,1,0:T(8,128)S(1)} %shard_map.62.refs_0_.refs_1_), custom_call_target="tpu_custom_call" | custom-call | bytes 3000000 | tf_op jit(solution)/shard_map/pallas_call | solution.py:31
  21.5 0.3 shard_map.65.refs_3_
  21.9 0.1 collective-permute-start.6
  21.9 0.1 shard_map.67
  22.1 1.6 %collective-permute-start.10 = (f32[5,64,128]{2,1,0:T(8,128)S(1)}, f32[5,64,128]{2,1,0:T(8,128)S(1)}, u32[]{:S(2)}, u32[]{:S(2)}) collective-permute-start(f32[5,64,128]{2,1,0:T(8,128)S(1)} %get-tuple-element.57.refs_3_), channel_id=1, source_target_pairs={{0,8},{4,12},{8,0},{12,4},{16,24},{20,28},{24,16},{28,20},{1,9},{5... | collective-permute-start | bytes 491528 | tf_op jit(solution)/shard_map/ppermute | solution.py:46
  23.7 0.1 shard_map.68
  23.8 0.9 %collective-permute-start.9 = (f32[5,64,128]{2,1,0:T(8,128)S(1)}, f32[5,64,128]{2,1,0:T(8,128)S(1)}, u32[]{:S(2)}, u32[]{:S(2)}) collective-permute-start(f32[5,64,128]{2,1,0:T(8,128)S(1)} %get-tuple-element.56), channel_id=1, source_target_pairs={{0,12},{4,8},{8,4},{12,0},{16,28},{20,24},{24,20},{28,16},{1,13},{... | collective-permute-start | bytes 491528 | tf_op jit(solution)/shard_map/ppermute | solution.py:46
  24.7 1.1 %collective-permute-start.11 = (f32[5,64,128]{2,1,0:T(8,128)S(1)}, f32[5,64,128]{2,1,0:T(8,128)S(1)}, u32[]{:S(2)}, u32[]{:S(2)}) collective-permute-start(f32[5,64,128]{2,1,0:T(8,128)S(1)} %get-tuple-element.58), channel_id=1, source_target_pairs={{0,4},{4,0},{8,12},{12,8},{16,20},{20,16},{24,28},{28,24},{1,5},{5... | collective-permute-start | bytes 491528 | tf_op jit(solution)/shard_map/ppermute | solution.py:46
  25.8 0.0 collective-permute-done.5.refs_1_
  25.8 2.2 %collective-permute-start.7 = (f32[2,128,128]{2,1,0:T(8,128)S(1)}, f32[2,128,128]{2,1,0:T(8,128)S(1)}, u32[]{:S(2)}, u32[]{:S(2)}) collective-permute-start(f32[2,128,128]{2,1,0:T(8,128)S(1)} %shard_map.64.refs_4_), channel_id=1, source_target_pairs={{0,16},{8,24},{16,0},{24,8},{1,17},{9,25},{17,1},{25,9},{2,18},{10... | collective-permute-start | bytes 393224 | tf_op jit(solution)/shard_map/ppermute | solution.py:54
  28.0 0.0 collective-permute-done.6.refs_2_
  28.0 2.1 %shard_map.66 = (f32[2,4,2,128,128]{4,3,2,1,0:T(8,128)S(1)}, f32[4,2,128,256]{3,2,1,0:T(8,128)S(1)}, f32[128,128]{1,0:T(8,128)S(1)}) custom-call(f32[2,4,2,128,128]{4,3,2,1,0:T(8,128)S(1)} %shard_map.62.refs_0_.refs_1_, f32[2,2,128,128]{3,2,1,0:T(8,128)S(1)} %collective-permute-done.5.refs_1_, f32[2,2,128,128]{3,2,1,0:T(8,128)S(1)} %collective-permute-done.6.refs_2_), custom_call_target="tpu_custom_call" | custom-call | bytes 30000000 | tf_op jit(solution)/shard_map/pallas_call | solution.py:31
  30.1 0.1 collective-permute-start.8
  30.2 4.5 %collective-permute-done.7.refs_4_.refs_2_ = f32[2,128,128]{2,1,0:T(8,128)S(1)} collective-permute-done((f32[2,128,128]{2,1,0:T(8,128)S(1)}, f32[2,128,128]{2,1,0:T(8,128)S(1)}, u32[]{:S(2)}, u32[]{:S(2)}) %collective-permute-start.7) | collective-permute-done | bytes 131104 | tf_op jit(solution)/shard_map/ppermute | solution.py:54
  34.6 0.9 %collective-permute-done.9.refs_0_ = f32[5,64,128]{2,1,0:T(8,128)S(1)} collective-permute-done((f32[5,64,128]{2,1,0:T(8,128)S(1)}, f32[5,64,128]{2,1,0:T(8,128)S(1)}, u32[]{:S(2)}, u32[]{:S(2)}) %collective-permute-start.9) | collective-permute-done | bytes 163872 | tf_op jit(solution)/shard_map/ppermute | solution.py:46
  35.5 0.0 collective-permute-done.10.refs_1_
  35.5 0.0 collective-permute-done.11.refs_2_
  35.5 0.3 shard_map.69.refs_4_.refs_0_
  35.8 2.5 %collective-permute-done.8.refs_3_ = f32[128,128]{1,0:T(8,128)S(1)} collective-permute-done((f32[128,128]{1,0:T(8,128)S(1)}, f32[128,128]{1,0:T(8,128)S(1)}, u32[]{:S(2)}, u32[]{:S(2)}) %collective-permute-start.8) | collective-permute-done | bytes 65568 | tf_op jit(solution)/shard_map/ppermute | solution.py:54
  38.3 0.1 shard_map.70
  38.4 4.0 %collective-permute-start.15 = (f32[288,128]{1,0:T(8,128)S(1)}, f32[288,128]{1,0:T(8,128)S(1)}, u32[]{:S(2)}, u32[]{:S(2)}) collective-permute-start(f32[288,128]{1,0:T(8,128)S(1)} %get-tuple-element.62.refs_1_), channel_id=1, source_target_pairs={{0,16},{8,24},{16,0},{24,8},{1,17},{9,25},{17,1},{25,9},{2,18},{10... | collective-permute-start | bytes 442376 | tf_op jit(solution)/shard_map/ppermute | solution.py:54
  42.4 3.0 %collective-permute-start.12 = (f32[2,2,64,128]{3,2,1,0:T(8,128)S(1)}, f32[2,2,64,128]{3,2,1,0:T(8,128)S(1)}, u32[]{:S(2)}, u32[]{:S(2)}) collective-permute-start(f32[2,2,64,128]{3,2,1,0:T(8,128)S(1)} %get-tuple-element.63), channel_id=1, source_target_pairs={{0,12},{4,8},{8,4},{12,0},{16,28},{20,24},{24,20},{28,16},{1,13},{... | collective-permute-start | bytes 393224 | tf_op jit(solution)/shard_map/ppermute | solution.py:46
  45.4 0.0 collective-permute-start.13
  45.4 0.6 %collective-permute-start.14 = (f32[2,2,64,128]{3,2,1,0:T(8,128)S(1)}, f32[2,2,64,128]{3,2,1,0:T(8,128)S(1)}, u32[]{:S(2)}, u32[]{:S(2)}) collective-permute-start(f32[2,2,64,128]{3,2,1,0:T(8,128)S(1)} %get-tuple-element.65), channel_id=1, source_target_pairs={{0,4},{4,0},{8,12},{12,8},{16,20},{20,16},{24,28},{28,24},{1,5},{5... | collective-permute-start | bytes 393224 | tf_op jit(solution)/shard_map/ppermute | solution.py:46
  46.1 1.5 %collective-permute-done.15.refs_3_ = f32[288,128]{1,0:T(8,128)S(1)} collective-permute-done((f32[288,128]{1,0:T(8,128)S(1)}, f32[288,128]{1,0:T(8,128)S(1)}, u32[]{:S(2)}, u32[]{:S(2)}) %collective-permute-start.15) | collective-permute-done | bytes 147488 | tf_op jit(solution)/shard_map/ppermute | solution.py:54
  47.5 1.7 %shard_map.73 = (f32[2,64,128]{2,1,0:T(8,128)S(1)}, f32[2,64,128]{2,1,0:T(8,128)S(1)}, f32[2,64,128]{2,1,0:T(8,128)S(1)}, f32[2,64,128]{2,1,0:T(8,128)S(1)}) custom-call(f32[4,2,128,256]{3,2,1,0:T(8,128)S(1)} %shard_map.69.refs_4_.refs_0_, f32[2,4,2,128,128]{4,3,2,1,0:T(8,128)S(1)} %shard_map.62.refs_0_.refs_1_, ...), custom_call_target="tpu_custom_call" | custom-call | bytes 3000000 | tf_op jit(solution)/shard_map/pallas_call | solution.py:31
  49.3 2.6 %collective-permute-start.16 = (f32[2,64,128]{2,1,0:T(8,128)S(1)}, f32[2,64,128]{2,1,0:T(8,128)S(1)}, u32[]{:S(2)}, u32[]{:S(2)}) collective-permute-start(f32[2,64,128]{2,1,0:T(8,128)S(1)} %get-tuple-element.68), channel_id=1, source_target_pairs={{0,12},{4,8},{8,4},{12,0},{16,28},{20,24},{24,20},{28,16},{1,13},{... | collective-permute-start | bytes 196616 | tf_op jit(solution)/shard_map/ppermute | solution.py:46
  51.9 0.0 collective-permute-start.17
  51.9 0.0 collective-permute-done.12.refs_0_
  51.9 0.9 %collective-permute-start.18 = (f32[2,64,128]{2,1,0:T(8,128)S(1)}, f32[2,64,128]{2,1,0:T(8,128)S(1)}, u32[]{:S(2)}, u32[]{:S(2)}) collective-permute-start(f32[2,64,128]{2,1,0:T(8,128)S(1)} %get-tuple-element.70), channel_id=1, source_target_pairs={{0,4},{4,0},{8,12},{12,8},{16,20},{20,16},{24,28},{28,24},{1,5},{5... | collective-permute-start | bytes 196616 | tf_op jit(solution)/shard_map/ppermute | solution.py:46
  52.8 0.0 collective-permute-done.13.refs_1_
  52.8 0.0 collective-permute-done.14.refs_2_
  52.8 0.9 %shard_map.72 = f32[2,2,4,64,128]{4,3,2,1,0:T(8,128)} custom-call(f32[2,2,64,128]{3,2,1,0:T(8,128)S(1)} %collective-permute-done.12.refs_0_, f32[2,2,64,128]{3,2,1,0:T(8,128)S(1)} %collective-permute-done.13.refs_1_, f32[2,2,64,128]{3,2,1,0:T(8,128)S(1)} %collective-permute-done.14.refs_2_, f32[2,2,64,128]{3,2,1,0:T(8,128)S(1)} %get-tuple-element.66.refs_3_), custom_call_target="tpu_custom_call" | custom-call | bytes 3000000 | tf_op jit(solution)/shard_map/pallas_call | solution.py:31
  53.7 0.8 %collective-permute-done.16.refs_0_ = f32[2,64,128]{2,1,0:T(8,128)S(1)} collective-permute-done((f32[2,64,128]{2,1,0:T(8,128)S(1)}, f32[2,64,128]{2,1,0:T(8,128)S(1)}, u32[]{:S(2)}, u32[]{:S(2)}) %collective-permute-start.16) | collective-permute-done | bytes 65568 | tf_op jit(solution)/shard_map/ppermute | solution.py:46
  54.5 1.6 %collective-permute-done.17.refs_1_ = f32[2,64,128]{2,1,0:T(8,128)S(1)} collective-permute-done((f32[2,64,128]{2,1,0:T(8,128)S(1)}, f32[2,64,128]{2,1,0:T(8,128)S(1)}, u32[]{:S(2)}, u32[]{:S(2)}) %collective-permute-start.17) | collective-permute-done | bytes 65568 | tf_op jit(solution)/shard_map/ppermute | solution.py:46
  56.1 0.0 collective-permute-done.18.refs_2_
  56.1 0.6 %shard_map.74 = f32[2,64,128]{2,1,0:T(8,128)} custom-call(f32[2,64,128]{2,1,0:T(8,128)S(1)} %collective-permute-done.16.refs_0_, f32[2,64,128]{2,1,0:T(8,128)S(1)} %collective-permute-done.17.refs_1_, f32[2,64,128]{2,1,0:T(8,128)S(1)} %collective-permute-done.18.refs_2_, f32[2,64,128]{2,1,0:T(8,128)S(1)} %get-tuple-element.71.refs_3_), custom_call_target="tpu_custom_call" | custom-call | bytes 3000000 | tf_op jit(solution)/shard_map/pallas_call | solution.py:31
  (4 shorter events, 0.1 us)
Async XLA Ops:
  0.6 1.1 %copy-start.1 = (f32[2,2,4,64,128]{4,3,2,1,0:T(8,128)S(1)}, f32[2,2,4,64,128]{4,3,2,1,0:T(8,128)}, u32[]{:S(2)}) copy-start(f32[2,2,4,64,128]{4,3,2,1,0:T(8,128)} %refs_0_.3) | copy-start | bytes 1572868
  1.8 4.7 %copy-start = (f32[2,2,4,64,128]{4,3,2,1,0:T(8,128)S(1)}, f32[2,2,4,64,128]{4,3,2,1,0:T(8,128)}, u32[]{:S(2)}) copy-start(f32[2,2,4,64,128]{4,3,2,1,0:T(8,128)} %refs_0_.6) | copy-start | bytes 1572868
  1.8 16.7 %collective-permute-start = (f32[2,2,2,64,128]{4,3,2,1,0:T(8,128)S(1)}, f32[2,2,2,64,128]{4,3,2,1,0:T(8,128)S(1)}, u32[]{:S(2)}, u32[]{:S(2)}) collective-permute-start(f32[2,2,2,64,128]{4,3,2,1,0:T(8,128)S(1)} %get-tuple-element.41), channel_id=1, source_target_pairs={{0,12},{4,8},{8,4},{12,0},{16,28},{20,24},{24,20},{28,16},{1,13},{... | collective-permute-start | bytes 786440 | tf_op jit(solution)/shard_map/ppermute | solution.py:46
  5.9 12.6 %collective-permute-start.1 = (f32[2,2,2,64,128]{4,3,2,1,0:T(8,128)S(1)}, f32[2,2,2,64,128]{4,3,2,1,0:T(8,128)S(1)}, u32[]{:S(2)}, u32[]{:S(2)}) collective-permute-start(f32[2,2,2,64,128]{4,3,2,1,0:T(8,128)S(1)} %get-tuple-element.42.refs_2_), channel_id=1, source_target_pairs={{0,8},{4,12},{8,0},{12,4},{16,24},{20,28},{24,16},{28,20},{1,9},{5... | collective-permute-start | bytes 786440 | tf_op jit(solution)/shard_map/ppermute | solution.py:46
  6.3 12.2 %collective-permute-start.2 = (f32[2,2,2,64,128]{4,3,2,1,0:T(8,128)S(1)}, f32[2,2,2,64,128]{4,3,2,1,0:T(8,128)S(1)}, u32[]{:S(2)}, u32[]{:S(2)}) collective-permute-start(f32[2,2,2,64,128]{4,3,2,1,0:T(8,128)S(1)} %get-tuple-element.43), channel_id=1, source_target_pairs={{0,4},{4,0},{8,12},{12,8},{16,20},{20,16},{24,28},{28,24},{1,5},{5... | collective-permute-start | bytes 786440 | tf_op jit(solution)/shard_map/ppermute | solution.py:46
  6.8 2.0 %collective-permute-start.3 = (f32[2,64,128]{2,1,0:T(8,128)S(1)}, f32[2,64,128]{2,1,0:T(8,128)S(1)}, u32[]{:S(2)}, u32[]{:S(2)}) collective-permute-start(f32[2,64,128]{2,1,0:T(8,128)S(1)} %get-tuple-element.46), channel_id=1, source_target_pairs={{0,1},{1,0},{2,3},{3,2},{4,5},{5,4},{6,7},{7,6},{8,9},{9,8},{10,11... | collective-permute-start | bytes 196616 | tf_op jit(solution)/shard_map/ppermute | solution.py:85
  6.9 11.6 %collective-permute-start.4 = (f32[2,64,128]{2,1,0:T(8,128)S(1)}, f32[2,64,128]{2,1,0:T(8,128)S(1)}, u32[]{:S(2)}, u32[]{:S(2)}) collective-permute-start(f32[2,64,128]{2,1,0:T(8,128)S(1)} %get-tuple-element.47), channel_id=1, source_target_pairs={{1,2},{2,1},{0,4},{3,7},{5,6},{6,5},{4,0},{7,3},{9,10},{10,9},{8,1... | collective-permute-start | bytes 196616 | tf_op jit(solution)/shard_map/ppermute | solution.py:84
  18.8 7.0 %collective-permute-start.5 = (f32[2,2,128,128]{3,2,1,0:T(8,128)S(1)}, f32[2,2,128,128]{3,2,1,0:T(8,128)S(1)}, u32[]{:S(2)}, u32[]{:S(2)}) collective-permute-start(f32[2,2,128,128]{3,2,1,0:T(8,128)S(1)} %shard_map.63), channel_id=1, source_target_pairs={{1,2},{2,1},{0,4},{3,7},{5,6},{6,5},{4,0},{7,3},{9,10},{10,9},{8,1... | collective-permute-start | bytes 786440 | tf_op jit(solution)/shard_map/ppermute | solution.py:84
  21.9 6.1 %collective-permute-start.6 = (f32[2,2,128,128]{3,2,1,0:T(8,128)S(1)}, f32[2,2,128,128]{3,2,1,0:T(8,128)S(1)}, u32[]{:S(2)}, u32[]{:S(2)}) collective-permute-start(f32[2,2,128,128]{3,2,1,0:T(8,128)S(1)} %shard_map.65.refs_3_), channel_id=1, source_target_pairs={{0,1},{1,0},{2,3},{3,2},{4,5},{5,4},{6,7},{7,6},{8,9},{9,8},{10,11... | collective-permute-start | bytes 786440 | tf_op jit(solution)/shard_map/ppermute | solution.py:85
  22.1 13.4 %collective-permute-start.10 = (f32[5,64,128]{2,1,0:T(8,128)S(1)}, f32[5,64,128]{2,1,0:T(8,128)S(1)}, u32[]{:S(2)}, u32[]{:S(2)}) collective-permute-start(f32[5,64,128]{2,1,0:T(8,128)S(1)} %get-tuple-element.57.refs_3_), channel_id=1, source_target_pairs={{0,8},{4,12},{8,0},{12,4},{16,24},{20,28},{24,16},{28,20},{1,9},{5... | collective-permute-start | bytes 491528 | tf_op jit(solution)/shard_map/ppermute | solution.py:46
  23.8 11.7 %collective-permute-start.9 = (f32[5,64,128]{2,1,0:T(8,128)S(1)}, f32[5,64,128]{2,1,0:T(8,128)S(1)}, u32[]{:S(2)}, u32[]{:S(2)}) collective-permute-start(f32[5,64,128]{2,1,0:T(8,128)S(1)} %get-tuple-element.56), channel_id=1, source_target_pairs={{0,12},{4,8},{8,4},{12,0},{16,28},{20,24},{24,20},{28,16},{1,13},{... | collective-permute-start | bytes 491528 | tf_op jit(solution)/shard_map/ppermute | solution.py:46
  24.7 10.8 %collective-permute-start.11 = (f32[5,64,128]{2,1,0:T(8,128)S(1)}, f32[5,64,128]{2,1,0:T(8,128)S(1)}, u32[]{:S(2)}, u32[]{:S(2)}) collective-permute-start(f32[5,64,128]{2,1,0:T(8,128)S(1)} %get-tuple-element.58), channel_id=1, source_target_pairs={{0,4},{4,0},{8,12},{12,8},{16,20},{20,16},{24,28},{28,24},{1,5},{5... | collective-permute-start | bytes 491528 | tf_op jit(solution)/shard_map/ppermute | solution.py:46
  25.8 8.8 %collective-permute-start.7 = (f32[2,128,128]{2,1,0:T(8,128)S(1)}, f32[2,128,128]{2,1,0:T(8,128)S(1)}, u32[]{:S(2)}, u32[]{:S(2)}) collective-permute-start(f32[2,128,128]{2,1,0:T(8,128)S(1)} %shard_map.64.refs_4_), channel_id=1, source_target_pairs={{0,16},{8,24},{16,0},{24,8},{1,17},{9,25},{17,1},{25,9},{2,18},{10... | collective-permute-start | bytes 393224 | tf_op jit(solution)/shard_map/ppermute | solution.py:54
  30.1 8.2 %collective-permute-start.8 = (f32[128,128]{1,0:T(8,128)S(1)}, f32[128,128]{1,0:T(8,128)S(1)}, u32[]{:S(2)}, u32[]{:S(2)}) collective-permute-start(f32[128,128]{1,0:T(8,128)S(1)} %get-tuple-element.53), channel_id=1, source_target_pairs={{0,16},{8,24},{16,0},{24,8},{1,17},{9,25},{17,1},{25,9},{2,18},{10... | collective-permute-start | bytes 196616 | tf_op jit(solution)/shard_map/ppermute | solution.py:54
  38.4 9.2 %collective-permute-start.15 = (f32[288,128]{1,0:T(8,128)S(1)}, f32[288,128]{1,0:T(8,128)S(1)}, u32[]{:S(2)}, u32[]{:S(2)}) collective-permute-start(f32[288,128]{1,0:T(8,128)S(1)} %get-tuple-element.62.refs_1_), channel_id=1, source_target_pairs={{0,16},{8,24},{16,0},{24,8},{1,17},{9,25},{17,1},{25,9},{2,18},{10... | collective-permute-start | bytes 442376 | tf_op jit(solution)/shard_map/ppermute | solution.py:54
  42.4 9.4 %collective-permute-start.12 = (f32[2,2,64,128]{3,2,1,0:T(8,128)S(1)}, f32[2,2,64,128]{3,2,1,0:T(8,128)S(1)}, u32[]{:S(2)}, u32[]{:S(2)}) collective-permute-start(f32[2,2,64,128]{3,2,1,0:T(8,128)S(1)} %get-tuple-element.63), channel_id=1, source_target_pairs={{0,12},{4,8},{8,4},{12,0},{16,28},{20,24},{24,20},{28,16},{1,13},{... | collective-permute-start | bytes 393224 | tf_op jit(solution)/shard_map/ppermute | solution.py:46
  45.4 7.4 %collective-permute-start.13 = (f32[2,2,64,128]{3,2,1,0:T(8,128)S(1)}, f32[2,2,64,128]{3,2,1,0:T(8,128)S(1)}, u32[]{:S(2)}, u32[]{:S(2)}) collective-permute-start(f32[2,2,64,128]{3,2,1,0:T(8,128)S(1)} %get-tuple-element.64), channel_id=1, source_target_pairs={{0,8},{4,12},{8,0},{12,4},{16,24},{20,28},{24,16},{28,20},{1,9},{5... | collective-permute-start | bytes 393224 | tf_op jit(solution)/shard_map/ppermute | solution.py:46
  45.4 7.4 %collective-permute-start.14 = (f32[2,2,64,128]{3,2,1,0:T(8,128)S(1)}, f32[2,2,64,128]{3,2,1,0:T(8,128)S(1)}, u32[]{:S(2)}, u32[]{:S(2)}) collective-permute-start(f32[2,2,64,128]{3,2,1,0:T(8,128)S(1)} %get-tuple-element.65), channel_id=1, source_target_pairs={{0,4},{4,0},{8,12},{12,8},{16,20},{20,16},{24,28},{28,24},{1,5},{5... | collective-permute-start | bytes 393224 | tf_op jit(solution)/shard_map/ppermute | solution.py:46
  49.3 5.2 %collective-permute-start.16 = (f32[2,64,128]{2,1,0:T(8,128)S(1)}, f32[2,64,128]{2,1,0:T(8,128)S(1)}, u32[]{:S(2)}, u32[]{:S(2)}) collective-permute-start(f32[2,64,128]{2,1,0:T(8,128)S(1)} %get-tuple-element.68), channel_id=1, source_target_pairs={{0,12},{4,8},{8,4},{12,0},{16,28},{20,24},{24,20},{28,16},{1,13},{... | collective-permute-start | bytes 196616 | tf_op jit(solution)/shard_map/ppermute | solution.py:46
  51.9 4.3 %collective-permute-start.17 = (f32[2,64,128]{2,1,0:T(8,128)S(1)}, f32[2,64,128]{2,1,0:T(8,128)S(1)}, u32[]{:S(2)}, u32[]{:S(2)}) collective-permute-start(f32[2,64,128]{2,1,0:T(8,128)S(1)} %get-tuple-element.69), channel_id=1, source_target_pairs={{0,8},{4,12},{8,0},{12,4},{16,24},{20,28},{24,16},{28,20},{1,9},{5... | collective-permute-start | bytes 196616 | tf_op jit(solution)/shard_map/ppermute | solution.py:46
  51.9 4.3 %collective-permute-start.18 = (f32[2,64,128]{2,1,0:T(8,128)S(1)}, f32[2,64,128]{2,1,0:T(8,128)S(1)}, u32[]{:S(2)}, u32[]{:S(2)}) collective-permute-start(f32[2,64,128]{2,1,0:T(8,128)S(1)} %get-tuple-element.70), channel_id=1, source_target_pairs={{0,4},{4,0},{8,12},{12,8},{16,20},{20,16},{24,28},{28,24},{1,5},{5... | collective-permute-start | bytes 196616 | tf_op jit(solution)/shard_map/ppermute | solution.py:46

commit v8 on v7

--- a/solution.py
+++ b/solution.py
@@ -276,7 +276,7 @@
             carry[1, strip, :] = b
         return 0
 
-    lax.fori_loop(0, planes, plane, 0)
+    lax.fori_loop(0, planes, plane, 0, unroll=True)
 
 
 def sweep_scratch(rows, wide=2 * LANES):

time: 56.9 us -> 56.9 us (level)
  no operation moved by 1% of the time
where the time goes in v8:
time: 56.9 us; the launch traced here: 56.7 us
  starting transfers between devices  25.8 us (45%)
  waiting for transfers between devices  21.4 us (38%)
  Pallas kernels  7.67 us (13%)
  other arithmetic  0.96 us (2%)
  between operations  0.8 us (1%)
    ppermute x12, starting transfers between devices, member_swap(): return lax.ppermute(block, ('depth', 'gx'), pairs)  15.8 us
    ppermute x2, waiting for transfers between devices, side_swaps(): got_second = lax.ppermute(second, ('gx', 'gy'), pairs)  9.69 us
    ppermute x3, waiting for transfers between devices, depth_pair_swap(): lax.ppermute(block, 'depth', [(z, z ^ 2) for z in range(lax.axis_size('de...  8 us
    pallas_call x16, Pallas kernels, call(): pl.pallas_call(lambda *refs: kernel(position(), *refs), out_shape=[jax.Sh...  7.67 us
    ppermute x3, starting transfers between devices, depth_pair_swap(): lax.ppermute(block, 'depth', [(z, z ^ 2) for z in range(lax.axis_size('de...  6.2 us
    ppermute x12, waiting for transfers between devices, member_swap(): return lax.ppermute(block, ('depth', 'gx'), pairs)  3.67 us
    ppermute x2, starting transfers between devices, side_swaps(): got_second = lax.ppermute(second, ('gx', 'gy'), pairs)  3.59 us
  transfers between devices with their start and end apart: 19, of which 7 were waited for; matrix products, arithmetic and copies ran while one was open for 0% of the time, Pallas kernels for 12%

profile of v8, /device:TPU:0, one launch (start us, length us, event | category | flops | bytes accessed | tf_op | source)
XLA Modules:
  0.0 56.7 jit_solution(15743030664536378536)
XLA Ops:
  0.6 0.0 copy-start.1
  0.6 1.0 %divide_bitcast_fusion = (f32[2,1,64,128]{3,2,1,0:T(8,128)S(1)}, f32[2,1,64,128]{3,2,1,0:T(8,128)S(1)}) fusion(f32[2,64,128]{2,1,0:T(8,128)} %param.7, f32[2,64,128]{2,1,0:T(8,128)} %param.6), kind=kLoop, calls=%fused_computation.2 | loop fusion | flops 114688 | bytes 262144 | tf_op jit(solution)/shard_map/stack | solution.py:294
  1.6 0.1 copy-done.1
  1.8 0.0 copy-start
  1.8 4.0 %collective-permute-start = (f32[2,2,2,64,128]{4,3,2,1,0:T(8,128)S(1)}, f32[2,2,2,64,128]{4,3,2,1,0:T(8,128)S(1)}, u32[]{:S(2)}, u32[]{:S(2)}) collective-permute-start(f32[2,2,2,64,128]{4,3,2,1,0:T(8,128)S(1)} %get-tuple-element.41), channel_id=1, source_target_pairs={{0,12},{4,8},{8,4},{12,0},{16,28},{20,24},{24,20},{28,16},{1,13},{... | collective-permute-start | bytes 786440 | tf_op jit(solution)/shard_map/ppermute | solution.py:46
  5.9 0.4 collective-permute-start.1
  6.3 0.2 collective-permute-start.2
  6.5 0.0 copy-done
  6.5 0.3 shard_map.61
  6.8 0.1 collective-permute-start.3
  6.9 1.9 %collective-permute-start.4 = (f32[2,64,128]{2,1,0:T(8,128)S(1)}, f32[2,64,128]{2,1,0:T(8,128)S(1)}, u32[]{:S(2)}, u32[]{:S(2)}) collective-permute-start(f32[2,64,128]{2,1,0:T(8,128)S(1)} %get-tuple-element.47), channel_id=1, source_target_pairs={{1,2},{2,1},{0,4},{3,7},{5,6},{6,5},{4,0},{7,3},{9,10},{10,9},{8,1... | collective-permute-start | bytes 196616 | tf_op jit(solution)/shard_map/ppermute | solution.py:84
  8.8 0.0 collective-permute-done.3.refs_1_
  8.8 9.7 %collective-permute-done.4.refs_2_ = f32[2,64,128]{2,1,0:T(8,128)S(1)} collective-permute-done((f32[2,64,128]{2,1,0:T(8,128)S(1)}, f32[2,64,128]{2,1,0:T(8,128)S(1)}, u32[]{:S(2)}, u32[]{:S(2)}) %collective-permute-start.4) | collective-permute-done | bytes 65568 | tf_op jit(solution)/shard_map/ppermute | solution.py:84
  18.5 0.0 collective-permute-done.refs_0_
  18.5 0.0 collective-permute-done.1.refs_1_
  18.5 0.0 collective-permute-done.2.refs_2_
  18.5 0.3 shard_map.63
  18.8 1.7 %collective-permute-start.5 = (f32[2,2,128,128]{3,2,1,0:T(8,128)S(1)}, f32[2,2,128,128]{3,2,1,0:T(8,128)S(1)}, u32[]{:S(2)}, u32[]{:S(2)}) collective-permute-start(f32[2,2,128,128]{3,2,1,0:T(8,128)S(1)} %shard_map.63), channel_id=1, source_target_pairs={{1,2},{2,1},{0,4},{3,7},{5,6},{6,5},{4,0},{7,3},{9,10},{10,9},{8,1... | collective-permute-start | bytes 786440 | tf_op jit(solution)/shard_map/ppermute | solution.py:84
  20.5 0.1 shard_map.62.refs_0_.refs_1_
  20.6 0.7 %shard_map.64.refs_4_ = f32[2,128,128]{2,1,0:T(8,128)S(1)} custom-call(f32[2,4,2,128,128]{4,3,2,1,0:T(8,128)S(1)} %shard_map.62.refs_0_.refs_1_), custom_call_target="tpu_custom_call" | custom-call | bytes 3000000 | tf_op jit(solution)/shard_map/pallas_call | solution.py:31
  21.3 0.3 shard_map.65.refs_3_
  21.7 0.1 collective-permute-start.6
  21.7 0.1 shard_map.67
  21.9 1.6 %collective-permute-start.10 = (f32[5,64,128]{2,1,0:T(8,128)S(1)}, f32[5,64,128]{2,1,0:T(8,128)S(1)}, u32[]{:S(2)}, u32[]{:S(2)}) collective-permute-start(f32[5,64,128]{2,1,0:T(8,128)S(1)} %get-tuple-element.57.refs_3_), channel_id=1, source_target_pairs={{0,8},{4,12},{8,0},{12,4},{16,24},{20,28},{24,16},{28,20},{1,9},{5... | collective-permute-start | bytes 491528 | tf_op jit(solution)/shard_map/ppermute | solution.py:46
  23.5 0.1 shard_map.68
  23.6 0.9 %collective-permute-start.9 = (f32[5,64,128]{2,1,0:T(8,128)S(1)}, f32[5,64,128]{2,1,0:T(8,128)S(1)}, u32[]{:S(2)}, u32[]{:S(2)}) collective-permute-start(f32[5,64,128]{2,1,0:T(8,128)S(1)} %get-tuple-element.56), channel_id=1, source_target_pairs={{0,12},{4,8},{8,4},{12,0},{16,28},{20,24},{24,20},{28,16},{1,13},{... | collective-permute-start | bytes 491528 | tf_op jit(solution)/shard_map/ppermute | solution.py:46
  24.5 1.1 %collective-permute-start.11 = (f32[5,64,128]{2,1,0:T(8,128)S(1)}, f32[5,64,128]{2,1,0:T(8,128)S(1)}, u32[]{:S(2)}, u32[]{:S(2)}) collective-permute-start(f32[5,64,128]{2,1,0:T(8,128)S(1)} %get-tuple-element.58), channel_id=1, source_target_pairs={{0,4},{4,0},{8,12},{12,8},{16,20},{20,16},{24,28},{28,24},{1,5},{5... | collective-permute-start | bytes 491528 | tf_op jit(solution)/shard_map/ppermute | solution.py:46
  25.6 0.0 collective-permute-done.5.refs_1_
  25.6 2.4 %collective-permute-start.7 = (f32[2,128,128]{2,1,0:T(8,128)S(1)}, f32[2,128,128]{2,1,0:T(8,128)S(1)}, u32[]{:S(2)}, u32[]{:S(2)}) collective-permute-start(f32[2,128,128]{2,1,0:T(8,128)S(1)} %shard_map.64.refs_4_), channel_id=1, source_target_pairs={{0,16},{8,24},{16,0},{24,8},{1,17},{9,25},{17,1},{25,9},{2,18},{10... | collective-permute-start | bytes 393224 | tf_op jit(solution)/shard_map/ppermute | solution.py:54
  28.0 0.0 collective-permute-done.6.refs_2_
  28.0 2.1 %shard_map.66 = (f32[2,4,2,128,128]{4,3,2,1,0:T(8,128)S(1)}, f32[4,2,128,256]{3,2,1,0:T(8,128)S(1)}, f32[128,128]{1,0:T(8,128)S(1)}) custom-call(f32[2,4,2,128,128]{4,3,2,1,0:T(8,128)S(1)} %shard_map.62.refs_0_.refs_1_, f32[2,2,128,128]{3,2,1,0:T(8,128)S(1)} %collective-permute-done.5.refs_1_, f32[2,2,128,128]{3,2,1,0:T(8,128)S(1)} %collective-permute-done.6.refs_2_), custom_call_target="tpu_custom_call" | custom-call | bytes 30000000 | tf_op jit(solution)/shard_map/pallas_call | solution.py:31
  30.1 0.1 collective-permute-start.8
  30.1 4.3 %collective-permute-done.7.refs_4_.refs_2_ = f32[2,128,128]{2,1,0:T(8,128)S(1)} collective-permute-done((f32[2,128,128]{2,1,0:T(8,128)S(1)}, f32[2,128,128]{2,1,0:T(8,128)S(1)}, u32[]{:S(2)}, u32[]{:S(2)}) %collective-permute-start.7) | collective-permute-done | bytes 131104 | tf_op jit(solution)/shard_map/ppermute | solution.py:54
  34.4 0.9 %collective-permute-done.9.refs_0_ = f32[5,64,128]{2,1,0:T(8,128)S(1)} collective-permute-done((f32[5,64,128]{2,1,0:T(8,128)S(1)}, f32[5,64,128]{2,1,0:T(8,128)S(1)}, u32[]{:S(2)}, u32[]{:S(2)}) %collective-permute-start.9) | collective-permute-done | bytes 163872 | tf_op jit(solution)/shard_map/ppermute | solution.py:46
  35.3 0.0 collective-permute-done.10.refs_1_
  35.3 0.0 collective-permute-done.11.refs_2_
  35.3 0.3 shard_map.69.refs_4_.refs_0_
  35.6 2.7 %collective-permute-done.8.refs_3_ = f32[128,128]{1,0:T(8,128)S(1)} collective-permute-done((f32[128,128]{1,0:T(8,128)S(1)}, f32[128,128]{1,0:T(8,128)S(1)}, u32[]{:S(2)}, u32[]{:S(2)}) %collective-permute-start.8) | collective-permute-done | bytes 65568 | tf_op jit(solution)/shard_map/ppermute | solution.py:54
  38.3 0.1 shard_map.70
  38.4 3.8 %collective-permute-start.15 = (f32[288,128]{1,0:T(8,128)S(1)}, f32[288,128]{1,0:T(8,128)S(1)}, u32[]{:S(2)}, u32[]{:S(2)}) collective-permute-start(f32[288,128]{1,0:T(8,128)S(1)} %get-tuple-element.62.refs_1_), channel_id=1, source_target_pairs={{0,16},{8,24},{16,0},{24,8},{1,17},{9,25},{17,1},{25,9},{2,18},{10... | collective-permute-start | bytes 442376 | tf_op jit(solution)/shard_map/ppermute | solution.py:54
  42.2 3.2 %collective-permute-start.12 = (f32[2,2,64,128]{3,2,1,0:T(8,128)S(1)}, f32[2,2,64,128]{3,2,1,0:T(8,128)S(1)}, u32[]{:S(2)}, u32[]{:S(2)}) collective-permute-start(f32[2,2,64,128]{3,2,1,0:T(8,128)S(1)} %get-tuple-element.63), channel_id=1, source_target_pairs={{0,12},{4,8},{8,4},{12,0},{16,28},{20,24},{24,20},{28,16},{1,13},{... | collective-permute-start | bytes 393224 | tf_op jit(solution)/shard_map/ppermute | solution.py:46
  45.4 0.0 collective-permute-start.13
  45.4 0.6 %collective-permute-start.14 = (f32[2,2,64,128]{3,2,1,0:T(8,128)S(1)}, f32[2,2,64,128]{3,2,1,0:T(8,128)S(1)}, u32[]{:S(2)}, u32[]{:S(2)}) collective-permute-start(f32[2,2,64,128]{3,2,1,0:T(8,128)S(1)} %get-tuple-element.65), channel_id=1, source_target_pairs={{0,4},{4,0},{8,12},{12,8},{16,20},{20,16},{24,28},{28,24},{1,5},{5... | collective-permute-start | bytes 393224 | tf_op jit(solution)/shard_map/ppermute | solution.py:46
  46.0 1.0 %collective-permute-done.15.refs_3_ = f32[288,128]{1,0:T(8,128)S(1)} collective-permute-done((f32[288,128]{1,0:T(8,128)S(1)}, f32[288,128]{1,0:T(8,128)S(1)}, u32[]{:S(2)}, u32[]{:S(2)}) %collective-permute-start.15) | collective-permute-done | bytes 147488 | tf_op jit(solution)/shard_map/ppermute | solution.py:54
  47.0 1.7 %shard_map.73 = (f32[2,64,128]{2,1,0:T(8,128)S(1)}, f32[2,64,128]{2,1,0:T(8,128)S(1)}, f32[2,64,128]{2,1,0:T(8,128)S(1)}, f32[2,64,128]{2,1,0:T(8,128)S(1)}) custom-call(f32[4,2,128,256]{3,2,1,0:T(8,128)S(1)} %shard_map.69.refs_4_.refs_0_, f32[2,4,2,128,128]{4,3,2,1,0:T(8,128)S(1)} %shard_map.62.refs_0_.refs_1_, ...), custom_call_target="tpu_custom_call" | custom-call | bytes 3000000 | tf_op jit(solution)/shard_map/pallas_call | solution.py:31
  48.7 3.1 %collective-permute-start.16 = (f32[2,64,128]{2,1,0:T(8,128)S(1)}, f32[2,64,128]{2,1,0:T(8,128)S(1)}, u32[]{:S(2)}, u32[]{:S(2)}) collective-permute-start(f32[2,64,128]{2,1,0:T(8,128)S(1)} %get-tuple-element.68), channel_id=1, source_target_pairs={{0,12},{4,8},{8,4},{12,0},{16,28},{20,24},{24,20},{28,16},{1,13},{... | collective-permute-start | bytes 196616 | tf_op jit(solution)/shard_map/ppermute | solution.py:46
  51.8 0.0 collective-permute-start.17
  51.8 0.0 collective-permute-done.12.refs_0_
  51.8 0.6 %collective-permute-start.18 = (f32[2,64,128]{2,1,0:T(8,128)S(1)}, f32[2,64,128]{2,1,0:T(8,128)S(1)}, u32[]{:S(2)}, u32[]{:S(2)}) collective-permute-start(f32[2,64,128]{2,1,0:T(8,128)S(1)} %get-tuple-element.70), channel_id=1, source_target_pairs={{0,4},{4,0},{8,12},{12,8},{16,20},{20,16},{24,28},{28,24},{1,5},{5... | collective-permute-start | bytes 196616 | tf_op jit(solution)/shard_map/ppermute | solution.py:46
  52.4 0.0 collective-permute-done.13.refs_1_
  52.4 0.0 collective-permute-done.14.refs_2_
  52.5 0.9 %shard_map.72 = f32[2,2,4,64,128]{4,3,2,1,0:T(8,128)} custom-call(f32[2,2,64,128]{3,2,1,0:T(8,128)S(1)} %collective-permute-done.12.refs_0_, f32[2,2,64,128]{3,2,1,0:T(8,128)S(1)} %collective-permute-done.13.refs_1_, f32[2,2,64,128]{3,2,1,0:T(8,128)S(1)} %collective-permute-done.14.refs_2_, f32[2,2,64,128]{3,2,1,0:T(8,128)S(1)} %get-tuple-element.66.refs_3_), custom_call_target="tpu_custom_call" | custom-call | bytes 3000000 | tf_op jit(solution)/shard_map/pallas_call | solution.py:31
  53.3 0.7 %collective-permute-done.16.refs_0_ = f32[2,64,128]{2,1,0:T(8,128)S(1)} collective-permute-done((f32[2,64,128]{2,1,0:T(8,128)S(1)}, f32[2,64,128]{2,1,0:T(8,128)S(1)}, u32[]{:S(2)}, u32[]{:S(2)}) %collective-permute-start.16) | collective-permute-done | bytes 65568 | tf_op jit(solution)/shard_map/ppermute | solution.py:46
  54.0 2.0 %collective-permute-done.17.refs_1_ = f32[2,64,128]{2,1,0:T(8,128)S(1)} collective-permute-done((f32[2,64,128]{2,1,0:T(8,128)S(1)}, f32[2,64,128]{2,1,0:T(8,128)S(1)}, u32[]{:S(2)}, u32[]{:S(2)}) %collective-permute-start.17) | collective-permute-done | bytes 65568 | tf_op jit(solution)/shard_map/ppermute | solution.py:46
  56.1 0.0 collective-permute-done.18.refs_2_
  56.1 0.6 %shard_map.74 = f32[2,64,128]{2,1,0:T(8,128)} custom-call(f32[2,64,128]{2,1,0:T(8,128)S(1)} %collective-permute-done.16.refs_0_, f32[2,64,128]{2,1,0:T(8,128)S(1)} %collective-permute-done.17.refs_1_, f32[2,64,128]{2,1,0:T(8,128)S(1)} %collective-permute-done.18.refs_2_, f32[2,64,128]{2,1,0:T(8,128)S(1)} %get-tuple-element.71.refs_3_), custom_call_target="tpu_custom_call" | custom-call | bytes 3000000 | tf_op jit(solution)/shard_map/pallas_call | solution.py:31
  (4 shorter events, 0.1 us)
Async XLA Ops:
  0.6 1.1 %copy-start.1 = (f32[2,2,4,64,128]{4,3,2,1,0:T(8,128)S(1)}, f32[2,2,4,64,128]{4,3,2,1,0:T(8,128)}, u32[]{:S(2)}) copy-start(f32[2,2,4,64,128]{4,3,2,1,0:T(8,128)} %refs_0_.3) | copy-start | bytes 1572868
  1.8 4.7 %copy-start = (f32[2,2,4,64,128]{4,3,2,1,0:T(8,128)S(1)}, f32[2,2,4,64,128]{4,3,2,1,0:T(8,128)}, u32[]{:S(2)}) copy-start(f32[2,2,4,64,128]{4,3,2,1,0:T(8,128)} %refs_0_.6) | copy-start | bytes 1572868
  1.8 16.7 %collective-permute-start = (f32[2,2,2,64,128]{4,3,2,1,0:T(8,128)S(1)}, f32[2,2,2,64,128]{4,3,2,1,0:T(8,128)S(1)}, u32[]{:S(2)}, u32[]{:S(2)}) collective-permute-start(f32[2,2,2,64,128]{4,3,2,1,0:T(8,128)S(1)} %get-tuple-element.41), channel_id=1, source_target_pairs={{0,12},{4,8},{8,4},{12,0},{16,28},{20,24},{24,20},{28,16},{1,13},{... | collective-permute-start | bytes 786440 | tf_op jit(solution)/shard_map/ppermute | solution.py:46
  5.9 12.6 %collective-permute-start.1 = (f32[2,2,2,64,128]{4,3,2,1,0:T(8,128)S(1)}, f32[2,2,2,64,128]{4,3,2,1,0:T(8,128)S(1)}, u32[]{:S(2)}, u32[]{:S(2)}) collective-permute-start(f32[2,2,2,64,128]{4,3,2,1,0:T(8,128)S(1)} %get-tuple-element.42.refs_2_), channel_id=1, source_target_pairs={{0,8},{4,12},{8,0},{12,4},{16,24},{20,28},{24,16},{28,20},{1,9},{5... | collective-permute-start | bytes 786440 | tf_op jit(solution)/shard_map/ppermute | solution.py:46
  6.3 12.2 %collective-permute-start.2 = (f32[2,2,2,64,128]{4,3,2,1,0:T(8,128)S(1)}, f32[2,2,2,64,128]{4,3,2,1,0:T(8,128)S(1)}, u32[]{:S(2)}, u32[]{:S(2)}) collective-permute-start(f32[2,2,2,64,128]{4,3,2,1,0:T(8,128)S(1)} %get-tuple-element.43), channel_id=1, source_target_pairs={{0,4},{4,0},{8,12},{12,8},{16,20},{20,16},{24,28},{28,24},{1,5},{5... | collective-permute-start | bytes 786440 | tf_op jit(solution)/shard_map/ppermute | solution.py:46
  6.8 2.0 %collective-permute-start.3 = (f32[2,64,128]{2,1,0:T(8,128)S(1)}, f32[2,64,128]{2,1,0:T(8,128)S(1)}, u32[]{:S(2)}, u32[]{:S(2)}) collective-permute-start(f32[2,64,128]{2,1,0:T(8,128)S(1)} %get-tuple-element.46), channel_id=1, source_target_pairs={{0,1},{1,0},{2,3},{3,2},{4,5},{5,4},{6,7},{7,6},{8,9},{9,8},{10,11... | collective-permute-start | bytes 196616 | tf_op jit(solution)/shard_map/ppermute | solution.py:85
  6.9 11.6 %collective-permute-start.4 = (f32[2,64,128]{2,1,0:T(8,128)S(1)}, f32[2,64,128]{2,1,0:T(8,128)S(1)}, u32[]{:S(2)}, u32[]{:S(2)}) collective-permute-start(f32[2,64,128]{2,1,0:T(8,128)S(1)} %get-tuple-element.47), channel_id=1, source_target_pairs={{1,2},{2,1},{0,4},{3,7},{5,6},{6,5},{4,0},{7,3},{9,10},{10,9},{8,1... | collective-permute-start | bytes 196616 | tf_op jit(solution)/shard_map/ppermute | solution.py:84
  18.8 6.8 %collective-permute-start.5 = (f32[2,2,128,128]{3,2,1,0:T(8,128)S(1)}, f32[2,2,128,128]{3,2,1,0:T(8,128)S(1)}, u32[]{:S(2)}, u32[]{:S(2)}) collective-permute-start(f32[2,2,128,128]{3,2,1,0:T(8,128)S(1)} %shard_map.63), channel_id=1, source_target_pairs={{1,2},{2,1},{0,4},{3,7},{5,6},{6,5},{4,0},{7,3},{9,10},{10,9},{8,1... | collective-permute-start | bytes 786440 | tf_op jit(solution)/shard_map/ppermute | solution.py:84
  21.7 6.3 %collective-permute-start.6 = (f32[2,2,128,128]{3,2,1,0:T(8,128)S(1)}, f32[2,2,128,128]{3,2,1,0:T(8,128)S(1)}, u32[]{:S(2)}, u32[]{:S(2)}) collective-permute-start(f32[2,2,128,128]{3,2,1,0:T(8,128)S(1)} %shard_map.65.refs_3_), channel_id=1, source_target_pairs={{0,1},{1,0},{2,3},{3,2},{4,5},{5,4},{6,7},{7,6},{8,9},{9,8},{10,11... | collective-permute-start | bytes 786440 | tf_op jit(solution)/shard_map/ppermute | solution.py:85
  21.9 13.5 %collective-permute-start.10 = (f32[5,64,128]{2,1,0:T(8,128)S(1)}, f32[5,64,128]{2,1,0:T(8,128)S(1)}, u32[]{:S(2)}, u32[]{:S(2)}) collective-permute-start(f32[5,64,128]{2,1,0:T(8,128)S(1)} %get-tuple-element.57.refs_3_), channel_id=1, source_target_pairs={{0,8},{4,12},{8,0},{12,4},{16,24},{20,28},{24,16},{28,20},{1,9},{5... | collective-permute-start | bytes 491528 | tf_op jit(solution)/shard_map/ppermute | solution.py:46
  23.6 11.7 %collective-permute-start.9 = (f32[5,64,128]{2,1,0:T(8,128)S(1)}, f32[5,64,128]{2,1,0:T(8,128)S(1)}, u32[]{:S(2)}, u32[]{:S(2)}) collective-permute-start(f32[5,64,128]{2,1,0:T(8,128)S(1)} %get-tuple-element.56), channel_id=1, source_target_pairs={{0,12},{4,8},{8,4},{12,0},{16,28},{20,24},{24,20},{28,16},{1,13},{... | collective-permute-start | bytes 491528 | tf_op jit(solution)/shard_map/ppermute | solution.py:46
  24.5 10.8 %collective-permute-start.11 = (f32[5,64,128]{2,1,0:T(8,128)S(1)}, f32[5,64,128]{2,1,0:T(8,128)S(1)}, u32[]{:S(2)}, u32[]{:S(2)}) collective-permute-start(f32[5,64,128]{2,1,0:T(8,128)S(1)} %get-tuple-element.58), channel_id=1, source_target_pairs={{0,4},{4,0},{8,12},{12,8},{16,20},{20,16},{24,28},{28,24},{1,5},{5... | collective-permute-start | bytes 491528 | tf_op jit(solution)/shard_map/ppermute | solution.py:46
  25.6 8.8 %collective-permute-start.7 = (f32[2,128,128]{2,1,0:T(8,128)S(1)}, f32[2,128,128]{2,1,0:T(8,128)S(1)}, u32[]{:S(2)}, u32[]{:S(2)}) collective-permute-start(f32[2,128,128]{2,1,0:T(8,128)S(1)} %shard_map.64.refs_4_), channel_id=1, source_target_pairs={{0,16},{8,24},{16,0},{24,8},{1,17},{9,25},{17,1},{25,9},{2,18},{10... | collective-permute-start | bytes 393224 | tf_op jit(solution)/shard_map/ppermute | solution.py:54
  30.1 8.2 %collective-permute-start.8 = (f32[128,128]{1,0:T(8,128)S(1)}, f32[128,128]{1,0:T(8,128)S(1)}, u32[]{:S(2)}, u32[]{:S(2)}) collective-permute-start(f32[128,128]{1,0:T(8,128)S(1)} %get-tuple-element.53), channel_id=1, source_target_pairs={{0,16},{8,24},{16,0},{24,8},{1,17},{9,25},{17,1},{25,9},{2,18},{10... | collective-permute-start | bytes 196616 | tf_op jit(solution)/shard_map/ppermute | solution.py:54
  38.4 8.6 %collective-permute-start.15 = (f32[288,128]{1,0:T(8,128)S(1)}, f32[288,128]{1,0:T(8,128)S(1)}, u32[]{:S(2)}, u32[]{:S(2)}) collective-permute-start(f32[288,128]{1,0:T(8,128)S(1)} %get-tuple-element.62.refs_1_), channel_id=1, source_target_pairs={{0,16},{8,24},{16,0},{24,8},{1,17},{9,25},{17,1},{25,9},{2,18},{10... | collective-permute-start | bytes 442376 | tf_op jit(solution)/shard_map/ppermute | solution.py:54
  42.2 9.6 %collective-permute-start.12 = (f32[2,2,64,128]{3,2,1,0:T(8,128)S(1)}, f32[2,2,64,128]{3,2,1,0:T(8,128)S(1)}, u32[]{:S(2)}, u32[]{:S(2)}) collective-permute-start(f32[2,2,64,128]{3,2,1,0:T(8,128)S(1)} %get-tuple-element.63), channel_id=1, source_target_pairs={{0,12},{4,8},{8,4},{12,0},{16,28},{20,24},{24,20},{28,16},{1,13},{... | collective-permute-start | bytes 393224 | tf_op jit(solution)/shard_map/ppermute | solution.py:46
  45.4 7.1 %collective-permute-start.13 = (f32[2,2,64,128]{3,2,1,0:T(8,128)S(1)}, f32[2,2,64,128]{3,2,1,0:T(8,128)S(1)}, u32[]{:S(2)}, u32[]{:S(2)}) collective-permute-start(f32[2,2,64,128]{3,2,1,0:T(8,128)S(1)} %get-tuple-element.64), channel_id=1, source_target_pairs={{0,8},{4,12},{8,0},{12,4},{16,24},{20,28},{24,16},{28,20},{1,9},{5... | collective-permute-start | bytes 393224 | tf_op jit(solution)/shard_map/ppermute | solution.py:46
  45.4 7.1 %collective-permute-start.14 = (f32[2,2,64,128]{3,2,1,0:T(8,128)S(1)}, f32[2,2,64,128]{3,2,1,0:T(8,128)S(1)}, u32[]{:S(2)}, u32[]{:S(2)}) collective-permute-start(f32[2,2,64,128]{3,2,1,0:T(8,128)S(1)} %get-tuple-element.65), channel_id=1, source_target_pairs={{0,4},{4,0},{8,12},{12,8},{16,20},{20,16},{24,28},{28,24},{1,5},{5... | collective-permute-start | bytes 393224 | tf_op jit(solution)/shard_map/ppermute | solution.py:46
  48.7 5.3 %collective-permute-start.16 = (f32[2,64,128]{2,1,0:T(8,128)S(1)}, f32[2,64,128]{2,1,0:T(8,128)S(1)}, u32[]{:S(2)}, u32[]{:S(2)}) collective-permute-start(f32[2,64,128]{2,1,0:T(8,128)S(1)} %get-tuple-element.68), channel_id=1, source_target_pairs={{0,12},{4,8},{8,4},{12,0},{16,28},{20,24},{24,20},{28,16},{1,13},{... | collective-permute-start | bytes 196616 | tf_op jit(solution)/shard_map/ppermute | solution.py:46
  51.8 4.3 %collective-permute-start.17 = (f32[2,64,128]{2,1,0:T(8,128)S(1)}, f32[2,64,128]{2,1,0:T(8,128)S(1)}, u32[]{:S(2)}, u32[]{:S(2)}) collective-permute-start(f32[2,64,128]{2,1,0:T(8,128)S(1)} %get-tuple-element.69), channel_id=1, source_target_pairs={{0,8},{4,12},{8,0},{12,4},{16,24},{20,28},{24,16},{28,20},{1,9},{5... | collective-permute-start | bytes 196616 | tf_op jit(solution)/shard_map/ppermute | solution.py:46
  51.8 4.3 %collective-permute-start.18 = (f32[2,64,128]{2,1,0:T(8,128)S(1)}, f32[2,64,128]{2,1,0:T(8,128)S(1)}, u32[]{:S(2)}, u32[]{:S(2)}) collective-permute-start(f32[2,64,128]{2,1,0:T(8,128)S(1)} %get-tuple-element.70), channel_id=1, source_target_pairs={{0,4},{4,0},{8,12},{12,8},{16,20},{20,16},{24,28},{28,24},{1,5},{5... | collective-permute-start | bytes 196616 | tf_op jit(solution)/shard_map/ppermute | solution.py:46
